TPU v7x, 32 devices: a whole 2x2x4 slice. The times are simulated.
32 devices in a mesh: groups: 2 (over y), expert: 4 (over z), dp: 4 (over x, core).
Axes of the slice: x: 2, y: 2, z: 4, core: 2. Of those that a mesh axis runs over, the one named last changes fastest.
Arguments:
- tokens: bfloat16 [1024, 2048], P(('groups', 'expert', 'dp')), parts along dimension 0, may hold values from -6 to 6
- out_grad: bfloat16 [1024, 2048], P(('groups', 'expert', 'dp')), parts along dimension 0, may hold values from -6 to 6
- expert_ids: int32 [1024, 8], P(('groups', 'expert', 'dp')), parts along dimension 0, may hold values from 0 to 15, as said below
- slot_pos: int32 [1024, 8], P(('groups', 'expert', 'dp')), parts along dimension 0, may hold values from -1 to 15, as said below
- combine_weight: float32 [1024, 8], P(('groups', 'expert', 'dp')), parts along dimension 0, may hold values from 0.05 to 0.6
- w_gate: bfloat16 [768, 16, 2048], P('dp', 'expert'), may hold values from -0.125 to 0.125
- w_up: bfloat16 [768, 16, 2048], P('dp', 'expert'), may hold values from -0.125 to 0.125
- w_down: bfloat16 [768, 16, 2048], P('dp', 'expert'), may hold values from -0.21875 to 0.21875
Outputs:
- layer_out: bfloat16 [1024, 2048], P(('groups', 'expert', 'dp')), parts along dimension 0
- input_grad: bfloat16 [1024, 2048], P(('groups', 'expert', 'dp')), parts along dimension 0
- weight_grad: float32 [1024, 8], P(('groups', 'expert', 'dp')), parts along dimension 0
- down_grad: bfloat16 [1536, 16, 2048], P(('groups', 'dp'), 'expert'), parts along dimension 0
There are 2 independent parts, one for each index of `groups`. A program takes and returns all parts, laid end to end along the dimension named above; an argument that names none is the same for every part. Nothing has to cross between parts.
Inputs may be any that keep to these rules, and one draw needn't show every extreme that they name: `expert_ids`: each row names 8 different experts. In every aligned block of 32 rows one expert, the same for all blocks, is named by at least 17 rows. `slot_pos`: within each aligned block of 32 rows, the entries that name one expert hold distinct slots 0, 1, 2 and so on in a seeded priority order, and those past the first 16 hold -1; so every block fills all 16 slots of one expert and drops at least one entry.
All inputs are finite; a program needn't handle non-finite values.
Results may differ from a plain program's by a relative error of at most 0.009.
Values may be sent and summed in bfloat16 or wider, within the bound.
No kernel may reach another device: no remote copies, remote signals or barrier semaphores. Data moves between devices by JAX's collectives and lax.ppermute only.
A program may use at most 192 MiB of HBM per device.

v0:
```python
import jax
import jax.numpy as jnp
from jax import lax
from jax.sharding import PartitionSpec as P


def slot_places(expert_ids, slot_pos, local_experts, row_total, capacity):
    flat_place = (
        expert_ids % local_experts * row_total + expert_ids // local_experts * capacity + slot_pos
    )
    return jnp.where(slot_pos >= 0, flat_place, -1)


def local(tokens, out_grad, expert_ids, slot_pos, combine_weight, w_gate, w_up, w_down):
    local_experts = w_gate.shape[1]
    expert_peers = lax.axis_size("expert")
    tok_count = tokens.shape[0]
    top_count = expert_ids.shape[1]
    model_width = tokens.shape[1]
    capacity = tok_count * top_count // (local_experts * expert_peers)
    row_total = expert_peers * capacity
    slot_count = local_experts * row_total
    kept_mask = slot_pos >= 0
    flat_place = slot_places(expert_ids, slot_pos, local_experts, row_total, capacity)
    places = jnp.arange(slot_count, dtype=jnp.int32)
    onehot = (flat_place[:, :, None] == places[None, None, :]).astype(jnp.float32)
    present = jnp.sum(onehot, axis=1)
    weighted = jnp.sum(onehot * combine_weight[:, :, None], axis=1)
    sent_rows = jnp.einsum(
        "tw,td->wd", present.astype(jnp.bfloat16), tokens, preferred_element_type=jnp.float32
    )
    sent_cot = jnp.einsum(
        "tw,td->wd", weighted, out_grad.astype(jnp.float32), precision=lax.Precision.HIGHEST
    )
    sent_rows = sent_rows.astype(jnp.bfloat16).reshape(local_experts, row_total, model_width)
    sent_cot = sent_cot.astype(jnp.bfloat16).reshape(local_experts, row_total, model_width)
    expert_rows, expert_cot = (
        lax.all_to_all(sent_rows, "expert", split_axis=1, concat_axis=1, tiled=True),
        lax.all_to_all(sent_cot, "expert", split_axis=1, concat_axis=1, tiled=True),
    )
    gate_piece = lax.all_gather(w_gate, "dp", axis=0, tiled=True)
    up_piece = lax.all_gather(w_up, "dp", axis=0, tiled=True)
    down_piece = lax.all_gather(w_down, "dp", axis=0, tiled=True)
    gate_pre = jnp.einsum(
        "nld,lrd->lnr", gate_piece, expert_rows, preferred_element_type=jnp.float32
    )
    up_pre = jnp.einsum("nld,lrd->lnr", up_piece, expert_rows, preferred_element_type=jnp.float32)
    sigmoid_val = jax.nn.sigmoid(gate_pre)
    hidden = (gate_pre * sigmoid_val * up_pre).astype(jnp.bfloat16)
    expert_out = jnp.einsum("lnr,nld->lrd", hidden, down_piece, preferred_element_type=jnp.float32)
    hidden_grad = jnp.einsum(
        "nld,lrd->lnr", down_piece, expert_cot, preferred_element_type=jnp.float32
    )
    gate_grad = (
        hidden_grad * up_pre * sigmoid_val * (1.0 + gate_pre * (1.0 - sigmoid_val))
    ).astype(jnp.bfloat16)
    up_grad = (hidden_grad * gate_pre * sigmoid_val).astype(jnp.bfloat16)
    slot_back = jnp.einsum(
        "lnr,nld->lrd", gate_grad, gate_piece, preferred_element_type=jnp.float32
    )
    slot_back = slot_back + jnp.einsum(
        "lnr,nld->lrd", up_grad, up_piece, preferred_element_type=jnp.float32
    )
    hidden_all, expert_out, slot_back = (hidden, expert_out, slot_back)
    back_out, back_grad = (
        lax.all_to_all(
            expert_out.astype(jnp.bfloat16), "expert", split_axis=1, concat_axis=1, tiled=True
        ),
        lax.all_to_all(
            slot_back.astype(jnp.bfloat16), "expert", split_axis=1, concat_axis=1, tiled=True
        ),
    )
    back_out = back_out.reshape(slot_count, model_width)
    back_grad = back_grad.reshape(slot_count, model_width)
    safe_place = jnp.maximum(flat_place, 0)
    picked_out = jnp.where(
        kept_mask[:, :, None], jnp.take(back_out, safe_place, axis=0).astype(jnp.float32), 0.0
    )
    picked_grad = jnp.where(
        kept_mask[:, :, None], jnp.take(back_grad, safe_place, axis=0).astype(jnp.float32), 0.0
    )
    layer_out = jnp.sum(combine_weight[:, :, None] * picked_out, axis=1).astype(jnp.bfloat16)
    input_grad = jnp.sum(picked_grad, axis=1).astype(jnp.bfloat16)
    weight_grad = jnp.sum(picked_out * out_grad.astype(jnp.float32)[:, None, :], axis=2)
    down_grad = lax.psum_scatter(
        jnp.einsum(
            "lnr,lrd->nld", hidden_all, expert_cot, preferred_element_type=jnp.float32
        ).astype(jnp.bfloat16),
        "dp",
        scatter_dimension=0,
        tiled=True,
    )
    return (layer_out, input_grad, weight_grad, down_grad)


def solution(mesh):
    in_specs = (
        P(("groups", "expert", "dp"), None),
        P(("groups", "expert", "dp"), None),
        P(("groups", "expert", "dp"), None),
        P(("groups", "expert", "dp"), None),
        P(("groups", "expert", "dp"), None),
        P("dp", "expert", None),
        P("dp", "expert", None),
        P("dp", "expert", None),
    )
    out_specs = (
        P(("groups", "expert", "dp"), None),
        P(("groups", "expert", "dp"), None),
        P(("groups", "expert", "dp"), None),
        P(("groups", "dp"), "expert", None),
    )
    return jax.shard_map(local, mesh=mesh, in_specs=in_specs, out_specs=out_specs, check_vma=False)
```

profile of v0, /device:TPU:0, one launch (start us, length us, event | category | flops | bytes accessed | tf_op | source)
XLA Modules:
  0.0 499.7 jit_solution(9583693527816766069)
XLA Ops:
  7.2 5.4 %copy.62 = bf16[192,4,2048]{2,0,1:T(8,128)(2,1)} copy(bf16[192,4,2048]{2,1,0:T(4,128)(2,1)} %param.15) | data formatting | bytes 6291456 | tf_op args[5]
  12.8 5.3 %copy.64 = bf16[192,4,2048]{2,0,1:T(8,128)(2,1)} copy(bf16[192,4,2048]{2,1,0:T(4,128)(2,1)} %param.16) | data formatting | bytes 6291456 | tf_op args[6]
  18.1 3.4 copy.66
  24.2 6.3 %all-to-all-start = ((bf16[4,64,2048]{2,0,1:T(4,128)(2,1)}), bf16[4,64,2048]{2,0,1:T(4,128)(2,1)S(1)}, u32[]{:S(2)}, u32[]{:S(2)}) async-start(bf16[4,64,2048]{2,0,1:T(4,128)(2,1)} %copy.61), calls=%async_computation | async-start | bytes 2097152 | tf_op jit(solution)/shard_map/all_to_all | solution.py:38
  33.4 22.8 %all-to-all-done = bf16[4,64,2048]{2,0,1:T(4,128)(2,1)S(1)} async-done(((bf16[4,64,2048]{2,0,1:T(4,128)(2,1)}), bf16[4,64,2048]{2,0,1:T(4,128)(2,1)S(1)}, u32[]{:S(2)}, u32[]{:S(2)}) %all-to-all-start) | async-done | bytes 1048608 | tf_op jit(solution)/shard_map/all_to_all | solution.py:38
  56.2 3.5 all-to-all-start.2
  60.0 37.7 %all-gather.4.cloned.1.call-done = bf16[768,4,2048]{2,0,1:T(8,128)(2,1)} async-done(((bf16[192,4,2048]{2,0,1:T(8,128)(2,1)}), bf16[768,4,2048]{2,0,1:T(8,128)(2,1)}) %all-gather.4.cloned.1.call-update) | async-done | bytes 12582928 | tf_op jit(solution)/shard_map/all_gather | solution.py:41
  97.7 8.6 %convolution_bitcast_fusion.2 = f32[4,768,64]{1,2,0:T(8,128)S(1)} fusion(bf16[768,4,2048]{2,0,1:T(8,128)(2,1)} %all-gather.4.cloned.1.call-done, bf16[4,64,2048]{2,0,1:T(4,128)(2,1)S(1)} %all-to-all-done), kind=kOutput, calls=%fused_computation.14 | convolution fusion | flops 805306368 | bytes 14417920 | tf_op jit(solution)/shard_map/nld,lrd->lnr/dot_general | solution.py:44
  106.2 75.1 %all-gather.6.cloned.1.call-done = bf16[768,4,2048]{2,0,1:T(8,128)(2,1)} async-done(((bf16[192,4,2048]{2,0,1:T(8,128)(2,1)}), bf16[768,4,2048]{2,0,1:T(8,128)(2,1)}) %all-gather.6.cloned.1.call-update) | async-done | bytes 12582928 | tf_op jit(solution)/shard_map/all_gather | solution.py:42
  181.4 9.5 %multiply_convert_fusion.2 = (bf16[4,768,64]{1,2,0:T(8,128)(2,1)S(1)}, f32[4,768,64]{1,2,0:T(8,128)}) fusion(f32[4,768,64]{1,2,0:T(8,128)S(1)} %convolution_bitcast_fusion.2, bf16[768,4,2048]{2,0,1:T(8,128)(2,1)} %all-gather.6.cloned.1.call-done, bf16[4,64,2048]{2,0,1:T(4,128)(2,1)S(1)} %all-to-all-done), kind=kOutput, calls=%fused_computation.23 | convolution fusion | flops 806486016 | bytes 15597568 | tf_op jit(solution)/shard_map/nld,lrd->lnr/dot_general | solution.py:47
  190.9 8.4 %convert_bitcast_fusion = bf16[768,4,2048]{0,2,1:T(8,128)(2,1)} fusion(bf16[4,768,64]{1,2,0:T(8,128)(2,1)S(1)} %get-tuple-element.29, bf16[4,64,2048]{2,0,1:T(4,128)(2,1)S(1)} %all-to-all-done.2), kind=kOutput, calls=%fused_computation.2 | convolution fusion | flops 811597824 | bytes 14024704 | tf_op jit(solution)/shard_map/lnr,lrd->nld/dot_general | solution.py:86
  199.2 21.9 %copy.78 = bf16[768,4,2048]{2,1,0:T(4,128)(2,1)} copy(bf16[768,4,2048]{0,2,1:T(8,128)(2,1)} %convert_bitcast_fusion) | data formatting | bytes 25165824 | tf_op jit(solution)/shard_map/convert_element_type | solution.py:88
  221.1 44.0 %all-gather.8.cloned.1.call-done = bf16[768,4,2048]{2,0,1:T(8,128)(2,1)} async-done(((bf16[192,4,2048]{2,0,1:T(8,128)(2,1)}), bf16[768,4,2048]{2,0,1:T(8,128)(2,1)}) %all-gather.8.cloned.1.call-update) | async-done | bytes 12582928 | tf_op jit(solution)/shard_map/all_gather | solution.py:43
  265.1 6.9 %convolution_convert_fusion = bf16[4,64,2048]{2,1,0:T(8,128)(2,1)S(1)} fusion(bf16[4,768,64]{1,2,0:T(8,128)(2,1)S(1)} %get-tuple-element.29, bf16[768,4,2048]{2,0,1:T(8,128)(2,1)} %all-gather.8.cloned.1.call-done), kind=kOutput, calls=%fused_computation.5 | convolution fusion | flops 805830656 | bytes 14024704 | tf_op jit(solution)/shard_map/lnr,nld->lrd/dot_general | solution.py:50
  273.7 4.6 all-to-all-start.1
  278.3 8.9 %convolution_bitcast_fusion = f32[4,768,64]{1,2,0:T(8,128)S(1)} fusion(bf16[768,4,2048]{2,0,1:T(8,128)(2,1)} %all-gather.8.cloned.1.call-done, bf16[4,64,2048]{2,0,1:T(4,128)(2,1)S(1)} %all-to-all-done.2), kind=kOutput, calls=%fused_computation.12 | convolution fusion | flops 805306368 | bytes 14417920 | tf_op jit(solution)/shard_map/nld,lrd->lnr/dot_general | solution.py:51
  287.2 7.2 %fusion.5 = f32[4,64,2048]{2,1,0:T(8,128)S(1)} fusion(bf16[768,4,2048]{2,0,1:T(8,128)(2,1)} %all-gather.4.cloned.1.call-done, f32[4,768,64]{1,2,0:T(8,128)S(1)} %convolution_bitcast_fusion.2, f32[4,768,64]{1,2,0:T(8,128)S(1)} %convolution_bitcast_fusion, f32[4,768,64]{1,2,0:T(8,128)S(1)} %copy-done.2), kind=kOutput, calls=%fused_computation.25 | convolution fusion | flops 807272448 | bytes 17039360 | tf_op jit(solution)/shard_map/lnr,nld->lrd/dot_general | solution.py:58
  294.5 2.4 fusion
  298.7 5.9 %all-to-all-done.1 = bf16[4,64,2048]{2,0,1:T(4,128)(2,1)} async-done(((bf16[4,64,2048]{2,0,1:T(4,128)(2,1)}), bf16[4,64,2048]{2,0,1:T(4,128)(2,1)}, u32[]{:S(2)}, u32[]{:S(2)}) %all-to-all-start.1) | async-done | bytes 1048608 | tf_op jit(solution)/shard_map/all_to_all | solution.py:66
  304.6 3.8 all-to-all-start.3
  313.2 20.2 %all-to-all-done.3 = bf16[4,64,2048]{2,0,1:T(4,128)(2,1)S(1)} async-done(((bf16[4,64,2048]{2,0,1:T(4,128)(2,1)}), bf16[4,64,2048]{2,0,1:T(4,128)(2,1)S(1)}, u32[]{:S(2)}, u32[]{:S(2)}) %all-to-all-start.3) | async-done | bytes 1048608 | tf_op jit(solution)/shard_map/all_to_all | solution.py:69
  335.3 3.4 multiply_reduce_fusion
  339.4 148.7 %all-reduce.3.cloned.1.call-done = bf16[768,4,2048]{2,1,0:T(4,128)(2,1)} async-done(((bf16[768,4,2048]{2,1,0:T(4,128)(2,1)}), bf16[768,4,2048]{2,1,0:T(4,128)(2,1)}) %all-reduce.3.cloned.1.call-update) | async-done | bytes 12582928
  488.1 5.1 %constant_dynamic-slice_fusion = bf16[192,4,2048]{2,1,0:T(4,128)(2,1)} fusion(bf16[768,4,2048]{2,1,0:T(4,128)(2,1)} %all-reduce.3.cloned.1.call-done, u32[]{:T(128)S(6)} %multiply.1), kind=kLoop, calls=%fused_computation.51 | loop fusion | bytes 6291460
  (61 shorter events, 16.3 us)
Async XLA Ops:
  7.2 14.8 %copy-start = (bf16[32,2048]{1,0:T(8,128)(2,1)S(1)}, bf16[32,2048]{1,0:T(8,128)(2,1)}, u32[]{:S(2)}) copy-start(bf16[32,2048]{1,0:T(8,128)(2,1)} %param.10) | copy-start | bytes 393220
  7.2 10.9 %copy-start.3 = (bf16[192,4,2048]{2,1,0:T(4,128)(2,1)S(1)}, bf16[192,4,2048]{2,1,0:T(4,128)(2,1)}, u32[]{:S(2)}) copy-start(bf16[192,4,2048]{2,1,0:T(4,128)(2,1)} %param.17) | copy-start | bytes 9437188
  7.2 90.5 %all-gather.4.cloned.1.call-start = ((), (), s32[]{:S(2)}) async-start(), calls=%async_computation.4 | async-start | bytes 15728640 | tf_op jit(solution)/shard_map/all_gather | solution.py:41
  12.7 8.8 %copy-start.7 = (f32[32,8]{0,1:T(8,128)S(1)}, f32[32,8]{0,1:T(8,128)}, u32[]{:S(2)}) copy-start(f32[32,8]{0,1:T(8,128)} %param.14) | copy-start | bytes 3076
  12.7 8.9 %copy-start.8 = (s32[32,8]{0,1:T(8,128)S(1)}, s32[32,8]{0,1:T(8,128)}, u32[]{:S(2)}) copy-start(s32[32,8]{0,1:T(8,128)} %param.13) | copy-start | bytes 3076
  12.7 8.9 %copy-start.9 = (s32[32,8]{0,1:T(8,128)S(1)}, s32[32,8]{0,1:T(8,128)}, u32[]{:S(2)}) copy-start(s32[32,8]{0,1:T(8,128)} %param.12) | copy-start | bytes 3076
  12.7 17.8 %copy-start.4 = (bf16[32,2048]{1,0:T(8,128)(2,1)S(1)}, bf16[32,2048]{1,0:T(8,128)(2,1)}, u32[]{:S(2)}) copy-start(bf16[32,2048]{1,0:T(8,128)(2,1)} %param.11) | copy-start | bytes 393220
  12.7 168.7 %all-gather.6.cloned.1.call-start = ((), (), s32[]{:S(2)}) async-start(), calls=%async_computation.5 | async-start | bytes 15728640 | tf_op jit(solution)/shard_map/all_gather | solution.py:42
  18.0 247.0 %all-gather.8.cloned.1.call-start = ((), (), s32[]{:S(2)}) async-start(), calls=%async_computation.6 | async-start | bytes 15728640 | tf_op jit(solution)/shard_map/all_gather | solution.py:43
  21.6 38.4 %copy-start.6 = (f32[32,8]{1,0:T(8,128)}, f32[32,8]{1,0:T(8,128)S(1)}, u32[]{:S(2)}) copy-start(f32[32,8]{1,0:T(8,128)S(1)} %copy.57) | copy-start | bytes 3076
  24.2 32.0 %all-to-all-start = ((bf16[4,64,2048]{2,0,1:T(4,128)(2,1)}), bf16[4,64,2048]{2,0,1:T(4,128)(2,1)S(1)}, u32[]{:S(2)}, u32[]{:S(2)}) async-start(bf16[4,64,2048]{2,0,1:T(4,128)(2,1)} %copy.61), calls=%async_computation | async-start | bytes 2097152 | tf_op jit(solution)/shard_map/all_to_all | solution.py:38
  56.2 134.6 %all-to-all-start.2 = ((bf16[4,64,2048]{2,0,1:T(4,128)(2,1)}), bf16[4,64,2048]{2,0,1:T(4,128)(2,1)S(1)}, u32[]{:S(2)}, u32[]{:S(2)}) async-start(bf16[4,64,2048]{2,0,1:T(4,128)(2,1)} %copy.72), calls=%async_computation.2 | async-start | bytes 2097152 | tf_op jit(solution)/shard_map/all_to_all | solution.py:39
  59.7 428.4 %all-reduce.3.cloned.1.call-start = ((), (), s32[]{:S(2)}) async-start(), calls=%async_computation.7 | async-start | bytes 25165824
  271.9 15.3 %copy-start.2 = (f32[4,768,64]{1,2,0:T(8,128)S(1)}, f32[4,768,64]{1,2,0:T(8,128)}, u32[]{:S(2)}) copy-start(f32[4,768,64]{1,2,0:T(8,128)} %get-tuple-element.30) | copy-start | bytes 2359300
  273.7 30.9 %all-to-all-start.1 = ((bf16[4,64,2048]{2,0,1:T(4,128)(2,1)}), bf16[4,64,2048]{2,0,1:T(4,128)(2,1)}, u32[]{:S(2)}, u32[]{:S(2)}) async-start(bf16[4,64,2048]{2,0,1:T(4,128)(2,1)} %copy.67), calls=%async_computation.1 | async-start | bytes 2097152 | tf_op jit(solution)/shard_map/all_to_all | solution.py:66
  278.3 16.1 %slice-start = ((s8[12582912]{0:T(1024)(128)(4,1)}), s8[4194304]{0:T(1024)(128)(4,1)S(1)}, s32[]{:S(2)}) async-start(s8[12582912]{0:T(1024)(128)(4,1)} %bitcast.37), calls=%async_computation.8 | async-start | bytes 8388608
  278.3 16.1 %slice-start.1 = ((s8[12582912]{0:T(1024)(128)(4,1)}), s8[4194304]{0:T(1024)(128)(4,1)S(1)}, s32[]{:S(2)}) async-start(s8[12582912]{0:T(1024)(128)(4,1)} %bitcast.37), calls=%async_computation.9 | async-start | bytes 8388608
  287.2 7.3 %slice-start.2 = ((s8[12582912]{0:T(1024)(128)(4,1)}), s8[4194304]{0:T(1024)(128)(4,1)S(1)}, s32[]{:S(2)}) async-start(s8[12582912]{0:T(1024)(128)(4,1)} %bitcast.37), calls=%async_computation.10 | async-start | bytes 8388608
  294.5 13.9 %copy-start.5 = (bf16[32,2048]{1,0:T(8,128)(2,1)S(1)}, bf16[32,2048]{1,0:T(8,128)(2,1)}, u32[]{:S(2)}) copy-start(bf16[32,2048]{1,0:T(8,128)(2,1)} %param.11) | copy-start | bytes 393220
  294.5 14.3 %copy-start.10 = (u32[32]{0:T(128)S(1)}, u32[32]{0:T(128)}, u32[]{:S(2)}) copy-start(u32[32]{0:T(128)} %constant.55) | copy-start | bytes 388
  304.6 28.8 %all-to-all-start.3 = ((bf16[4,64,2048]{2,0,1:T(4,128)(2,1)}), bf16[4,64,2048]{2,0,1:T(4,128)(2,1)S(1)}, u32[]{:S(2)}, u32[]{:S(2)}) async-start(bf16[4,64,2048]{2,0,1:T(4,128)(2,1)} %copy.74), calls=%async_computation.3 | async-start | bytes 2097152 | tf_op jit(solution)/shard_map/all_to_all | solution.py:69
  311.9 181.4 %copy-start.1 = (bf16[32,2048]{1,0:T(8,128)(2,1)S(1)}, bf16[32,2048]{1,0:T(8,128)(2,1)}, u32[]{:S(2)}) copy-start(bf16[32,2048]{1,0:T(8,128)(2,1)} %param.10) | copy-start | bytes 393220
Sparse Core Ops, SparseCore 0:
  12.8 84.7 all-gather.3
  99.2 82.0 all-gather.5
  182.9 82.0 all-gather.7
  267.4 220.6 all-reduce.2
where the time goes:
time: 501 us; the launch traced here: 500 us
  waiting for transfers between devices  354 us (71%)
  local copies, waits for them, and re-layouts  55.2 us (11%)
  matrix products  53.2 us (11%)
  starting transfers between devices  18.6 us (4%)
  between operations  14.7 us (3%)
    unnamed x5, waiting for transfers between devices  149 us
    all_gather x1, waiting for transfers between devices, local(): up_piece = lax.all_gather(w_up, 'dp', axis=0, tiled=True)  75.1 us
    all_gather x1, waiting for transfers between devices, local(): down_piece = lax.all_gather(w_down, 'dp', axis=0, tiled=True)  44 us
    all_gather x1, waiting for transfers between devices, local(): gate_piece = lax.all_gather(w_gate, 'dp', axis=0, tiled=True)  37.7 us
    all_to_all x1, waiting for transfers between devices, local(): lax.all_to_all(sent_rows, 'expert', split_axis=1, concat_axis=1, tiled=True)  22.8 us
    convert_element_type x1, local copies, waits for them, and re-layouts, local(): down_grad = lax.psum_scatter(jnp.einsum('lnr,lrd->nld', hidden_all, exper...  21.9 us
    unnamed x35, local copies, waits for them, and re-layouts  20.5 us
    all_to_all x1, waiting for transfers between devices, local(): lax.all_to_all(slot_back.astype(jnp.bfloat16), 'expert', split_axis=1, co...  20.2 us
  transfers between devices with their start and end apart: 8, of which 7 were waited for; matrix products, arithmetic and copies ran while one was open for 20% of the time, Pallas kernels for 0%

commit v1 on v0

--- a/solution.py
+++ b/solution.py
@@ -93,6 +93,111 @@
     return (layer_out, input_grad, weight_grad, down_grad)
 
 
+def hypercube(size):
+    return [1 << bit for bit in range(size.bit_length() - 1)]
+
+
+def gather_rows(rows):
+    expert_peers = lax.axis_size("expert")
+    dp_peers = lax.axis_size("dp")
+    pieces = [rows]
+    for shift in range(1, expert_peers):
+        pairs = [(i, (i + shift) % expert_peers) for i in range(expert_peers)]
+        pieces.append(lax.ppermute(rows, "expert", pairs))
+    held = jnp.concatenate(pieces, axis=0)
+    for bit in reversed(hypercube(dp_peers)):
+        other = lax.ppermute(held, "dp", [(i, i ^ bit) for i in range(dp_peers)])
+        held = jnp.concatenate([held, other], axis=0)
+    return held
+
+
+def scatter_sum(part):
+    expert_peers = lax.axis_size("expert")
+    dp_peers = lax.axis_size("dp")
+    for bit in hypercube(dp_peers):
+        half = part.shape[0] // 2
+        sent = part[half:].astype(jnp.bfloat16)
+        other = lax.ppermute(sent, "dp", [(i, i ^ bit) for i in range(dp_peers)])
+        part = part[:half].astype(jnp.float32) + other.astype(jnp.float32)
+    block = part.shape[0] // expert_peers
+    total = part[:block]
+    for shift in range(1, expert_peers):
+        pairs = [(i, (i - shift) % expert_peers) for i in range(expert_peers)]
+        sent = part[shift * block : (shift + 1) * block].astype(jnp.bfloat16)
+        total = total + lax.ppermute(sent, "expert", pairs).astype(jnp.float32)
+    return total
+
+
+def dot_last(a, b):
+    return lax.dot_general(a, b, (((1,), (1,)), ((), ())), preferred_element_type=jnp.float32)
+
+
+def dot_plain(a, b):
+    return lax.dot_general(a, b, (((1,), (0,)), ((), ())), preferred_element_type=jnp.float32)
+
+
+def dot_first(a, b):
+    return lax.dot_general(a, b, (((0,), (0,)), ((), ())), preferred_element_type=jnp.float32)
+
+
+def local_tokens(tokens, out_grad, expert_ids, slot_pos, combine_weight, w_gate, w_up, w_down):
+    units, local_experts, width = w_gate.shape
+    experts = local_experts * lax.axis_size("expert")
+    first_expert = lax.axis_index("expert") * local_experts
+    picked = (expert_ids[:, :, None] == jnp.arange(experts, dtype=jnp.int32)) & (slot_pos >= 0)[:, :, None]
+    weight = jnp.sum(jnp.where(picked, combine_weight[:, :, None], 0.0), axis=1)
+    high = lax.reduce_precision(weight, 8, 7)
+    side = -(-2 * experts // 128) * 128
+    routed = jnp.concatenate([high, weight - high], axis=1).astype(jnp.bfloat16)
+    routed = jnp.pad(routed, ((0, 0), (0, side - 2 * experts)))
+
+    token_rows = gather_rows(jnp.concatenate([tokens, routed], axis=1))
+    grad_rows = gather_rows(out_grad)
+    weight_rows = token_rows[:, width:]
+    token_rows = token_rows[:, :width]
+
+    unit_rows = units * local_experts
+    gate_w = w_gate.reshape(unit_rows, width)
+    up_w = w_up.reshape(unit_rows, width)
+    down_w = w_down.reshape(unit_rows, width)
+    unit_expert = first_expert + jnp.arange(unit_rows, dtype=jnp.int32) % local_experts
+    columns = jnp.arange(side, dtype=jnp.int32)
+    spread = (columns[:, None] % experts == unit_expert[None, :]) & (columns < 2 * experts)[:, None]
+    collect = (unit_expert[:, None] == columns[None, :]).astype(jnp.bfloat16)
+    mask = dot_plain(weight_rows, spread.astype(jnp.bfloat16))
+
+    gate_pre = dot_last(token_rows, gate_w)
+    up_pre = dot_last(token_rows, up_w)
+    sig = jax.nn.sigmoid(gate_pre)
+    hidden = gate_pre * sig * up_pre
+    hidden_weighted = (hidden * mask).astype(jnp.bfloat16)
+    out_part = dot_plain(hidden_weighted, down_w).astype(jnp.bfloat16)
+    layer_out = scatter_sum(out_part).astype(jnp.bfloat16)
+
+    hidden_grad = dot_last(grad_rows, down_w)
+    product = jnp.where(mask > 0, hidden * hidden_grad, 0.0).astype(jnp.bfloat16)
+    product_part = dot_plain(product, collect).astype(jnp.bfloat16)
+    hidden_grad = hidden_grad * mask
+    gate_grad = (hidden_grad * up_pre * sig * (1.0 + gate_pre * (1.0 - sig))).astype(jnp.bfloat16)
+    up_grad = (hidden_grad * gate_pre * sig).astype(jnp.bfloat16)
+    grad_part = (dot_plain(gate_grad, gate_w) + dot_plain(up_grad, up_w)).astype(jnp.bfloat16)
+    sums = scatter_sum(jnp.concatenate([grad_part, product_part], axis=1))
+    input_grad = sums[:, :width].astype(jnp.bfloat16)
+    per_expert = sums[:, width : width + experts]
+    weight_grad = jnp.sum(jnp.where(picked, per_expert[:, None, :], 0.0), axis=2)
+    down_grad = dot_first(hidden_weighted, grad_rows).astype(jnp.bfloat16)
+    return (layer_out, input_grad, weight_grad, down_grad.reshape(units, local_experts, width))
+
+
+def plan(tokens, out_grad, expert_ids, slot_pos, combine_weight, w_gate, w_up, w_down):
+    args = (tokens, out_grad, expert_ids, slot_pos, combine_weight, w_gate, w_up, w_down)
+    slots = tokens.shape[0] * expert_ids.shape[1] // lax.axis_size("expert")
+    dp_peers = lax.axis_size("dp")
+    if tokens.shape[0] < slots and dp_peers & (dp_peers - 1) == 0:
+        return local_tokens(*args)
+    return local(*args)
+
+
 def solution(mesh):
     in_specs = (
         P(("groups", "expert", "dp"), None),
@@ -110,4 +215,4 @@
         P(("groups", "expert", "dp"), None),
         P(("groups", "dp"), "expert", None),
     )
-    return jax.shard_map(local, mesh=mesh, in_specs=in_specs, out_specs=out_specs, check_vma=False)
+    return jax.shard_map(plan, mesh=mesh, in_specs=in_specs, out_specs=out_specs, check_vma=False)

time: 501 us -> 125 us (0.25)
  waiting for transfers between devices: 354 us -> 51.5 us
  matrix products: 53.2 us -> 16.3 us
  local copies, waits for them, and re-layouts: 55.2 us -> 25.1 us
  between operations: 14.7 us -> 1.06 us
  other arithmetic: 3.72 us -> 9.33 us
    all_gather x3 -> x0, waiting for transfers between devices: 157 us -> none  [the longest x1 75.1 us: local(): up_piece = lax.all_gather(w_up, 'dp', axis=0, tiled=True)]
    unnamed x5 -> x0, waiting for transfers between devices: 149 us -> none
    ppermute x0 -> x20, waiting for transfers between devices: none -> 51.5 us  [the longest x4 21.2 us: scatter_sum(): other = lax.ppermute(sent, 'dp', [(i, i ^ bit) for i in range(dp_peers)])]
    all_to_all x4 -> x0, waiting for transfers between devices: 48.9 us -> none  [the longest x1 22.8 us: local(): lax.all_to_all(sent_rows, 'expert', split_axis=1, concat_axis=1, tiled=True)]
    dot_general x9, matrix products: 53.2 us -> 16.3 us  [the longest x5 7.13 us: dot_plain(): lax.dot_general(a, b, (((1,), (0,)), ((), ())), preferred_element_type=jn...]
    convert_element_type x3 -> x0, local copies, waits for them, and re-layouts: 25.5 us -> none  [the longest x1 21.9 us: local(): down_grad = lax.psum_scatter(jnp.einsum('lnr,lrd->nld', hidden_all, exper...]
    ppermute x0 -> x20, starting transfers between devices: none -> 21 us  [the longest x6 11.9 us: gather_rows(): pieces.append(lax.ppermute(rows, 'expert', pairs))]
    all_to_all x4 -> x0, starting transfers between devices: 18.2 us -> none  [the longest x1 6.32 us: local(): lax.all_to_all(sent_rows, 'expert', split_axis=1, concat_axis=1, tiled=True)]
  transfers between devices with their start and end apart: 8 -> 20, of which waited for: 7 -> 8; matrix products, arithmetic and copies ran while one was open for 20% -> 30% of each run, Pallas kernels for 0% -> 0%
where the time goes in v1:
time: 125 us; the launch traced here: 124 us
  waiting for transfers between devices  51.5 us (41%)
  local copies, waits for them, and re-layouts  25.1 us (20%)
  starting transfers between devices  21 us (17%)
  matrix products  16.3 us (13%)
  other arithmetic  9.33 us (7%)
    ppermute x4, waiting for transfers between devices, scatter_sum(): other = lax.ppermute(sent, 'dp', [(i, i ^ bit) for i in range(dp_peers)])  21.2 us
    ppermute x4, waiting for transfers between devices, gather_rows(): other = lax.ppermute(held, 'dp', [(i, i ^ bit) for i in range(dp_peers)])  19.7 us
    ppermute x6, starting transfers between devices, gather_rows(): pieces.append(lax.ppermute(rows, 'expert', pairs))  11.9 us
    ppermute x6, waiting for transfers between devices, scatter_sum(): total = total + lax.ppermute(sent, 'expert', pairs).astype(jnp.float32)  10.6 us
    dot_general x5, matrix products, dot_plain(): lax.dot_general(a, b, (((1,), (0,)), ((), ())), preferred_element_type=jn...  7.13 us
    reshape x1, local copies, waits for them, and re-layouts, local_tokens(): down_grad.reshape(units, local_experts, width)  5.69 us
    reshape x1, local copies, waits for them, and re-layouts, local_tokens(): gate_w = w_gate.reshape(unit_rows, width)  5.64 us
    dot_general x3, matrix products, dot_last(): lax.dot_general(a, b, (((1,), (1,)), ((), ())), preferred_element_type=jn...  5.5 us
  transfers between devices with their start and end apart: 20, of which 8 were waited for; matrix products, arithmetic and copies ran while one was open for 30% of the time, Pallas kernels for 0%

profile of v1, /device:TPU:0, one launch (start us, length us, event | category | flops | bytes accessed | tf_op | source)
XLA Modules:
  0.0 124.4 jit_solution(11077326068690701492)
XLA Ops:
  0.6 5.1 %collective-permute-start.12 = (bf16[32,2048]{1,0:T(8,128)(2,1)}, bf16[32,2048]{1,0:T(8,128)(2,1)}, u32[]{:S(2)}, u32[]{:S(2)}) collective-permute-start(bf16[32,2048]{1,0:T(8,128)(2,1)} %param.9), channel_id=1, source_target_pairs={{0,12},{4,0},{8,4},{12,8},{1,13},{5,1},{9,5},{13,9},{2,14},{6,2},{... | collective-permute-start | bytes 393224 | tf_op jit(solution)/shard_map/ppermute | solution.py:106
  8.9 1.8 %constant_dynamic-update-slice_fusion.4 = (bf16[256,2176]{1,0:T(8,128)(2,1)}, bf16[512,2176]{1,0:T(8,128)(2,1)}, bf16[32,2176]{1,0:T(8,128)(2,1)}) fusion(bf16[32,128]{1,0:T(8,128)(2,1)S(1)} %pad.4.clone, bf16[32,2048]{1,0:T(8,128)(2,1)} %param.8), kind=kLoop, calls=%fused_computation.58 | loop fusion | flops 278526 | bytes 557056
  10.6 1.9 %collective-permute-start.1 = (bf16[32,2176]{1,0:T(8,128)(2,1)}, bf16[32,2176]{1,0:T(8,128)(2,1)S(1)}, u32[]{:S(2)}, u32[]{:S(2)}) collective-permute-start(bf16[32,2176]{1,0:T(8,128)(2,1)} %get-tuple-element.26), channel_id=1, source_target_pairs={{0,8},{4,12},{8,0},{12,4},{1,9},{5,13},{9,1},{13,5},{2,10},{6,14},... | collective-permute-start | bytes 417800 | tf_op jit(solution)/shard_map/ppermute | solution.py:106
  14.0 5.6 %reshape.63 = bf16[768,2048]{1,0:T(8,128)(2,1)} reshape(bf16[192,4,2048]{2,1,0:T(4,128)(2,1)} %param.13) | data formatting | bytes 6291456 | tf_op jit(solution)/shard_map/reshape | solution.py:160
  19.7 2.9 %reshape.64 = bf16[768,2048]{1,0:T(8,128)(2,1)} reshape(bf16[192,4,2048]{2,1,0:T(4,128)(2,1)S(1)} %copy-done) | data formatting | bytes 6291456 | tf_op jit(solution)/shard_map/reshape | solution.py:161
  22.6 3.7 %reshape.65 = bf16[768,2048]{1,0:T(8,128)(2,1)S(1)} reshape(bf16[192,4,2048]{2,1,0:T(4,128)(2,1)} %param.15) | data formatting | bytes 6291456 | tf_op jit(solution)/shard_map/reshape | solution.py:162
  27.5 2.4 %collective-permute-start.2 = (bf16[32,2176]{1,0:T(8,128)(2,1)}, bf16[32,2176]{1,0:T(8,128)(2,1)S(1)}, u32[]{:S(2)}, u32[]{:S(2)}) collective-permute-start(bf16[32,2176]{1,0:T(8,128)(2,1)} %get-tuple-element.26), channel_id=1, source_target_pairs={{0,12},{4,0},{8,4},{12,8},{1,13},{5,1},{9,5},{13,9},{2,14},{6,2},{... | collective-permute-start | bytes 417800 | tf_op jit(solution)/shard_map/ppermute | solution.py:106
  31.0 1.6 %collective-permute-start.13 = (bf16[128,2048]{1,0:T(8,128)(2,1)S(1)}, bf16[128,2048]{1,0:T(8,128)(2,1)S(1)}, u32[]{:S(2)}, u32[]{:S(2)}) collective-permute-start(bf16[128,2048]{1,0:T(8,128)(2,1)S(1)} %pad_maximum_fusion.2), channel_id=1, source_target_pairs={{0,2},{1,3},{2,0},{3,1},{4,6},{5,7},{6,4},{7,5},{8,10},{9,11},{10,... | collective-permute-start | bytes 1572872 | tf_op jit(solution)/shard_map/ppermute | solution.py:109
  36.1 9.8 %collective-permute-done.13 = bf16[128,2048]{1,0:T(8,128)(2,1)S(1)} collective-permute-done((bf16[128,2048]{1,0:T(8,128)(2,1)S(1)}, bf16[128,2048]{1,0:T(8,128)(2,1)S(1)}, u32[]{:S(2)}, u32[]{:S(2)}) %collective-permute-start.13) | collective-permute-done | bytes 524320 | tf_op jit(solution)/shard_map/ppermute | solution.py:109
  46.1 9.1 %collective-permute-done.3 = bf16[128,2176]{1,0:T(8,128)(2,1)S(1)} collective-permute-done((bf16[128,2176]{1,0:T(8,128)(2,1)S(1)}, bf16[128,2176]{1,0:T(8,128)(2,1)S(1)}, u32[]{:S(2)}, u32[]{:S(2)}) %collective-permute-start.3) | collective-permute-done | bytes 557088 | tf_op jit(solution)/shard_map/ppermute | solution.py:109
  55.6 1.8 %fusion.37 = f32[512,768]{1,0:T(8,128)S(1)} fusion(bf16[512,2048]{1,0:T(8,128)(2,1)S(1)} %constant_dynamic-update-slice_fusion.16, bf16[768,2048]{1,0:T(8,128)(2,1)S(1)} %reshape.65), kind=kOutput, calls=%fused_computation.96 | convolution fusion | flops 1610612736 | bytes 6815744 | tf_op jit(solution)/shard_map/dot_general | solution.py:132
  58.4 1.9 %fusion.2 = f32[512,768]{1,0:T(8,128)S(1)} fusion(bf16[768,2048]{1,0:T(8,128)(2,1)S(1)} %copy-done.2, bf16[512,2176]{1,0:T(8,128)(2,1)S(1)} %constant_dynamic-update-slice_fusion.5), kind=kOutput, calls=%fused_computation.9 | convolution fusion | flops 1610612736 | bytes 6815744 | tf_op jit(solution)/shard_map/dot_general | solution.py:132
  60.3 1.8 %fusion = f32[512,768]{1,0:T(8,128)S(1)} fusion(bf16[768,2048]{1,0:T(8,128)(2,1)S(1)} %copy-done.1, bf16[512,2176]{1,0:T(8,128)(2,1)S(1)} %constant_dynamic-update-slice_fusion.5), kind=kOutput, calls=%fused_computation.7 | convolution fusion | flops 1610612736 | bytes 6815744 | tf_op jit(solution)/shard_map/dot_general | solution.py:132
  62.8 1.8 %convolution_convert_fusion.1 = bf16[512,2048]{1,0:T(8,128)(2,1)S(1)} fusion(bf16[512,768]{1,0:T(8,128)(2,1)S(1)} %get-tuple-element.37, bf16[768,2048]{1,0:T(8,128)(2,1)S(1)} %reshape.65), kind=kOutput, calls=%fused_computation.2 | convolution fusion | flops 1611661312 | bytes 6029312 | tf_op jit(solution)/shard_map/dot_general | solution.py:136
  64.6 2.1 %fusion.5 = f32[512,2048]{1,0:T(8,128)S(1)} fusion(bf16[768,2048]{1,0:T(8,128)(2,1)S(1)} %copy-done.2, f32[512,768]{1,0:T(8,128)S(1)} %fusion.2, f32[512,768]{1,0:T(8,128)S(1)} %fusion, f32[512,768]{1,0:T(8,128)S(1)} %fusion.37, f32[512,768]{1,0:T(8,128)S(1)} %get-tuple-element.38), kind=kOutput, calls=%fused_computation.24 | convolution fusion | flops 1614938112 | bytes 13631488 | tf_op jit(solution)/shard_map/dot_general | solution.py:136
  66.7 1.9 %add_convert_fusion = bf16[512,2048]{1,0:T(8,128)(2,1)S(1)} fusion(f32[512,2048]{1,0:T(8,128)S(1)} %fusion.5, bf16[768,2048]{1,0:T(8,128)(2,1)S(1)} %copy-done.1, f32[512,768]{1,0:T(8,128)S(1)} %fusion.2, f32[512,768]{1,0:T(8,128)S(1)} %fusion.37, f32[512,768]{1,0:T(8,128)S(1)} %get-tuple-element.38), kind=kOutput, calls=%fused_computation | convolution fusion | flops 1615462400 | bytes 14155776 | tf_op jit(solution)/shard_map/dot_general | solution.py:136
  72.0 3.7 %convolution_convert_fusion = bf16[768,2048]{1,0:T(8,128)(2,1)} fusion(bf16[512,768]{1,0:T(8,128)(2,1)S(1)} %get-tuple-element.37, bf16[512,2048]{1,0:T(8,128)(2,1)S(1)} %constant_dynamic-update-slice_fusion.16), kind=kOutput, calls=%fused_computation.1 | convolution fusion | flops 1612185600 | bytes 6029312 | tf_op jit(solution)/shard_map/dot_general | solution.py:140
  75.7 5.7 %reshape.66 = bf16[192,4,2048]{2,1,0:T(4,128)(2,1)} reshape(bf16[768,2048]{1,0:T(8,128)(2,1)} %convolution_convert_fusion) | data formatting | bytes 6291456 | tf_op jit(solution)/shard_map/reshape | solution.py:189
  81.4 1.9 %convert_add_fusion.1 = f32[256,2048]{1,0:T(8,128)S(1)} fusion(bf16[256,2048]{1,0:T(8,128)(2,1)} %collective-permute-done.5, bf16[512,2048]{1,0:T(8,128)(2,1)} %copy-done.3), kind=kLoop, calls=%fused_computation.6 | loop fusion | flops 1572864 | bytes 4194304 | tf_op jit(solution)/shard_map/add | solution.py:121
  85.9 12.4 %collective-permute-done.6 = bf16[128,2048]{1,0:T(8,128)(2,1)S(1)} collective-permute-done((bf16[128,2048]{1,0:T(8,128)(2,1)S(1)}, bf16[128,2048]{1,0:T(8,128)(2,1)S(1)}, u32[]{:S(2)}, u32[]{:S(2)}) %collective-permute-start.6) | collective-permute-done | bytes 524320 | tf_op jit(solution)/shard_map/ppermute | solution.py:120
  100.5 8.8 %collective-permute-done.16 = bf16[128,2176]{1,0:T(8,128)(2,1)S(1)} collective-permute-done((bf16[128,2176]{1,0:T(8,128)(2,1)S(1)}, bf16[128,2176]{1,0:T(8,128)(2,1)S(1)}, u32[]{:S(2)}, u32[]{:S(2)}) %collective-permute-start.16) | collective-permute-done | bytes 557088 | tf_op jit(solution)/shard_map/ppermute | solution.py:120
  112.4 4.0 %collective-permute-done.17 = bf16[32,2176]{1,0:T(8,128)(2,1)S(1)} collective-permute-done((bf16[32,2176]{1,0:T(8,128)(2,1)S(1)}, bf16[32,2176]{1,0:T(8,128)(2,1)S(1)}, u32[]{:S(2)}, u32[]{:S(2)}) %collective-permute-start.17) | collective-permute-done | bytes 139296 | tf_op jit(solution)/shard_map/ppermute | solution.py:127
  116.4 2.0 %collective-permute-done.19 = bf16[32,2176]{1,0:T(8,128)(2,1)S(1)} collective-permute-done((bf16[32,2176]{1,0:T(8,128)(2,1)S(1)}, bf16[32,2176]{1,0:T(8,128)(2,1)S(1)}, u32[]{:S(2)}, u32[]{:S(2)}) %collective-permute-start.19) | collective-permute-done | bytes 139296 | tf_op jit(solution)/shard_map/ppermute | solution.py:127
  118.4 4.5 %collective-permute-done.18 = bf16[32,2176]{1,0:T(8,128)(2,1)S(1)} collective-permute-done((bf16[32,2176]{1,0:T(8,128)(2,1)S(1)}, bf16[32,2176]{1,0:T(8,128)(2,1)S(1)}, u32[]{:S(2)}, u32[]{:S(2)}) %collective-permute-start.18) | collective-permute-done | bytes 139296 | tf_op jit(solution)/shard_map/ppermute | solution.py:127
  (92 shorter events, 24.9 us)
Async XLA Ops:
  0.6 26.8 %collective-permute-start.12 = (bf16[32,2048]{1,0:T(8,128)(2,1)}, bf16[32,2048]{1,0:T(8,128)(2,1)}, u32[]{:S(2)}, u32[]{:S(2)}) collective-permute-start(bf16[32,2048]{1,0:T(8,128)(2,1)} %param.9), channel_id=1, source_target_pairs={{0,12},{4,0},{8,4},{12,8},{1,13},{5,1},{9,5},{13,9},{2,14},{6,2},{... | collective-permute-start | bytes 393224 | tf_op jit(solution)/shard_map/ppermute | solution.py:106
  5.7 24.1 %collective-permute-start.11 = (bf16[32,2048]{1,0:T(8,128)(2,1)}, bf16[32,2048]{1,0:T(8,128)(2,1)}, u32[]{:S(2)}, u32[]{:S(2)}) collective-permute-start(bf16[32,2048]{1,0:T(8,128)(2,1)} %param.9), channel_id=1, source_target_pairs={{0,8},{4,12},{8,0},{12,4},{1,9},{5,13},{9,1},{13,5},{2,10},{6,14},... | collective-permute-start | bytes 393224 | tf_op jit(solution)/shard_map/ppermute | solution.py:106
  5.7 24.1 %collective-permute-start.10 = (bf16[32,2048]{1,0:T(8,128)(2,1)}, bf16[32,2048]{1,0:T(8,128)(2,1)}, u32[]{:S(2)}, u32[]{:S(2)}) collective-permute-start(bf16[32,2048]{1,0:T(8,128)(2,1)} %param.9), channel_id=1, source_target_pairs={{0,4},{4,8},{8,12},{12,0},{1,5},{5,9},{9,13},{13,1},{2,6},{6,10},{... | collective-permute-start | bytes 393224 | tf_op jit(solution)/shard_map/ppermute | solution.py:106
  10.6 24.7 %collective-permute-start.1 = (bf16[32,2176]{1,0:T(8,128)(2,1)}, bf16[32,2176]{1,0:T(8,128)(2,1)S(1)}, u32[]{:S(2)}, u32[]{:S(2)}) collective-permute-start(bf16[32,2176]{1,0:T(8,128)(2,1)} %get-tuple-element.26), channel_id=1, source_target_pairs={{0,8},{4,12},{8,0},{12,4},{1,9},{5,13},{9,1},{13,5},{2,10},{6,14},... | collective-permute-start | bytes 417800 | tf_op jit(solution)/shard_map/ppermute | solution.py:106
  12.6 22.8 %collective-permute-start = (bf16[32,2176]{1,0:T(8,128)(2,1)}, bf16[32,2176]{1,0:T(8,128)(2,1)S(1)}, u32[]{:S(2)}, u32[]{:S(2)}) collective-permute-start(bf16[32,2176]{1,0:T(8,128)(2,1)} %get-tuple-element.26), channel_id=1, source_target_pairs={{0,4},{4,8},{8,12},{12,0},{1,5},{5,9},{9,13},{13,1},{2,6},{6,10},{... | collective-permute-start | bytes 417800 | tf_op jit(solution)/shard_map/ppermute | solution.py:106
  26.3 9.7 %copy-start.7 = (bf16[256,2176]{1,0:T(8,128)(2,1)S(1)}, bf16[256,2176]{1,0:T(8,128)(2,1)}, u32[]{:S(2)}) copy-start(bf16[256,2176]{1,0:T(8,128)(2,1)} %get-tuple-element.24) | copy-start | bytes 3342340
  26.4 9.7 %copy-start.11 = (bf16[512,2176]{1,0:T(8,128)(2,1)S(1)}, bf16[512,2176]{1,0:T(8,128)(2,1)}, u32[]{:S(2)}) copy-start(bf16[512,2176]{1,0:T(8,128)(2,1)} %get-tuple-element.25) | copy-start | bytes 6684676
  27.5 7.9 %collective-permute-start.2 = (bf16[32,2176]{1,0:T(8,128)(2,1)}, bf16[32,2176]{1,0:T(8,128)(2,1)S(1)}, u32[]{:S(2)}, u32[]{:S(2)}) collective-permute-start(bf16[32,2176]{1,0:T(8,128)(2,1)} %get-tuple-element.26), channel_id=1, source_target_pairs={{0,12},{4,0},{8,4},{12,8},{1,13},{5,1},{9,5},{13,9},{2,14},{6,2},{... | collective-permute-start | bytes 417800 | tf_op jit(solution)/shard_map/ppermute | solution.py:106
  31.0 14.9 %collective-permute-start.13 = (bf16[128,2048]{1,0:T(8,128)(2,1)S(1)}, bf16[128,2048]{1,0:T(8,128)(2,1)S(1)}, u32[]{:S(2)}, u32[]{:S(2)}) collective-permute-start(bf16[128,2048]{1,0:T(8,128)(2,1)S(1)} %pad_maximum_fusion.2), channel_id=1, source_target_pairs={{0,2},{1,3},{2,0},{3,1},{4,6},{5,7},{6,4},{7,5},{8,10},{9,11},{10,... | collective-permute-start | bytes 1572872 | tf_op jit(solution)/shard_map/ppermute | solution.py:109
  35.5 19.8 %collective-permute-start.3 = (bf16[128,2176]{1,0:T(8,128)(2,1)S(1)}, bf16[128,2176]{1,0:T(8,128)(2,1)S(1)}, u32[]{:S(2)}, u32[]{:S(2)}) collective-permute-start(bf16[128,2176]{1,0:T(8,128)(2,1)S(1)} %pad_maximum_fusion.1), channel_id=1, source_target_pairs={{0,2},{1,3},{2,0},{3,1},{4,6},{5,7},{6,4},{7,5},{8,10},{9,11},{10,... | collective-permute-start | bytes 1671176 | tf_op jit(solution)/shard_map/ppermute | solution.py:109
  46.0 9.5 %collective-permute-start.14 = (bf16[256,2048]{1,0:T(8,128)(2,1)S(1)}, bf16[256,2048]{1,0:T(8,128)(2,1)S(1)}, u32[]{:S(2)}, u32[]{:S(2)}) collective-permute-start(bf16[256,2048]{1,0:T(8,128)(2,1)S(1)} %get-tuple-element.13), channel_id=1, source_target_pairs={{0,1},{1,0},{2,3},{3,2},{4,5},{5,4},{6,7},{7,6},{8,9},{9,8},{10,11... | collective-permute-start | bytes 3145736 | tf_op jit(solution)/shard_map/ppermute | solution.py:109
  55.4 2.8 %collective-permute-start.4 = (bf16[256,2176]{1,0:T(8,128)(2,1)S(1)}, bf16[256,2176]{1,0:T(8,128)(2,1)S(1)}, u32[]{:S(2)}, u32[]{:S(2)}) collective-permute-start(bf16[256,2176]{1,0:T(8,128)(2,1)S(1)} %get-tuple-element.11), channel_id=1, source_target_pairs={{0,1},{1,0},{2,3},{3,2},{4,5},{5,4},{6,7},{7,6},{8,9},{9,8},{10,11... | collective-permute-start | bytes 3342344 | tf_op jit(solution)/shard_map/ppermute | solution.py:109
  69.7 11.7 %collective-permute-start.5 = (bf16[256,2048]{1,0:T(8,128)(2,1)}, bf16[256,2048]{1,0:T(8,128)(2,1)}, u32[]{:S(2)}, u32[]{:S(2)}) collective-permute-start(bf16[256,2048]{1,0:T(8,128)(2,1)} %slice.92), channel_id=1, source_target_pairs={{0,1},{1,0},{2,3},{3,2},{4,5},{5,4},{6,7},{7,6},{8,9},{9,8},{10,11... | collective-permute-start | bytes 3145736 | tf_op jit(solution)/shard_map/ppermute | solution.py:120
  71.7 13.3 %collective-permute-start.15 = (bf16[256,2176]{1,0:T(8,128)(2,1)}, bf16[256,2176]{1,0:T(8,128)(2,1)S(1)}, u32[]{:S(2)}, u32[]{:S(2)}) collective-permute-start(bf16[256,2176]{1,0:T(8,128)(2,1)} %pad_maximum_fusion), channel_id=1, source_target_pairs={{0,1},{1,0},{2,3},{3,2},{4,5},{5,4},{6,7},{7,6},{8,9},{9,8},{10,11... | collective-permute-start | bytes 3342344 | tf_op jit(solution)/shard_map/ppermute | solution.py:120
  83.4 14.8 %collective-permute-start.6 = (bf16[128,2048]{1,0:T(8,128)(2,1)S(1)}, bf16[128,2048]{1,0:T(8,128)(2,1)S(1)}, u32[]{:S(2)}, u32[]{:S(2)}) collective-permute-start(bf16[128,2048]{1,0:T(8,128)(2,1)S(1)} %slice.142), channel_id=1, source_target_pairs={{0,2},{1,3},{2,0},{3,1},{4,6},{5,7},{6,4},{7,5},{8,10},{9,11},{10,... | collective-permute-start | bytes 1572872 | tf_op jit(solution)/shard_map/ppermute | solution.py:120
  85.3 24.1 %collective-permute-start.16 = (bf16[128,2176]{1,0:T(8,128)(2,1)S(1)}, bf16[128,2176]{1,0:T(8,128)(2,1)S(1)}, u32[]{:S(2)}, u32[]{:S(2)}) collective-permute-start(bf16[128,2176]{1,0:T(8,128)(2,1)S(1)} %slice.141), channel_id=1, source_target_pairs={{0,2},{1,3},{2,0},{3,1},{4,6},{5,7},{6,4},{7,5},{8,10},{9,11},{10,... | collective-permute-start | bytes 1671176 | tf_op jit(solution)/shard_map/ppermute | solution.py:120
  98.4 13.2 %collective-permute-start.7 = (bf16[32,2048]{1,0:T(8,128)(2,1)S(1)}, bf16[32,2048]{1,0:T(8,128)(2,1)S(1)}, u32[]{:S(2)}, u32[]{:S(2)}) collective-permute-start(bf16[32,2048]{1,0:T(8,128)(2,1)S(1)} %get-tuple-element.15), channel_id=1, source_target_pairs={{0,12},{4,0},{8,4},{12,8},{1,13},{5,1},{9,5},{13,9},{2,14},{6,2},{... | collective-permute-start | bytes 393224 | tf_op jit(solution)/shard_map/ppermute | solution.py:127
  99.3 12.3 %collective-permute-start.9 = (bf16[32,2048]{1,0:T(8,128)(2,1)S(1)}, bf16[32,2048]{1,0:T(8,128)(2,1)S(1)}, u32[]{:S(2)}, u32[]{:S(2)}) collective-permute-start(bf16[32,2048]{1,0:T(8,128)(2,1)S(1)} %get-tuple-element.16), channel_id=1, source_target_pairs={{0,4},{4,8},{8,12},{12,0},{1,5},{5,9},{9,13},{13,1},{2,6},{6,10},{... | collective-permute-start | bytes 393224 | tf_op jit(solution)/shard_map/ppermute | solution.py:127
  100.5 11.1 %collective-permute-start.8 = (bf16[32,2048]{1,0:T(8,128)(2,1)S(1)}, bf16[32,2048]{1,0:T(8,128)(2,1)S(1)}, u32[]{:S(2)}, u32[]{:S(2)}) collective-permute-start(bf16[32,2048]{1,0:T(8,128)(2,1)S(1)} %get-tuple-element.17), channel_id=1, source_target_pairs={{0,8},{4,12},{8,0},{12,4},{1,9},{5,13},{9,1},{13,5},{2,10},{6,14},... | collective-permute-start | bytes 393224 | tf_op jit(solution)/shard_map/ppermute | solution.py:127
  109.5 14.3 %copy-start.8 = (s32[32,8]{0,1:T(8,128)S(1)}, s32[32,8]{0,1:T(8,128)}, u32[]{:S(2)}) copy-start(s32[32,8]{0,1:T(8,128)} %param.10) | copy-start | bytes 3076
  109.5 14.2 %copy-start.10 = (pred[32,8]{0,1:T(8,128)(4,1)S(1)}, pred[32,8]{0,1:T(8,128)(4,1)}, u32[]{:S(2)}) copy-start(pred[32,8]{0,1:T(8,128)(4,1)} %copy-done.9) | copy-start | bytes 772
  109.6 6.8 %collective-permute-start.17 = (bf16[32,2176]{1,0:T(8,128)(2,1)S(1)}, bf16[32,2176]{1,0:T(8,128)(2,1)S(1)}, u32[]{:S(2)}, u32[]{:S(2)}) collective-permute-start(bf16[32,2176]{1,0:T(8,128)(2,1)S(1)} %get-tuple-element.8), channel_id=1, source_target_pairs={{0,12},{4,0},{8,4},{12,8},{1,13},{5,1},{9,5},{13,9},{2,14},{6,2},{... | collective-permute-start | bytes 417800 | tf_op jit(solution)/shard_map/ppermute | solution.py:127
  110.5 8.0 %collective-permute-start.19 = (bf16[32,2176]{1,0:T(8,128)(2,1)S(1)}, bf16[32,2176]{1,0:T(8,128)(2,1)S(1)}, u32[]{:S(2)}, u32[]{:S(2)}) collective-permute-start(bf16[32,2176]{1,0:T(8,128)(2,1)S(1)} %get-tuple-element.9), channel_id=1, source_target_pairs={{0,4},{4,8},{8,12},{12,0},{1,5},{5,9},{9,13},{13,1},{2,6},{6,10},{... | collective-permute-start | bytes 417800 | tf_op jit(solution)/shard_map/ppermute | solution.py:127
  111.6 11.3 %collective-permute-start.18 = (bf16[32,2176]{1,0:T(8,128)(2,1)S(1)}, bf16[32,2176]{1,0:T(8,128)(2,1)S(1)}, u32[]{:S(2)}, u32[]{:S(2)}) collective-permute-start(bf16[32,2176]{1,0:T(8,128)(2,1)S(1)} %get-tuple-element.10), channel_id=1, source_target_pairs={{0,8},{4,12},{8,0},{12,4},{1,9},{5,13},{9,1},{13,5},{2,10},{6,14},... | collective-permute-start | bytes 417800 | tf_op jit(solution)/shard_map/ppermute | solution.py:127
  (8 other events, 34.8 us)

commit v2 on v0

--- a/solution.py
+++ b/solution.py
@@ -1,6 +1,8 @@
 import jax
 import jax.numpy as jnp
 from jax import lax
+from jax.experimental import pallas as pl
+from jax.experimental.pallas import tpu as pltpu
 from jax.sharding import PartitionSpec as P
 
 
@@ -93,6 +95,370 @@
     return (layer_out, input_grad, weight_grad, down_grad)
 
 
+def over_z(rows, shift):
+    peers = lax.axis_size("expert")
+    return lax.ppermute(rows, "expert", [(i, (i + shift) % peers) for i in range(peers)])
+
+
+def over_dp(rows, bit):
+    return lax.ppermute(rows, "dp", [(i, i ^ bit) for i in range(lax.axis_size("dp"))])
+
+
+def after(value, *others):
+    return lax.optimization_barrier((value,) + others)[0]
+
+
+def add(kept, other):
+    return kept.astype(jnp.float32) + other.astype(jnp.float32)
+
+
+def narrow(rows):
+    return rows.astype(jnp.bfloat16)
+
+
+def cross_x(part):
+    block = part.shape[0] // 8
+    far_x = over_dp(part[7 * block :], 2)
+    rest_x = over_dp(part[4 * block : 7 * block], 2)
+    far = narrow(add(part[3 * block : 4 * block], far_x))
+    rest = add(part[: 3 * block], rest_x)
+    return rest[:block], narrow(rest[block : 2 * block]), narrow(rest[2 * block :]), far
+
+
+def cross_z(own, near_left, near_right, far):
+    far_sum = over_z(far, -2)
+    left, right = over_z(near_left, -1), over_z(near_right, -3)
+    return add(own, far_sum) + add(left, right)
+
+
+def dot_last(a, b):
+    return lax.dot_general(a, b, (((1,), (1,)), ((), ())), preferred_element_type=jnp.float32)
+
+
+def dot_plain(a, b):
+    return lax.dot_general(a, b, (((1,), (0,)), ((), ())), preferred_element_type=jnp.float32)
+
+
+def dot_first(a, b):
+    return lax.dot_general(a, b, (((0,), (0,)), ((), ())), preferred_element_type=jnp.float32)
+
+
+UNIT_TILE = 256
+WIDTH_TILE = 512
+
+
+def place_rows(pieces, rows):
+    start = 0
+    for piece in pieces:
+        count = piece.shape[0]
+        rows[pl.ds(start, count), :] = piece[...]
+        start += count
+
+
+def forward_kernel(spread, collect, *refs):
+    del collect
+    pieces, refs = refs[:5], refs[5:]
+    gate_a, gate_b, up_a, up_b, down_a, down_b, out, gate_out, up_out, mask, weighted, rows = refs
+    step = pl.program_id(0)
+    tiles = weighted.shape[1] // UNIT_TILE
+    features = gate_a.shape[1]
+
+    @pl.when(step == 0)
+    def _():
+        place_rows(pieces, rows)
+        mask[...] = dot_plain(rows[:, features:], spread[...])
+
+    def units(gate_w, up_w):
+        token_rows = rows[:, :features]
+        gate_pre = dot_last(token_rows, gate_w[...])
+        up_pre = dot_last(token_rows, up_w[...])
+        gate_out[...] = gate_pre
+        up_out[...] = up_pre
+        hidden = gate_pre * jax.nn.sigmoid(gate_pre) * up_pre
+        at = pl.multiple_of(step * UNIT_TILE, UNIT_TILE)
+        weighted[:, pl.ds(at, UNIT_TILE)] = (hidden * mask[...]).astype(jnp.bfloat16)
+
+    @pl.when(step < tiles // 2)
+    def _():
+        units(gate_a, up_a)
+
+    @pl.when((step >= tiles // 2) & (step < tiles))
+    def _():
+        units(gate_b, up_b)
+
+    @pl.when(step >= tiles)
+    def _():
+        half = down_a.shape[0]
+        total = dot_plain(weighted[:, :half], down_a[...]) + dot_plain(weighted[:, half:], down_b[...])
+        out[...] = total.astype(jnp.bfloat16)
+
+
+def backward_kernel(spread, collect, *refs):
+    del spread
+    pieces, refs = refs[:6], refs[6:]
+    gate_a, gate_b, up_a, up_b, down_a, down_b, gate_in, up_in, mask, out, product_out, rows, gate_grad, up_grad, product = refs
+    step = pl.program_id(0)
+    tiles = gate_grad.shape[1] // UNIT_TILE
+
+    @pl.when(step == 0)
+    def _():
+        place_rows(pieces, rows)
+        product[...] = jnp.zeros_like(product)
+
+    def units(down_w):
+        hidden_grad = dot_last(rows[...], down_w[...])
+        gate_pre, up_pre, weight = gate_in[...], up_in[...], mask[...]
+        sig = jax.nn.sigmoid(gate_pre)
+        gate_sig = gate_pre * sig
+        product[...] += jnp.where(weight > 0, gate_sig * up_pre * hidden_grad, 0.0)
+        hidden_grad = hidden_grad * weight
+        at = pl.multiple_of(step * UNIT_TILE, UNIT_TILE)
+        slope = sig * (1.0 + gate_pre * (1.0 - sig))
+        gate_grad[:, pl.ds(at, UNIT_TILE)] = (hidden_grad * up_pre * slope).astype(jnp.bfloat16)
+        up_grad[:, pl.ds(at, UNIT_TILE)] = (hidden_grad * gate_sig).astype(jnp.bfloat16)
+
+    @pl.when(step < tiles // 2)
+    def _():
+        units(down_a)
+
+    @pl.when((step >= tiles // 2) & (step < tiles))
+    def _():
+        units(down_b)
+
+    @pl.when(step == tiles)
+    def _():
+        product_out[...] = dot_plain(product[...].astype(jnp.bfloat16), collect[...]).astype(jnp.bfloat16)
+
+    @pl.when(step >= tiles)
+    def _():
+        half = gate_a.shape[0]
+        total = dot_plain(gate_grad[:, :half], gate_a[...]) + dot_plain(gate_grad[:, half:], gate_b[...])
+        total += dot_plain(up_grad[:, :half], up_a[...]) + dot_plain(up_grad[:, half:], up_b[...])
+        out[...] = total.astype(jnp.bfloat16)
+
+
+def merge_kernel(gate, up, down, merged):
+    for slot, part in enumerate((gate, up, down)):
+        merged[slot] = part[...].reshape(merged.shape[1:])
+
+
+def merge_units(gate, up, down):
+    units, experts, features = gate.shape
+    tile = 32
+    block = pl.BlockSpec((tile, experts, features), lambda i: (i, 0, 0))
+    return pl.pallas_call(
+        merge_kernel,
+        grid=(units // tile,),
+        in_specs=[block] * 3,
+        out_specs=pl.BlockSpec((3, tile * experts, features), lambda i: (0, i, 0)),
+        out_shape=jax.ShapeDtypeStruct((3, units * experts, features), gate.dtype),
+        compiler_params=pltpu.CompilerParams(**PARAMS),
+        cost_estimate=pl.CostEstimate(flops=0, bytes_accessed=12 * gate.size, transcendentals=0),
+        name="merge_units",
+    )(gate, up, down)
+
+
+def whole(array):
+    return pl.BlockSpec(array.shape, lambda i: (0, 0))
+
+
+def by_units(array, slot, first):
+    last = array.shape[1] // UNIT_TILE - 1
+    return pl.BlockSpec((None, UNIT_TILE, array.shape[2]), lambda i: (slot, jnp.clip(i - first, 0, last), 0))
+
+
+def by_width(array, slot, first):
+    return pl.BlockSpec((None, array.shape[1], WIDTH_TILE), lambda i: (slot, 0, jnp.maximum(i - first, 0)))
+
+
+def unit_columns(rows, tiles):
+    return pl.BlockSpec((rows, UNIT_TILE), lambda i: (0, jnp.minimum(i, tiles - 1)))
+
+
+def width_columns(rows, tiles):
+    return pl.BlockSpec((rows, WIDTH_TILE), lambda i: (0, jnp.maximum(i - tiles, 0)))
+
+
+def cost(rows, units, features, products):
+    return pl.CostEstimate(
+        flops=2 * rows * units * features * products,
+        bytes_accessed=6 * units * features + 4 * rows * features,
+        transcendentals=rows * units,
+    )
+
+
+PARAMS = dict(dimension_semantics=("arbitrary",), vmem_limit_bytes=48 * 1024 * 1024)
+
+
+def forward(tables, pieces, weights):
+    half, features = weights[0].shape[1:]
+    rows = sum(piece.shape[0] for piece in pieces)
+    tiles = 2 * half // UNIT_TILE
+    operands = [*tables, *pieces, *weights * 3]
+    specs = [whole(x) for x in (*tables, *pieces)]
+    specs += [by_units(w, slot, n * tiles // 2) for slot in range(2) for n, w in enumerate(weights)]
+    specs += [by_width(w, 2, tiles) for w in weights]
+    return pl.pallas_call(
+        forward_kernel,
+        grid=(tiles + features // WIDTH_TILE,),
+        in_specs=specs,
+        out_specs=[
+            width_columns(rows, tiles),
+            unit_columns(rows, tiles),
+            unit_columns(rows, tiles),
+            pl.BlockSpec((rows, UNIT_TILE), lambda i: (0, 0)),
+            pl.BlockSpec((rows, 2 * half), lambda i: (0, 0)),
+        ],
+        out_shape=[
+            jax.ShapeDtypeStruct((rows, features), jnp.bfloat16),
+            jax.ShapeDtypeStruct((rows, 2 * half), jnp.float32),
+            jax.ShapeDtypeStruct((rows, 2 * half), jnp.float32),
+            jax.ShapeDtypeStruct((rows, UNIT_TILE), jnp.float32),
+            jax.ShapeDtypeStruct((rows, 2 * half), jnp.bfloat16),
+        ],
+        scratch_shapes=[pltpu.VMEM((rows, pieces[0].shape[1]), jnp.bfloat16)],
+        compiler_params=pltpu.CompilerParams(**PARAMS),
+        cost_estimate=cost(rows, 2 * half, features, 3),
+        name="forward_products",
+    )(*operands)
+
+
+def backward(tables, pieces, weights, gate_pre, up_pre, mask):
+    half, features = weights[0].shape[1:]
+    rows = sum(piece.shape[0] for piece in pieces)
+    tiles = 2 * half // UNIT_TILE
+    operands = [*tables, *pieces, *weights * 3, gate_pre, up_pre, mask]
+    specs = [whole(x) for x in (*tables, *pieces)]
+    specs += [by_width(w, slot, tiles) for slot in range(2) for w in weights]
+    specs += [by_units(w, 2, n * tiles // 2) for n, w in enumerate(weights)]
+    specs += [unit_columns(rows, tiles), unit_columns(rows, tiles), whole(mask)]
+    side = tables[1].shape[1]
+    return pl.pallas_call(
+        backward_kernel,
+        grid=(tiles + features // WIDTH_TILE,),
+        in_specs=specs,
+        out_specs=[
+            width_columns(rows, tiles),
+            pl.BlockSpec((rows, side), lambda i: (0, 0)),
+            pl.BlockSpec((rows, features), lambda i: (0, 0)),
+        ],
+        out_shape=[
+            jax.ShapeDtypeStruct((rows, features), jnp.bfloat16),
+            jax.ShapeDtypeStruct((rows, side), jnp.bfloat16),
+            jax.ShapeDtypeStruct((rows, features), jnp.bfloat16),
+        ],
+        scratch_shapes=[
+            pltpu.VMEM((rows, 2 * half), jnp.bfloat16),
+            pltpu.VMEM((rows, 2 * half), jnp.bfloat16),
+            pltpu.VMEM((rows, UNIT_TILE), jnp.float32),
+        ],
+        compiler_params=pltpu.CompilerParams(**PARAMS),
+        cost_estimate=cost(rows, 2 * half, features, 3),
+        name="backward_products",
+    )(*operands)
+
+
+def share_kernel(weighted, rows, other, out):
+    total = dot_first(weighted[...], rows[...]) + other[...].astype(jnp.float32)
+    out[...] = total.astype(jnp.bfloat16).reshape(out.shape)
+
+
+def finish_share(weighted, rows, other, local_experts):
+    count, features = rows.shape
+    units = other.shape[0] // local_experts
+    tile = UNIT_TILE // local_experts
+    return pl.pallas_call(
+        share_kernel,
+        grid=(units // tile,),
+        in_specs=[
+            pl.BlockSpec((count, UNIT_TILE), lambda i: (0, i)),
+            whole(rows),
+            pl.BlockSpec((UNIT_TILE, features), lambda i: (i, 0)),
+        ],
+        out_specs=pl.BlockSpec((tile, local_experts, features), lambda i: (i, 0, 0)),
+        out_shape=jax.ShapeDtypeStruct((units, local_experts, features), jnp.bfloat16),
+        compiler_params=pltpu.CompilerParams(**PARAMS),
+        cost_estimate=pl.CostEstimate(
+            flops=2 * count * other.size, bytes_accessed=4 * other.size, transcendentals=0
+        ),
+        name="finish_share",
+    )(weighted, rows, other)
+
+
+def local_tokens(tokens, out_grad, expert_ids, slot_pos, combine_weight, w_gate, w_up, w_down):
+    units, local_experts, width = w_gate.shape
+    experts = local_experts * lax.axis_size("expert")
+    first_expert = lax.axis_index("expert") * local_experts
+    unit_rows = units * local_experts
+    picked = (expert_ids[:, :, None] == jnp.arange(experts, dtype=jnp.int32)) & (slot_pos >= 0)[:, :, None]
+    weight = jnp.sum(jnp.where(picked, combine_weight[:, :, None], 0.0), axis=1)
+    high = lax.reduce_precision(weight, 8, 7)
+    side = -(-2 * experts // 128) * 128
+    routed = jnp.concatenate([high, weight - high], axis=1).astype(jnp.bfloat16)
+    routed = jnp.pad(routed, ((0, 0), (0, side - 2 * experts)))
+    unit_expert = first_expert + jnp.arange(UNIT_TILE, dtype=jnp.int32) % local_experts
+    columns = jnp.arange(side, dtype=jnp.int32)
+    spread = (columns[:, None] % experts == unit_expert[None, :]) & (columns < 2 * experts)[:, None]
+    collect = (unit_expert[:, None] == columns[None, :]).astype(jnp.bfloat16)
+    tables = (spread.astype(jnp.bfloat16), collect)
+
+    own_t = jnp.concatenate([tokens, routed], axis=1)
+    own_t, own_g, w_gate = lax.optimization_barrier((own_t, out_grad, w_gate))
+    column_t = [over_z(own_t, 1), over_z(own_t, 3), over_z(own_t, 2)]
+    own_gx = over_dp(own_g, 2)
+    weights = merge_units(w_gate, w_up, w_down)
+    column_t, own_gx, own_g, weights = lax.optimization_barrier((column_t, own_gx, own_g, weights))
+
+    pieces_t = [own_t, *column_t]
+    column_tx = over_dp(jnp.concatenate(pieces_t, axis=0), 2)
+    near_g = [over_z(own_g, 1), over_z(own_g, 3)]
+    far_g = over_z(own_g, 2)
+    weights_b = over_dp(weights, 1)
+    near_g, far_g, column_tx = lax.optimization_barrier((near_g, far_g, column_tx))
+
+    away_gx = over_dp(jnp.concatenate([*near_g, far_g], axis=0), 2)
+    weights = [weights, weights_b]
+    out_part, gate_pre, up_pre, mask, weighted = forward(tables, [*pieces_t, column_tx], weights)
+    out_part, away_gx = lax.optimization_barrier((out_part, away_gx))
+    out_pieces = cross_x(out_part)
+
+    grad_pieces = [out_grad, *near_g, far_g, own_gx, away_gx]
+    grad_part, product_part, grad_rows = backward(tables, grad_pieces, weights, gate_pre, up_pre, mask)
+    grad_part = jnp.concatenate([grad_part, product_part], axis=1)
+    grad_part, out_pieces, weighted_b = lax.optimization_barrier((grad_part, out_pieces, weighted[:, unit_rows:]))
+    block = own_t.shape[0]
+    far_x = over_dp(grad_part[7 * block :], 2)
+    rest_x = over_dp(grad_part[4 * block : 7 * block], 2)
+    share_b = narrow(dot_first(weighted_b, grad_rows))
+    far_x, share_b = lax.optimization_barrier((far_x, share_b))
+    other_share = over_dp(share_b, 1)
+    far = narrow(add(grad_part[3 * block : 4 * block], far_x))
+    far_sum = over_z(far, -2)
+    layer_out = narrow(cross_z(*out_pieces))
+    rest_x, other_share, layer_out = lax.optimization_barrier((rest_x, other_share, layer_out))
+    rest = add(grad_part[: 3 * block], rest_x)
+    left, right = over_z(narrow(rest[block : 2 * block]), -1), over_z(narrow(rest[2 * block :]), -3)
+    down_grad = finish_share(weighted, grad_rows, other_share, local_experts)
+    left, right, far_sum, down_grad = lax.optimization_barrier((left, right, far_sum, down_grad))
+    sums = add(rest[:block], far_sum) + add(left, right)
+    input_grad = narrow(sums[:, :width])
+    per_expert = sums[:, width : width + experts]
+    weight_grad = jnp.sum(jnp.where(picked, per_expert[:, None, :], 0.0), axis=2)
+    return (layer_out, input_grad, weight_grad, down_grad)
+
+
+def plan(tokens, out_grad, expert_ids, slot_pos, combine_weight, w_gate, w_up, w_down):
+    args = (tokens, out_grad, expert_ids, slot_pos, combine_weight, w_gate, w_up, w_down)
+    slots = tokens.shape[0] * expert_ids.shape[1] // lax.axis_size("expert")
+    unit_rows = w_gate.shape[0] * w_gate.shape[1]
+    tiled = w_gate.shape[0] % 64 == 0 and unit_rows % UNIT_TILE == 0 and UNIT_TILE % w_gate.shape[1] == 0
+    tiled = tiled and w_gate.shape[2] % WIDTH_TILE == 0 and tokens.shape[0] % 32 == 0
+    four = lax.axis_size("expert") == 4 and lax.axis_size("dp") == 4
+    if tokens.shape[0] < slots and tiled and four:
+        return local_tokens(*args)
+    return local(*args)
+
+
 def solution(mesh):
     in_specs = (
         P(("groups", "expert", "dp"), None),
@@ -110,4 +476,4 @@
         P(("groups", "expert", "dp"), None),
         P(("groups", "dp"), "expert", None),
     )
-    return jax.shard_map(local, mesh=mesh, in_specs=in_specs, out_specs=out_specs, check_vma=False)
+    return jax.shard_map(plan, mesh=mesh, in_specs=in_specs, out_specs=out_specs, check_vma=False)

time: 501 us -> 104 us (0.21)
  waiting for transfers between devices: 354 us -> 28.7 us
  local copies, waits for them, and re-layouts: 55.2 us -> 2.95 us
  matrix products: 53.2 us -> 1.01 us
  Pallas kernels: 0 us -> 38.4 us
  between operations: 14.7 us -> 0.84 us
  starting transfers between devices: 18.6 us -> 26.6 us
    all_gather x3 -> x0, waiting for transfers between devices: 157 us -> none  [the longest x1 75.1 us: local(): up_piece = lax.all_gather(w_up, 'dp', axis=0, tiled=True)]
    unnamed x5 -> x0, waiting for transfers between devices: 149 us -> none
    dot_general x9 -> x1, matrix products: 53.2 us -> 1.01 us  [dot_first(): lax.dot_general(a, b, (((0,), (0,)), ((), ())), preferred_element_type=jn...]
    all_to_all x4 -> x0, waiting for transfers between devices: 48.9 us -> none  [the longest x1 22.8 us: local(): lax.all_to_all(sent_rows, 'expert', split_axis=1, concat_axis=1, tiled=True)]
    pallas_call x0 -> x4, Pallas kernels: none -> 38.4 us  [the longest x1 14.4 us: forward(): pl.pallas_call(forward_kernel, grid=(tiles + features // WIDTH_TILE,), in...]
    ppermute x0 -> x21, waiting for transfers between devices: none -> 28.7 us  [the longest x12 25 us: over_z(): lax.ppermute(rows, 'expert', [(i, (i + shift) % peers) for i in range(pee...]
    ppermute x0 -> x21, starting transfers between devices: none -> 26.6 us  [the longest x12 18.2 us: over_z(): lax.ppermute(rows, 'expert', [(i, (i + shift) % peers) for i in range(pee...]
    convert_element_type x3 -> x0, local copies, waits for them, and re-layouts: 25.5 us -> none  [the longest x1 21.9 us: local(): down_grad = lax.psum_scatter(jnp.einsum('lnr,lrd->nld', hidden_all, exper...]
  transfers between devices with their start and end apart: 8 -> 21, of which waited for: 7 -> 9; matrix products, arithmetic and copies ran while one was open for 20% -> 2% of each run, Pallas kernels for 0% -> 37%
where the time goes in v2:
time: 104 us; the launch traced here: 103 us
  Pallas kernels  38.4 us (37%)
  waiting for transfers between devices  28.7 us (28%)
  starting transfers between devices  26.6 us (26%)
  other arithmetic  4.54 us (4%)
  local copies, waits for them, and re-layouts  2.95 us (3%)
    ppermute x12, waiting for transfers between devices, over_z(): lax.ppermute(rows, 'expert', [(i, (i + shift) % peers) for i in range(pee...  25 us
    ppermute x12, starting transfers between devices, over_z(): lax.ppermute(rows, 'expert', [(i, (i + shift) % peers) for i in range(pee...  18.2 us
    pallas_call x1, Pallas kernels, forward(): pl.pallas_call(forward_kernel, grid=(tiles + features // WIDTH_TILE,), in...  14.4 us
    pallas_call x1, Pallas kernels, backward(): pl.pallas_call(backward_kernel, grid=(tiles + features // WIDTH_TILE,), i...  13.5 us
    ppermute x9, starting transfers between devices, over_dp(): lax.ppermute(rows, 'dp', [(i, i ^ bit) for i in range(lax.axis_size('dp'))])  8.45 us
    pallas_call x1, Pallas kernels, merge_units(): pl.pallas_call(merge_kernel, grid=(units // tile,), in_specs=[block] * 3,...  7.56 us
    ppermute x9, waiting for transfers between devices, over_dp(): lax.ppermute(rows, 'dp', [(i, i ^ bit) for i in range(lax.axis_size('dp'))])  3.69 us
    pallas_call x1, Pallas kernels, finish_share(): pl.pallas_call(share_kernel, grid=(units // tile,), in_specs=[pl.BlockSpe...  2.91 us
  transfers between devices with their start and end apart: 21, of which 9 were waited for; matrix products, arithmetic and copies ran while one was open for 2% of the time, Pallas kernels for 37%

profile of v2, /device:TPU:0, one launch (start us, length us, event | category | flops | bytes accessed | tf_op | source)
XLA Modules:
  0.0 103.1 jit_solution(4871963795920685286)
XLA Ops:
  3.3 3.1 %collective-permute-start = (bf16[32,2176]{1,0:T(8,128)(2,1)S(1)}, bf16[32,2176]{1,0:T(8,128)(2,1)S(1)}, u32[]{:S(2)}, u32[]{:S(2)}) collective-permute-start(bf16[32,2176]{1,0:T(8,128)(2,1)S(1)} %pad_maximum_fusion.3.refs_0_), channel_id=1, source_target_pairs={{0,4},{4,8},{8,12},{12,0},{1,5},{5,9},{9,13},{13,1},{2,6},{6,10},{... | collective-permute-start | bytes 417800 | tf_op jit(solution)/shard_map/ppermute | solution.py:100
  6.3 2.1 %collective-permute-start.1 = (bf16[32,2176]{1,0:T(8,128)(2,1)S(1)}, bf16[32,2176]{1,0:T(8,128)(2,1)S(1)}, u32[]{:S(2)}, u32[]{:S(2)}) collective-permute-start(bf16[32,2176]{1,0:T(8,128)(2,1)S(1)} %pad_maximum_fusion.3.refs_0_), channel_id=1, source_target_pairs={{0,12},{4,0},{8,4},{12,8},{1,13},{5,1},{9,5},{13,9},{2,14},{6,2},{... | collective-permute-start | bytes 417800 | tf_op jit(solution)/shard_map/ppermute | solution.py:100
  9.4 1.5 %collective-permute-start.3 = (bf16[32,2048]{1,0:T(8,128)(2,1)}, bf16[32,2048]{1,0:T(8,128)(2,1)S(1)}, u32[]{:S(2)}, u32[]{:S(2)}) collective-permute-start(bf16[32,2048]{1,0:T(8,128)(2,1)} %refs_0_.1), channel_id=1, source_target_pairs={{0,2},{1,3},{2,0},{3,1},{4,6},{5,7},{6,4},{7,5},{8,10},{9,11},{10,... | collective-permute-start | bytes 393224 | tf_op jit(solution)/shard_map/ppermute | solution.py:104
  10.9 1.9 %copy-done = bf16[192,4,2048]{2,1,0:T(4,128)(2,1)S(1)} copy-done((bf16[192,4,2048]{2,1,0:T(4,128)(2,1)S(1)}, bf16[192,4,2048]{2,1,0:T(4,128)(2,1)}, u32[]{:S(2)}) %copy-start) | copy-done | bytes 3145752
  12.8 7.6 %merge_units.1.refs_5_.refs_7_.refs_9_.refs_6_.refs_8_.refs_10_ = bf16[3,768,2048]{2,1,0:T(8,128)(2,1)} custom-call(bf16[192,4,2048]{2,1,0:T(4,128)(2,1)S(1)} %copy-done, bf16[192,4,2048]{2,1,0:T(4,128)(2,1)} %up.1, bf16[192,4,2048]{2,1,0:T(4,128)(2,1)} %down.1), custom_call_target="tpu_custom_call" | custom-call | bytes 18874368 | tf_op jit(solution)/shard_map/merge_units/pallas_call | solution.py:249
  21.1 1.6 %collective-permute-start.7 = (bf16[128,2176]{1,0:T(8,128)(2,1)S(1)}, bf16[128,2176]{1,0:T(8,128)(2,1)S(1)}, u32[]{:S(2)}, u32[]{:S(2)}) collective-permute-start(bf16[128,2176]{1,0:T(8,128)(2,1)S(1)} %pad_maximum_fusion.1), channel_id=1, source_target_pairs={{0,2},{1,3},{2,0},{3,1},{4,6},{5,7},{6,4},{7,5},{8,10},{9,11},{10,... | collective-permute-start | bytes 1671176 | tf_op jit(solution)/shard_map/ppermute | solution.py:104
  22.9 3.8 %collective-permute-start.5 = (bf16[32,2048]{1,0:T(8,128)(2,1)S(1)}, bf16[32,2048]{1,0:T(8,128)(2,1)S(1)}, u32[]{:S(2)}, u32[]{:S(2)}) collective-permute-start(bf16[32,2048]{1,0:T(8,128)(2,1)S(1)} %copy-done.1), channel_id=1, source_target_pairs={{0,12},{4,0},{8,4},{12,8},{1,13},{5,1},{9,5},{13,9},{2,14},{6,2},{... | collective-permute-start | bytes 393224 | tf_op jit(solution)/shard_map/ppermute | solution.py:100
  26.7 4.2 %collective-permute-done.4.refs_1_ = bf16[32,2048]{1,0:T(8,128)(2,1)S(1)} collective-permute-done((bf16[32,2048]{1,0:T(8,128)(2,1)S(1)}, bf16[32,2048]{1,0:T(8,128)(2,1)S(1)}, u32[]{:S(2)}, u32[]{:S(2)}) %collective-permute-start.4) | collective-permute-done | bytes 131104 | tf_op jit(solution)/shard_map/ppermute | solution.py:100
  31.0 1.2 %collective-permute-done.5.refs_2_ = bf16[32,2048]{1,0:T(8,128)(2,1)S(1)} collective-permute-done((bf16[32,2048]{1,0:T(8,128)(2,1)S(1)}, bf16[32,2048]{1,0:T(8,128)(2,1)S(1)}, u32[]{:S(2)}, u32[]{:S(2)}) %collective-permute-start.5) | collective-permute-done | bytes 131104 | tf_op jit(solution)/shard_map/ppermute | solution.py:100
  32.1 4.9 %collective-permute-done.6.refs_3_ = bf16[32,2048]{1,0:T(8,128)(2,1)S(1)} collective-permute-done((bf16[32,2048]{1,0:T(8,128)(2,1)S(1)}, bf16[32,2048]{1,0:T(8,128)(2,1)S(1)}, u32[]{:S(2)}, u32[]{:S(2)}) %collective-permute-start.6) | collective-permute-done | bytes 131104 | tf_op jit(solution)/shard_map/ppermute | solution.py:100
  37.0 1.7 %collective-permute-start.9 = (bf16[96,2048]{1,0:T(8,128)(2,1)S(1)}, bf16[96,2048]{1,0:T(8,128)(2,1)S(1)}, u32[]{:S(2)}, u32[]{:S(2)}) collective-permute-start(bf16[96,2048]{1,0:T(8,128)(2,1)S(1)} %pad_maximum_fusion.2), channel_id=1, source_target_pairs={{0,2},{1,3},{2,0},{3,1},{4,6},{5,7},{6,4},{7,5},{8,10},{9,11},{10,... | collective-permute-start | bytes 1179656 | tf_op jit(solution)/shard_map/ppermute | solution.py:104
  38.8 14.4 %forward_products.1 = (bf16[256,2048]{1,0:T(8,128)(2,1)S(1)}, f32[256,1536]{1,0:T(8,128)S(1)}, f32[256,1536]{1,0:T(8,128)}, f32[256,256]{1,0:T(8,128)S(1)}, bf16[256,1536]{1,0:T(8,128)(2,1)S(1)}) custom-call(bf16[128,256]{1,0:T(8,128)(2,1)S(1)} %and_convert_fusion.spread, bf16[256,128]{1,0:T(8,128)(2,1)S(1)} %fusion.1.collect, ...), custom_call_target="tpu_custom_call" | custom-call | flops 4831838208 | bytes 20971520 | tf_op jit(solution)/shard_map/forward_products/pallas_call | solution.py:301
  53.7 1.6 %collective-permute-start.10 = (bf16[96,2048]{1,0:T(8,128)(2,1)S(1)}, bf16[96,2048]{1,0:T(8,128)(2,1)S(1)}, u32[]{:S(2)}, u32[]{:S(2)}) collective-permute-start(bf16[96,2048]{1,0:T(8,128)(2,1)S(1)} %slice.57), channel_id=1, source_target_pairs={{0,2},{1,3},{2,0},{3,1},{4,6},{5,7},{6,4},{7,5},{8,10},{9,11},{10,... | collective-permute-start | bytes 1179656 | tf_op jit(solution)/shard_map/ppermute | solution.py:104
  55.3 13.5 %backward_products.1 = (bf16[256,2048]{1,0:T(8,128)(2,1)S(1)}, bf16[256,128]{1,0:T(8,128)(2,1)S(1)}, bf16[256,2048]{1,0:T(8,128)(2,1)S(1)}) custom-call(bf16[128,256]{1,0:T(8,128)(2,1)S(1)} %and_convert_fusion.spread, bf16[256,128]{1,0:T(8,128)(2,1)S(1)} %fusion.1.collect, bf16[32,2048]{1,0:T(8,128)(2,1)S(1)} %copy-done.1, ...), custom_call_target="tpu_custom_call" | custom-call | flops 4831838208 | bytes 20971520 | tf_op jit(solution)/shard_map/backward_products/pallas_call | solution.py:336
  70.7 3.7 %collective-permute-done.13 = bf16[32,2176]{1,0:T(8,128)(2,1)S(1)} collective-permute-done((bf16[32,2176]{1,0:T(8,128)(2,1)S(1)}, bf16[32,2176]{1,0:T(8,128)(2,1)S(1)}, u32[]{:S(2)}, u32[]{:S(2)}) %collective-permute-start.13) | collective-permute-done | bytes 139296 | tf_op jit(solution)/shard_map/ppermute | solution.py:104
  74.4 1.4 %collective-permute-start.16 = (bf16[32,2048]{1,0:T(8,128)(2,1)S(1)}, bf16[32,2048]{1,0:T(8,128)(2,1)S(1)}, u32[]{:S(2)}, u32[]{:S(2)}) collective-permute-start(bf16[32,2048]{1,0:T(8,128)(2,1)S(1)} %get-tuple-element.70), channel_id=1, source_target_pairs={{0,12},{4,0},{8,4},{12,8},{1,13},{5,1},{9,5},{13,9},{2,14},{6,2},{... | collective-permute-start | bytes 393224 | tf_op jit(solution)/shard_map/ppermute | solution.py:100
  76.4 1.1 %collective-permute-start.12 = (bf16[96,2176]{1,0:T(8,128)(2,1)S(1)}, bf16[96,2176]{1,0:T(8,128)(2,1)S(1)}, u32[]{:S(2)}, u32[]{:S(2)}) collective-permute-start(bf16[96,2176]{1,0:T(8,128)(2,1)S(1)} %slice.64), channel_id=1, source_target_pairs={{0,2},{1,3},{2,0},{3,1},{4,6},{5,7},{6,4},{7,5},{8,10},{9,11},{10,... | collective-permute-start | bytes 1253384 | tf_op jit(solution)/shard_map/ppermute | solution.py:104
  77.6 5.6 %collective-permute-done.15 = bf16[32,2048]{1,0:T(8,128)(2,1)S(1)} collective-permute-done((bf16[32,2048]{1,0:T(8,128)(2,1)S(1)}, bf16[32,2048]{1,0:T(8,128)(2,1)S(1)}, u32[]{:S(2)}, u32[]{:S(2)}) %collective-permute-start.15) | collective-permute-done | bytes 131104 | tf_op jit(solution)/shard_map/ppermute | solution.py:100
  83.2 2.7 %collective-permute-done.16 = bf16[32,2048]{1,0:T(8,128)(2,1)S(1)} collective-permute-done((bf16[32,2048]{1,0:T(8,128)(2,1)S(1)}, bf16[32,2048]{1,0:T(8,128)(2,1)S(1)}, u32[]{:S(2)}, u32[]{:S(2)}) %collective-permute-start.16) | collective-permute-done | bytes 131104 | tf_op jit(solution)/shard_map/ppermute | solution.py:100
  86.7 4.1 %collective-permute-start.20 = (bf16[32,2176]{1,0:T(8,128)(2,1)S(1)}, bf16[32,2176]{1,0:T(8,128)(2,1)S(1)}, u32[]{:S(2)}, u32[]{:S(2)}) collective-permute-start(bf16[32,2176]{1,0:T(8,128)(2,1)S(1)} %add_convert_fusion), channel_id=1, source_target_pairs={{0,8},{4,12},{8,0},{12,4},{1,9},{5,13},{9,1},{13,5},{2,10},{6,14},... | collective-permute-start | bytes 417800 | tf_op jit(solution)/shard_map/ppermute | solution.py:100
  90.9 1.2 %collective-permute-start.18 = (bf16[32,2176]{1,0:T(8,128)(2,1)S(1)}, bf16[32,2176]{1,0:T(8,128)(2,1)S(1)}, u32[]{:S(2)}, u32[]{:S(2)}) collective-permute-start(bf16[32,2176]{1,0:T(8,128)(2,1)S(1)} %get-tuple-element.85), channel_id=1, source_target_pairs={{0,12},{4,0},{8,4},{12,8},{1,13},{5,1},{9,5},{13,9},{2,14},{6,2},{... | collective-permute-start | bytes 417800 | tf_op jit(solution)/shard_map/ppermute | solution.py:100
  93.0 2.9 %finish_share.1 = bf16[192,4,2048]{2,1,0:T(4,128)(2,1)} custom-call(bf16[256,1536]{1,0:T(8,128)(2,1)S(1)} %get-tuple-element.63.weighted, bf16[256,2048]{1,0:T(8,128)(2,1)S(1)} %get-tuple-element.66.rows, bf16[768,2048]{1,0:T(8,128)(2,1)S(1)} %collective-permute-done.14.other), custom_call_target="tpu_custom_call" | custom-call | flops 805306368 | bytes 6291456 | tf_op jit(solution)/shard_map/finish_share/pallas_call | solution.py:370
  95.9 2.8 %collective-permute-done.20 = bf16[32,2176]{1,0:T(8,128)(2,1)S(1)} collective-permute-done((bf16[32,2176]{1,0:T(8,128)(2,1)S(1)}, bf16[32,2176]{1,0:T(8,128)(2,1)S(1)}, u32[]{:S(2)}, u32[]{:S(2)}) %collective-permute-start.20) | collective-permute-done | bytes 139296 | tf_op jit(solution)/shard_map/ppermute | solution.py:100
  98.7 3.0 %collective-permute-done.19 = bf16[32,2176]{1,0:T(8,128)(2,1)S(1)} collective-permute-done((bf16[32,2176]{1,0:T(8,128)(2,1)S(1)}, bf16[32,2176]{1,0:T(8,128)(2,1)S(1)}, u32[]{:S(2)}, u32[]{:S(2)}) %collective-permute-start.19) | collective-permute-done | bytes 139296 | tf_op jit(solution)/shard_map/ppermute | solution.py:100
  (63 shorter events, 10.7 us)
Async XLA Ops:
  2.3 20.4 %copy-start.1 = (bf16[32,2048]{1,0:T(8,128)(2,1)S(1)}, bf16[32,2048]{1,0:T(8,128)(2,1)}, u32[]{:S(2)}) copy-start(bf16[32,2048]{1,0:T(8,128)(2,1)} %refs_0_.1) | copy-start | bytes 393220
  3.3 17.1 %collective-permute-start = (bf16[32,2176]{1,0:T(8,128)(2,1)S(1)}, bf16[32,2176]{1,0:T(8,128)(2,1)S(1)}, u32[]{:S(2)}, u32[]{:S(2)}) collective-permute-start(bf16[32,2176]{1,0:T(8,128)(2,1)S(1)} %pad_maximum_fusion.3.refs_0_), channel_id=1, source_target_pairs={{0,4},{4,8},{8,12},{12,0},{1,5},{5,9},{9,13},{13,1},{2,6},{6,10},{... | collective-permute-start | bytes 417800 | tf_op jit(solution)/shard_map/ppermute | solution.py:100
  6.3 14.0 %collective-permute-start.1 = (bf16[32,2176]{1,0:T(8,128)(2,1)S(1)}, bf16[32,2176]{1,0:T(8,128)(2,1)S(1)}, u32[]{:S(2)}, u32[]{:S(2)}) collective-permute-start(bf16[32,2176]{1,0:T(8,128)(2,1)S(1)} %pad_maximum_fusion.3.refs_0_), channel_id=1, source_target_pairs={{0,12},{4,0},{8,4},{12,8},{1,13},{5,1},{9,5},{13,9},{2,14},{6,2},{... | collective-permute-start | bytes 417800 | tf_op jit(solution)/shard_map/ppermute | solution.py:100
  8.4 12.6 %collective-permute-start.2 = (bf16[32,2176]{1,0:T(8,128)(2,1)S(1)}, bf16[32,2176]{1,0:T(8,128)(2,1)S(1)}, u32[]{:S(2)}, u32[]{:S(2)}) collective-permute-start(bf16[32,2176]{1,0:T(8,128)(2,1)S(1)} %pad_maximum_fusion.3.refs_0_), channel_id=1, source_target_pairs={{0,8},{4,12},{8,0},{12,4},{1,9},{5,13},{9,1},{13,5},{2,10},{6,14},... | collective-permute-start | bytes 417800 | tf_op jit(solution)/shard_map/ppermute | solution.py:100
  9.4 10.9 %collective-permute-start.3 = (bf16[32,2048]{1,0:T(8,128)(2,1)}, bf16[32,2048]{1,0:T(8,128)(2,1)S(1)}, u32[]{:S(2)}, u32[]{:S(2)}) collective-permute-start(bf16[32,2048]{1,0:T(8,128)(2,1)} %refs_0_.1), channel_id=1, source_target_pairs={{0,2},{1,3},{2,0},{3,1},{4,6},{5,7},{6,4},{7,5},{8,10},{9,11},{10,... | collective-permute-start | bytes 393224 | tf_op jit(solution)/shard_map/ppermute | solution.py:104
  10.9 1.9 %copy-start = (bf16[192,4,2048]{2,1,0:T(4,128)(2,1)S(1)}, bf16[192,4,2048]{2,1,0:T(4,128)(2,1)}, u32[]{:S(2)}) copy-start(bf16[192,4,2048]{2,1,0:T(4,128)(2,1)} %gate) | copy-start | bytes 9437188
  21.0 17.8 %collective-permute-start.8 = (bf16[3,768,2048]{2,1,0:T(8,128)(2,1)}, bf16[3,768,2048]{2,1,0:T(8,128)(2,1)}, u32[]{:S(2)}, u32[]{:S(2)}) collective-permute-start(bf16[3,768,2048]{2,1,0:T(8,128)(2,1)} %merge_units.1.refs_5_.refs_7_.refs_9_.refs_6_.refs_8_.refs_10_), channel_id=1, source_target_pairs={{0,1},{1,0},{2,3},{3,2},{4,5},{5,4},{6,7},{7,6},{8,9},{9,8},{10,11... | collective-permute-start | bytes 28311560 | tf_op jit(solution)/shard_map/ppermute | solution.py:104
  21.1 15.9 %collective-permute-start.7 = (bf16[128,2176]{1,0:T(8,128)(2,1)S(1)}, bf16[128,2176]{1,0:T(8,128)(2,1)S(1)}, u32[]{:S(2)}, u32[]{:S(2)}) collective-permute-start(bf16[128,2176]{1,0:T(8,128)(2,1)S(1)} %pad_maximum_fusion.1), channel_id=1, source_target_pairs={{0,2},{1,3},{2,0},{3,1},{4,6},{5,7},{6,4},{7,5},{8,10},{9,11},{10,... | collective-permute-start | bytes 1671176 | tf_op jit(solution)/shard_map/ppermute | solution.py:104
  22.7 8.2 %collective-permute-start.4 = (bf16[32,2048]{1,0:T(8,128)(2,1)S(1)}, bf16[32,2048]{1,0:T(8,128)(2,1)S(1)}, u32[]{:S(2)}, u32[]{:S(2)}) collective-permute-start(bf16[32,2048]{1,0:T(8,128)(2,1)S(1)} %copy-done.1), channel_id=1, source_target_pairs={{0,4},{4,8},{8,12},{12,0},{1,5},{5,9},{9,13},{13,1},{2,6},{6,10},{... | collective-permute-start | bytes 393224 | tf_op jit(solution)/shard_map/ppermute | solution.py:100
  22.9 9.3 %collective-permute-start.5 = (bf16[32,2048]{1,0:T(8,128)(2,1)S(1)}, bf16[32,2048]{1,0:T(8,128)(2,1)S(1)}, u32[]{:S(2)}, u32[]{:S(2)}) collective-permute-start(bf16[32,2048]{1,0:T(8,128)(2,1)S(1)} %copy-done.1), channel_id=1, source_target_pairs={{0,12},{4,0},{8,4},{12,8},{1,13},{5,1},{9,5},{13,9},{2,14},{6,2},{... | collective-permute-start | bytes 393224 | tf_op jit(solution)/shard_map/ppermute | solution.py:100
  26.6 10.4 %collective-permute-start.6 = (bf16[32,2048]{1,0:T(8,128)(2,1)S(1)}, bf16[32,2048]{1,0:T(8,128)(2,1)S(1)}, u32[]{:S(2)}, u32[]{:S(2)}) collective-permute-start(bf16[32,2048]{1,0:T(8,128)(2,1)S(1)} %copy-done.1), channel_id=1, source_target_pairs={{0,8},{4,12},{8,0},{12,4},{1,9},{5,13},{9,1},{13,5},{2,10},{6,14},... | collective-permute-start | bytes 393224 | tf_op jit(solution)/shard_map/ppermute | solution.py:100
  37.0 16.1 %collective-permute-start.9 = (bf16[96,2048]{1,0:T(8,128)(2,1)S(1)}, bf16[96,2048]{1,0:T(8,128)(2,1)S(1)}, u32[]{:S(2)}, u32[]{:S(2)}) collective-permute-start(bf16[96,2048]{1,0:T(8,128)(2,1)S(1)} %pad_maximum_fusion.2), channel_id=1, source_target_pairs={{0,2},{1,3},{2,0},{3,1},{4,6},{5,7},{6,4},{7,5},{8,10},{9,11},{10,... | collective-permute-start | bytes 1179656 | tf_op jit(solution)/shard_map/ppermute | solution.py:104
  53.2 15.8 %collective-permute-start.11 = (bf16[32,2048]{1,0:T(8,128)(2,1)S(1)}, bf16[32,2048]{1,0:T(8,128)(2,1)S(1)}, u32[]{:S(2)}, u32[]{:S(2)}) collective-permute-start(bf16[32,2048]{1,0:T(8,128)(2,1)S(1)} %slice.62), channel_id=1, source_target_pairs={{0,2},{1,3},{2,0},{3,1},{4,6},{5,7},{6,4},{7,5},{8,10},{9,11},{10,... | collective-permute-start | bytes 393224 | tf_op jit(solution)/shard_map/ppermute | solution.py:104
  53.7 15.4 %collective-permute-start.10 = (bf16[96,2048]{1,0:T(8,128)(2,1)S(1)}, bf16[96,2048]{1,0:T(8,128)(2,1)S(1)}, u32[]{:S(2)}, u32[]{:S(2)}) collective-permute-start(bf16[96,2048]{1,0:T(8,128)(2,1)S(1)} %slice.57), channel_id=1, source_target_pairs={{0,2},{1,3},{2,0},{3,1},{4,6},{5,7},{6,4},{7,5},{8,10},{9,11},{10,... | collective-permute-start | bytes 1179656 | tf_op jit(solution)/shard_map/ppermute | solution.py:104
  69.2 5.1 %collective-permute-start.13 = (bf16[32,2176]{1,0:T(8,128)(2,1)S(1)}, bf16[32,2176]{1,0:T(8,128)(2,1)S(1)}, u32[]{:S(2)}, u32[]{:S(2)}) collective-permute-start(bf16[32,2176]{1,0:T(8,128)(2,1)S(1)} %slice.65), channel_id=1, source_target_pairs={{0,2},{1,3},{2,0},{3,1},{4,6},{5,7},{6,4},{7,5},{8,10},{9,11},{10,... | collective-permute-start | bytes 417800 | tf_op jit(solution)/shard_map/ppermute | solution.py:104
  74.4 16.4 %collective-permute-start.14 = (bf16[768,2048]{1,0:T(8,128)(2,1)S(1)}, bf16[768,2048]{1,0:T(8,128)(2,1)S(1)}, u32[]{:S(2)}, u32[]{:S(2)}) collective-permute-start(bf16[768,2048]{1,0:T(8,128)(2,1)S(1)} %convolution_convert_fusion), channel_id=1, source_target_pairs={{0,1},{1,0},{2,3},{3,2},{4,5},{5,4},{6,7},{7,6},{8,9},{9,8},{10,11... | collective-permute-start | bytes 9437192 | tf_op jit(solution)/shard_map/ppermute | solution.py:104
  74.4 8.8 %collective-permute-start.15 = (bf16[32,2048]{1,0:T(8,128)(2,1)S(1)}, bf16[32,2048]{1,0:T(8,128)(2,1)S(1)}, u32[]{:S(2)}, u32[]{:S(2)}) collective-permute-start(bf16[32,2048]{1,0:T(8,128)(2,1)S(1)} %add_convert_fusion.2), channel_id=1, source_target_pairs={{0,8},{4,12},{8,0},{12,4},{1,9},{5,13},{9,1},{13,5},{2,10},{6,14},... | collective-permute-start | bytes 393224 | tf_op jit(solution)/shard_map/ppermute | solution.py:100
  74.4 11.5 %collective-permute-start.16 = (bf16[32,2048]{1,0:T(8,128)(2,1)S(1)}, bf16[32,2048]{1,0:T(8,128)(2,1)S(1)}, u32[]{:S(2)}, u32[]{:S(2)}) collective-permute-start(bf16[32,2048]{1,0:T(8,128)(2,1)S(1)} %get-tuple-element.70), channel_id=1, source_target_pairs={{0,12},{4,0},{8,4},{12,8},{1,13},{5,1},{9,5},{13,9},{2,14},{6,2},{... | collective-permute-start | bytes 393224 | tf_op jit(solution)/shard_map/ppermute | solution.py:100
  75.8 10.1 %collective-permute-start.17 = (bf16[32,2048]{1,0:T(8,128)(2,1)S(1)}, bf16[32,2048]{1,0:T(8,128)(2,1)S(1)}, u32[]{:S(2)}, u32[]{:S(2)}) collective-permute-start(bf16[32,2048]{1,0:T(8,128)(2,1)S(1)} %get-tuple-element.71), channel_id=1, source_target_pairs={{0,4},{4,8},{8,12},{12,0},{1,5},{5,9},{9,13},{13,1},{2,6},{6,10},{... | collective-permute-start | bytes 393224 | tf_op jit(solution)/shard_map/ppermute | solution.py:100
  76.4 14.3 %collective-permute-start.12 = (bf16[96,2176]{1,0:T(8,128)(2,1)S(1)}, bf16[96,2176]{1,0:T(8,128)(2,1)S(1)}, u32[]{:S(2)}, u32[]{:S(2)}) collective-permute-start(bf16[96,2176]{1,0:T(8,128)(2,1)S(1)} %slice.64), channel_id=1, source_target_pairs={{0,2},{1,3},{2,0},{3,1},{4,6},{5,7},{6,4},{7,5},{8,10},{9,11},{10,... | collective-permute-start | bytes 1253384 | tf_op jit(solution)/shard_map/ppermute | solution.py:104
  86.7 12.0 %collective-permute-start.20 = (bf16[32,2176]{1,0:T(8,128)(2,1)S(1)}, bf16[32,2176]{1,0:T(8,128)(2,1)S(1)}, u32[]{:S(2)}, u32[]{:S(2)}) collective-permute-start(bf16[32,2176]{1,0:T(8,128)(2,1)S(1)} %add_convert_fusion), channel_id=1, source_target_pairs={{0,8},{4,12},{8,0},{12,4},{1,9},{5,13},{9,1},{13,5},{2,10},{6,14},... | collective-permute-start | bytes 417800 | tf_op jit(solution)/shard_map/ppermute | solution.py:100
  90.9 7.8 %collective-permute-start.18 = (bf16[32,2176]{1,0:T(8,128)(2,1)S(1)}, bf16[32,2176]{1,0:T(8,128)(2,1)S(1)}, u32[]{:S(2)}, u32[]{:S(2)}) collective-permute-start(bf16[32,2176]{1,0:T(8,128)(2,1)S(1)} %get-tuple-element.85), channel_id=1, source_target_pairs={{0,12},{4,0},{8,4},{12,8},{1,13},{5,1},{9,5},{13,9},{2,14},{6,2},{... | collective-permute-start | bytes 417800 | tf_op jit(solution)/shard_map/ppermute | solution.py:100
  92.1 10.4 %copy-start.2 = (s32[32,8]{0,1:T(8,128)S(1)}, s32[32,8]{0,1:T(8,128)}, u32[]{:S(2)}) copy-start(s32[32,8]{0,1:T(8,128)} %param.10) | copy-start | bytes 3076
  92.1 9.5 %collective-permute-start.19 = (bf16[32,2176]{1,0:T(8,128)(2,1)S(1)}, bf16[32,2176]{1,0:T(8,128)(2,1)S(1)}, u32[]{:S(2)}, u32[]{:S(2)}) collective-permute-start(bf16[32,2176]{1,0:T(8,128)(2,1)S(1)} %get-tuple-element.84), channel_id=1, source_target_pairs={{0,4},{4,8},{8,12},{12,0},{1,5},{5,9},{9,13},{13,1},{2,6},{6,10},{... | collective-permute-start | bytes 417800 | tf_op jit(solution)/shard_map/ppermute | solution.py:100

commit v3 on v2

--- a/solution.py
+++ b/solution.py
@@ -95,40 +95,20 @@
     return (layer_out, input_grad, weight_grad, down_grad)
 
 
-def over_z(rows, shift):
-    peers = lax.axis_size("expert")
-    return lax.ppermute(rows, "expert", [(i, (i + shift) % peers) for i in range(peers)])
+def over_z(rows, bit):
+    return lax.ppermute(rows, "expert", [(i, i ^ bit) for i in range(lax.axis_size("expert"))])
 
 
 def over_dp(rows, bit):
     return lax.ppermute(rows, "dp", [(i, i ^ bit) for i in range(lax.axis_size("dp"))])
 
 
-def after(value, *others):
-    return lax.optimization_barrier((value,) + others)[0]
-
-
 def add(kept, other):
     return kept.astype(jnp.float32) + other.astype(jnp.float32)
 
 
 def narrow(rows):
     return rows.astype(jnp.bfloat16)
-
-
-def cross_x(part):
-    block = part.shape[0] // 8
-    far_x = over_dp(part[7 * block :], 2)
-    rest_x = over_dp(part[4 * block : 7 * block], 2)
-    far = narrow(add(part[3 * block : 4 * block], far_x))
-    rest = add(part[: 3 * block], rest_x)
-    return rest[:block], narrow(rest[block : 2 * block]), narrow(rest[2 * block :]), far
-
-
-def cross_z(own, near_left, near_right, far):
-    far_sum = over_z(far, -2)
-    left, right = over_z(near_left, -1), over_z(near_right, -3)
-    return add(own, far_sum) + add(left, right)
 
 
 def dot_last(a, b):
@@ -287,7 +267,7 @@
     )
 
 
-PARAMS = dict(dimension_semantics=("arbitrary",), vmem_limit_bytes=48 * 1024 * 1024)
+PARAMS = dict(dimension_semantics=("arbitrary",), vmem_limit_bytes=24 * 1024 * 1024)
 
 
 def forward(tables, pieces, weights):
@@ -404,43 +384,50 @@
 
     own_t = jnp.concatenate([tokens, routed], axis=1)
     own_t, own_g, w_gate = lax.optimization_barrier((own_t, out_grad, w_gate))
-    column_t = [over_z(own_t, 1), over_z(own_t, 3), over_z(own_t, 2)]
+    column_t = [over_z(own_t, bit) for bit in (2, 1, 3)]
     own_gx = over_dp(own_g, 2)
     weights = merge_units(w_gate, w_up, w_down)
     column_t, own_gx, own_g, weights = lax.optimization_barrier((column_t, own_gx, own_g, weights))
 
     pieces_t = [own_t, *column_t]
     column_tx = over_dp(jnp.concatenate(pieces_t, axis=0), 2)
-    near_g = [over_z(own_g, 1), over_z(own_g, 3)]
-    far_g = over_z(own_g, 2)
+    column_g = [over_z(own_g, bit) for bit in (2, 1, 3)]
     weights_b = over_dp(weights, 1)
-    near_g, far_g, column_tx = lax.optimization_barrier((near_g, far_g, column_tx))
-
-    away_gx = over_dp(jnp.concatenate([*near_g, far_g], axis=0), 2)
+    column_g, column_tx = lax.optimization_barrier((column_g, column_tx))
+
+    away_gx = over_dp(jnp.concatenate(column_g, axis=0), 2)
     weights = [weights, weights_b]
     out_part, gate_pre, up_pre, mask, weighted = forward(tables, [*pieces_t, column_tx], weights)
     out_part, away_gx = lax.optimization_barrier((out_part, away_gx))
-    out_pieces = cross_x(out_part)
-
-    grad_pieces = [out_grad, *near_g, far_g, own_gx, away_gx]
+
+    half = out_part.shape[0] // 2
+    pair, block = half // 2, half // 4
+    out_x = over_dp(out_part[half:], 2)
+    grad_pieces = [out_grad, *column_g, own_gx, away_gx]
     grad_part, product_part, grad_rows = backward(tables, grad_pieces, weights, gate_pre, up_pre, mask)
+    weighted_b = weighted[:, unit_rows:]
+    grad_part, product_part, out_x, weighted_b = lax.optimization_barrier((grad_part, product_part, out_x, weighted_b))
+
     grad_part = jnp.concatenate([grad_part, product_part], axis=1)
-    grad_part, out_pieces, weighted_b = lax.optimization_barrier((grad_part, out_pieces, weighted[:, unit_rows:]))
-    block = own_t.shape[0]
-    far_x = over_dp(grad_part[7 * block :], 2)
-    rest_x = over_dp(grad_part[4 * block : 7 * block], 2)
+    near_x = over_dp(grad_part[half + pair :], 2)
+    out_sum = add(out_part[:half], out_x)
+    out_near = over_z(narrow(out_sum[pair:]), 1)
     share_b = narrow(dot_first(weighted_b, grad_rows))
-    far_x, share_b = lax.optimization_barrier((far_x, share_b))
+    near_x, out_near, share_b = lax.optimization_barrier((near_x, out_near, share_b))
+
+    grad_near = over_z(narrow(add(grad_part[pair:half], near_x)), 1)
+    pair_x = over_dp(grad_part[half : half + pair], 2)
+    out_sum = add(out_sum[:pair], out_near)
+    out_far = over_z(narrow(out_sum[block:]), 2)
     other_share = over_dp(share_b, 1)
-    far = narrow(add(grad_part[3 * block : 4 * block], far_x))
-    far_sum = over_z(far, -2)
-    layer_out = narrow(cross_z(*out_pieces))
-    rest_x, other_share, layer_out = lax.optimization_barrier((rest_x, other_share, layer_out))
-    rest = add(grad_part[: 3 * block], rest_x)
-    left, right = over_z(narrow(rest[block : 2 * block]), -1), over_z(narrow(rest[2 * block :]), -3)
+    grad_near, pair_x, out_far, other_share = lax.optimization_barrier((grad_near, pair_x, out_far, other_share))
+
+    sums = add(add(grad_part[:pair], pair_x), grad_near)
+    grad_far = over_z(narrow(sums[block:]), 2)
+    layer_out = narrow(add(out_sum[:block], out_far))
     down_grad = finish_share(weighted, grad_rows, other_share, local_experts)
-    left, right, far_sum, down_grad = lax.optimization_barrier((left, right, far_sum, down_grad))
-    sums = add(rest[:block], far_sum) + add(left, right)
+    grad_far, down_grad, layer_out = lax.optimization_barrier((grad_far, down_grad, layer_out))
+    sums = add(sums[:block], grad_far)
     input_grad = narrow(sums[:, :width])
     per_expert = sums[:, width : width + experts]
     weight_grad = jnp.sum(jnp.where(picked, per_expert[:, None, :], 0.0), axis=2)

time: 104 us -> 98.1 us (0.943)
  local copies, waits for them, and re-layouts: 2.95 us -> 6.83 us
  Pallas kernels: 38.4 us -> 34.6 us
  starting transfers between devices: 26.6 us -> 23.3 us
  waiting for transfers between devices: 28.7 us -> 26.6 us
    ppermute x12 -> x10, waiting for transfers between devices: 25 us -> 20.5 us  [over_z(): lax.ppermute(rows, 'expert', [(i, i ^ bit) for i in range(lax.axis_size('...]
    unnamed x6 -> x11, local copies, waits for them, and re-layouts: 1.9 us -> 5.75 us
    pallas_call x1, Pallas kernels: 7.56 us -> 4.58 us  [merge_units(): pl.pallas_call(merge_kernel, grid=(units // tile,), in_specs=[block] * 3,...]
    ppermute x9 -> x8, starting transfers between devices: 8.45 us -> 5.95 us  [over_dp(): lax.ppermute(rows, 'dp', [(i, i ^ bit) for i in range(lax.axis_size('dp'))])]
    ppermute x9 -> x8, waiting for transfers between devices: 3.69 us -> 6.11 us  [over_dp(): lax.ppermute(rows, 'dp', [(i, i ^ bit) for i in range(lax.axis_size('dp'))])]
    ppermute x12 -> x10, starting transfers between devices: 18.2 us -> 17.3 us  [over_z(): lax.ppermute(rows, 'expert', [(i, i ^ bit) for i in range(lax.axis_size('...]
  transfers between devices with their start and end apart: 21 -> 18, of which waited for: 9 -> 9; matrix products, arithmetic and copies ran while one was open for 2% -> 2% of each run, Pallas kernels for 37% -> 35%
where the time goes in v3:
time: 98.1 us; the launch traced here: 97.6 us
  Pallas kernels  34.6 us (35%)
  waiting for transfers between devices  26.6 us (27%)
  starting transfers between devices  23.3 us (24%)
  local copies, waits for them, and re-layouts  6.83 us (7%)
  other arithmetic  4.38 us (4%)
  matrix products  1 us (1%)
    ppermute x10, waiting for transfers between devices, over_z(): lax.ppermute(rows, 'expert', [(i, i ^ bit) for i in range(lax.axis_size('...  20.5 us
    ppermute x10, starting transfers between devices, over_z(): lax.ppermute(rows, 'expert', [(i, i ^ bit) for i in range(lax.axis_size('...  17.3 us
    pallas_call x1, Pallas kernels, forward(): pl.pallas_call(forward_kernel, grid=(tiles + features // WIDTH_TILE,), in...  13.7 us
    pallas_call x1, Pallas kernels, backward(): pl.pallas_call(backward_kernel, grid=(tiles + features // WIDTH_TILE,), i...  13.5 us
    ppermute x8, waiting for transfers between devices, over_dp(): lax.ppermute(rows, 'dp', [(i, i ^ bit) for i in range(lax.axis_size('dp'))])  6.11 us
    ppermute x8, starting transfers between devices, over_dp(): lax.ppermute(rows, 'dp', [(i, i ^ bit) for i in range(lax.axis_size('dp'))])  5.95 us
    unnamed x11, local copies, waits for them, and re-layouts  5.75 us
    pallas_call x1, Pallas kernels, merge_units(): pl.pallas_call(merge_kernel, grid=(units // tile,), in_specs=[block] * 3,...  4.58 us
  transfers between devices with their start and end apart: 18, of which 9 were waited for; matrix products, arithmetic and copies ran while one was open for 2% of the time, Pallas kernels for 35%

profile of v3, /device:TPU:0, one launch (start us, length us, event | category | flops | bytes accessed | tf_op | source)
XLA Modules:
  0.0 97.6 jit_solution(15424251248618685670)
XLA Ops:
  2.3 0.9 pad_maximum_fusion.2.refs_0_
  3.2 5.1 %collective-permute-start.2 = (bf16[32,2176]{1,0:T(8,128)(2,1)S(1)}, bf16[32,2176]{1,0:T(8,128)(2,1)S(1)}, u32[]{:S(2)}, u32[]{:S(2)}) collective-permute-start(bf16[32,2176]{1,0:T(8,128)(2,1)S(1)} %pad_maximum_fusion.2.refs_0_), channel_id=1, source_target_pairs={{0,12},{4,8},{8,4},{12,0},{1,13},{5,9},{9,5},{13,1},{2,14},{6,10},... | collective-permute-start | bytes 417800 | tf_op jit(solution)/shard_map/ppermute | solution.py:99
  9.0 1.6 %collective-permute-start.3 = (bf16[32,2048]{1,0:T(8,128)(2,1)}, bf16[32,2048]{1,0:T(8,128)(2,1)S(1)}, u32[]{:S(2)}, u32[]{:S(2)}) collective-permute-start(bf16[32,2048]{1,0:T(8,128)(2,1)} %refs_0_.1), channel_id=1, source_target_pairs={{0,2},{1,3},{2,0},{3,1},{4,6},{5,7},{6,4},{7,5},{8,10},{9,11},{10,... | collective-permute-start | bytes 393224 | tf_op jit(solution)/shard_map/ppermute | solution.py:103
  10.6 1.9 %copy-done = bf16[192,4,2048]{2,1,0:T(4,128)(2,1)S(1)} copy-done((bf16[192,4,2048]{2,1,0:T(4,128)(2,1)S(1)}, bf16[192,4,2048]{2,1,0:T(4,128)(2,1)}, u32[]{:S(2)}) %copy-start) | copy-done | bytes 3145752
  12.5 1.9 %copy-done.1 = bf16[192,4,2048]{2,1,0:T(4,128)(2,1)S(1)} copy-done((bf16[192,4,2048]{2,1,0:T(4,128)(2,1)S(1)}, bf16[192,4,2048]{2,1,0:T(4,128)(2,1)}, u32[]{:S(2)}) %copy-start.1) | copy-done | bytes 3145752
  14.4 1.9 %copy-done.2 = bf16[192,4,2048]{2,1,0:T(4,128)(2,1)S(1)} copy-done((bf16[192,4,2048]{2,1,0:T(4,128)(2,1)S(1)}, bf16[192,4,2048]{2,1,0:T(4,128)(2,1)}, u32[]{:S(2)}) %copy-start.2) | copy-done | bytes 3145752
  16.3 4.6 %merge_units.1.refs_5_.refs_7_.refs_9_.refs_6_.refs_8_.refs_10_ = bf16[3,768,2048]{2,1,0:T(8,128)(2,1)} custom-call(bf16[192,4,2048]{2,1,0:T(4,128)(2,1)S(1)} %copy-done, bf16[192,4,2048]{2,1,0:T(4,128)(2,1)S(1)} %copy-done.1, bf16[192,4,2048]{2,1,0:T(4,128)(2,1)S(1)} %copy-done.2), custom_call_target="tpu_custom_call" | custom-call | bytes 18874368 | tf_op jit(solution)/shard_map/merge_units/pallas_call | solution.py:229
  21.9 3.6 %collective-permute-start.6 = (bf16[32,2048]{1,0:T(8,128)(2,1)S(1)}, bf16[32,2048]{1,0:T(8,128)(2,1)S(1)}, u32[]{:S(2)}, u32[]{:S(2)}) collective-permute-start(bf16[32,2048]{1,0:T(8,128)(2,1)S(1)} %copy-done.3), channel_id=1, source_target_pairs={{0,12},{4,8},{8,4},{12,0},{1,13},{5,9},{9,5},{13,1},{2,14},{6,10},... | collective-permute-start | bytes 393224 | tf_op jit(solution)/shard_map/ppermute | solution.py:99
  26.4 3.7 %collective-permute-done.6.refs_3_ = bf16[32,2048]{1,0:T(8,128)(2,1)S(1)} collective-permute-done((bf16[32,2048]{1,0:T(8,128)(2,1)S(1)}, bf16[32,2048]{1,0:T(8,128)(2,1)S(1)}, u32[]{:S(2)}, u32[]{:S(2)}) %collective-permute-start.6) | collective-permute-done | bytes 131104 | tf_op jit(solution)/shard_map/ppermute | solution.py:99
  30.1 3.5 %collective-permute-done.5.refs_2_ = bf16[32,2048]{1,0:T(8,128)(2,1)S(1)} collective-permute-done((bf16[32,2048]{1,0:T(8,128)(2,1)S(1)}, bf16[32,2048]{1,0:T(8,128)(2,1)S(1)}, u32[]{:S(2)}, u32[]{:S(2)}) %collective-permute-start.5) | collective-permute-done | bytes 131104 | tf_op jit(solution)/shard_map/ppermute | solution.py:99
  33.6 2.9 %collective-permute-done.4.refs_1_ = bf16[32,2048]{1,0:T(8,128)(2,1)S(1)} collective-permute-done((bf16[32,2048]{1,0:T(8,128)(2,1)S(1)}, bf16[32,2048]{1,0:T(8,128)(2,1)S(1)}, u32[]{:S(2)}, u32[]{:S(2)}) %collective-permute-start.4) | collective-permute-done | bytes 131104 | tf_op jit(solution)/shard_map/ppermute | solution.py:99
  36.6 1.6 %collective-permute-start.9 = (bf16[96,2048]{1,0:T(8,128)(2,1)S(1)}, bf16[96,2048]{1,0:T(8,128)(2,1)S(1)}, u32[]{:S(2)}, u32[]{:S(2)}) collective-permute-start(bf16[96,2048]{1,0:T(8,128)(2,1)S(1)} %pad_maximum_fusion.1), channel_id=1, source_target_pairs={{0,2},{1,3},{2,0},{3,1},{4,6},{5,7},{6,4},{7,5},{8,10},{9,11},{10,... | collective-permute-start | bytes 1179656 | tf_op jit(solution)/shard_map/ppermute | solution.py:103
  38.1 13.7 %forward_products.1 = (bf16[256,2048]{1,0:T(8,128)(2,1)S(1)}, f32[256,1536]{1,0:T(8,128)S(1)}, f32[256,1536]{1,0:T(8,128)S(1)}, f32[256,256]{1,0:T(8,128)S(1)}, bf16[256,1536]{1,0:T(8,128)(2,1)S(1)}) custom-call(bf16[128,256]{1,0:T(8,128)(2,1)S(1)} %and_convert_fusion.spread, bf16[256,128]{1,0:T(8,128)(2,1)S(1)} %fusion.1.collect, ...), custom_call_target="tpu_custom_call" | custom-call | flops 4831838208 | bytes 20971520 | tf_op jit(solution)/shard_map/forward_products/pallas_call | solution.py:281
  52.5 13.5 %backward_products.1 = (bf16[256,2048]{1,0:T(8,128)(2,1)S(1)}, bf16[256,128]{1,0:T(8,128)(2,1)S(1)}, bf16[256,2048]{1,0:T(8,128)(2,1)S(1)}) custom-call(bf16[128,256]{1,0:T(8,128)(2,1)S(1)} %and_convert_fusion.spread, bf16[256,128]{1,0:T(8,128)(2,1)S(1)} %fusion.1.collect, bf16[32,2048]{1,0:T(8,128)(2,1)S(1)} %copy-done.3, ...), custom_call_target="tpu_custom_call" | custom-call | flops 4831838208 | bytes 20971520 | tf_op jit(solution)/shard_map/backward_products/pallas_call | solution.py:316
  67.9 1.0 %convolution_convert_fusion = bf16[768,2048]{1,0:T(8,128)(2,1)S(1)} fusion(bf16[256,768]{1,0:T(8,128)(2,1)S(1)} %slice.50, bf16[256,2048]{1,0:T(8,128)(2,1)S(1)} %get-tuple-element.67.rows), kind=kOutput, calls=%fused_computation | convolution fusion | flops 806879232 | bytes 4587520 | tf_op jit(solution)/shard_map/dot_general | solution.py:123
  68.9 4.4 %collective-permute-done.12 = bf16[64,2048]{1,0:T(8,128)(2,1)S(1)} collective-permute-done((bf16[64,2048]{1,0:T(8,128)(2,1)S(1)}, bf16[64,2048]{1,0:T(8,128)(2,1)S(1)}, u32[]{:S(2)}, u32[]{:S(2)}) %collective-permute-start.12) | collective-permute-done | bytes 262176 | tf_op jit(solution)/shard_map/ppermute | solution.py:99
  73.3 1.3 %collective-permute-done.11 = bf16[64,2176]{1,0:T(8,128)(2,1)S(1)} collective-permute-done((bf16[64,2176]{1,0:T(8,128)(2,1)S(1)}, bf16[64,2176]{1,0:T(8,128)(2,1)S(1)}, u32[]{:S(2)}, u32[]{:S(2)}) %collective-permute-start.11) | collective-permute-done | bytes 278560 | tf_op jit(solution)/shard_map/ppermute | solution.py:103
  75.4 1.8 %collective-permute-start.13 = (bf16[64,2176]{1,0:T(8,128)(2,1)S(1)}, bf16[64,2176]{1,0:T(8,128)(2,1)S(1)}, u32[]{:S(2)}, u32[]{:S(2)}) collective-permute-start(bf16[64,2176]{1,0:T(8,128)(2,1)S(1)} %add_convert_fusion), channel_id=1, source_target_pairs={{0,4},{4,0},{8,12},{12,8},{1,5},{5,1},{9,13},{13,9},{2,6},{6,2},{1... | collective-permute-start | bytes 835592 | tf_op jit(solution)/shard_map/ppermute | solution.py:99
  77.2 1.7 %collective-permute-start.15 = (bf16[32,2048]{1,0:T(8,128)(2,1)S(1)}, bf16[32,2048]{1,0:T(8,128)(2,1)S(1)}, u32[]{:S(2)}, u32[]{:S(2)}) collective-permute-start(bf16[32,2048]{1,0:T(8,128)(2,1)S(1)} %slice.91), channel_id=1, source_target_pairs={{0,8},{4,12},{8,0},{12,4},{1,9},{5,13},{9,1},{13,5},{2,10},{6,14},... | collective-permute-start | bytes 393224 | tf_op jit(solution)/shard_map/ppermute | solution.py:99
  79.0 4.8 %collective-permute-done.14 = bf16[64,2176]{1,0:T(8,128)(2,1)S(1)} collective-permute-done((bf16[64,2176]{1,0:T(8,128)(2,1)S(1)}, bf16[64,2176]{1,0:T(8,128)(2,1)S(1)}, u32[]{:S(2)}, u32[]{:S(2)}) %collective-permute-start.14) | collective-permute-done | bytes 278560 | tf_op jit(solution)/shard_map/ppermute | solution.py:103
  83.7 2.6 %collective-permute-done.15 = bf16[32,2048]{1,0:T(8,128)(2,1)S(1)} collective-permute-done((bf16[32,2048]{1,0:T(8,128)(2,1)S(1)}, bf16[32,2048]{1,0:T(8,128)(2,1)S(1)}, u32[]{:S(2)}, u32[]{:S(2)}) %collective-permute-start.15) | collective-permute-done | bytes 131104 | tf_op jit(solution)/shard_map/ppermute | solution.py:99
  87.2 2.7 %collective-permute-start.17 = (bf16[32,2176]{1,0:T(8,128)(2,1)S(1)}, bf16[32,2176]{1,0:T(8,128)(2,1)S(1)}, u32[]{:S(2)}, u32[]{:S(2)}) collective-permute-start(bf16[32,2176]{1,0:T(8,128)(2,1)S(1)} %slice.89), channel_id=1, source_target_pairs={{0,8},{4,12},{8,0},{12,4},{1,9},{5,13},{9,1},{13,5},{2,10},{6,14},... | collective-permute-start | bytes 417800 | tf_op jit(solution)/shard_map/ppermute | solution.py:99
  90.5 2.9 %finish_share.1 = bf16[192,4,2048]{2,1,0:T(4,128)(2,1)} custom-call(bf16[256,1536]{1,0:T(8,128)(2,1)S(1)} %get-tuple-element.62.weighted, bf16[256,2048]{1,0:T(8,128)(2,1)S(1)} %get-tuple-element.67.rows, bf16[768,2048]{1,0:T(8,128)(2,1)S(1)} %collective-permute-done.16.other), custom_call_target="tpu_custom_call" | custom-call | flops 805306368 | bytes 6291456 | tf_op jit(solution)/shard_map/finish_share/pallas_call | solution.py:350
  93.5 2.7 %collective-permute-done.17 = bf16[32,2176]{1,0:T(8,128)(2,1)S(1)} collective-permute-done((bf16[32,2176]{1,0:T(8,128)(2,1)S(1)}, bf16[32,2176]{1,0:T(8,128)(2,1)S(1)}, u32[]{:S(2)}, u32[]{:S(2)}) %collective-permute-start.17) | collective-permute-done | bytes 139296 | tf_op jit(solution)/shard_map/ppermute | solution.py:99
  (60 shorter events, 10.5 us)
Async XLA Ops:
  3.2 17.7 %collective-permute-start.2 = (bf16[32,2176]{1,0:T(8,128)(2,1)S(1)}, bf16[32,2176]{1,0:T(8,128)(2,1)S(1)}, u32[]{:S(2)}, u32[]{:S(2)}) collective-permute-start(bf16[32,2176]{1,0:T(8,128)(2,1)S(1)} %pad_maximum_fusion.2.refs_0_), channel_id=1, source_target_pairs={{0,12},{4,8},{8,4},{12,0},{1,13},{5,9},{9,5},{13,1},{2,14},{6,10},... | collective-permute-start | bytes 417800 | tf_op jit(solution)/shard_map/ppermute | solution.py:99
  8.3 12.5 %collective-permute-start.1 = (bf16[32,2176]{1,0:T(8,128)(2,1)S(1)}, bf16[32,2176]{1,0:T(8,128)(2,1)S(1)}, u32[]{:S(2)}, u32[]{:S(2)}) collective-permute-start(bf16[32,2176]{1,0:T(8,128)(2,1)S(1)} %pad_maximum_fusion.2.refs_0_), channel_id=1, source_target_pairs={{0,4},{4,0},{8,12},{12,8},{1,5},{5,1},{9,13},{13,9},{2,6},{6,2},{1... | collective-permute-start | bytes 417800 | tf_op jit(solution)/shard_map/ppermute | solution.py:99
  8.3 12.6 %collective-permute-start = (bf16[32,2176]{1,0:T(8,128)(2,1)S(1)}, bf16[32,2176]{1,0:T(8,128)(2,1)S(1)}, u32[]{:S(2)}, u32[]{:S(2)}) collective-permute-start(bf16[32,2176]{1,0:T(8,128)(2,1)S(1)} %pad_maximum_fusion.2.refs_0_), channel_id=1, source_target_pairs={{0,8},{4,12},{8,0},{12,4},{1,9},{5,13},{9,1},{13,5},{2,10},{6,14},... | collective-permute-start | bytes 417800 | tf_op jit(solution)/shard_map/ppermute | solution.py:99
  9.0 11.9 %collective-permute-start.3 = (bf16[32,2048]{1,0:T(8,128)(2,1)}, bf16[32,2048]{1,0:T(8,128)(2,1)S(1)}, u32[]{:S(2)}, u32[]{:S(2)}) collective-permute-start(bf16[32,2048]{1,0:T(8,128)(2,1)} %refs_0_.1), channel_id=1, source_target_pairs={{0,2},{1,3},{2,0},{3,1},{4,6},{5,7},{6,4},{7,5},{8,10},{9,11},{10,... | collective-permute-start | bytes 393224 | tf_op jit(solution)/shard_map/ppermute | solution.py:103
  10.6 1.9 %copy-start = (bf16[192,4,2048]{2,1,0:T(4,128)(2,1)S(1)}, bf16[192,4,2048]{2,1,0:T(4,128)(2,1)}, u32[]{:S(2)}) copy-start(bf16[192,4,2048]{2,1,0:T(4,128)(2,1)} %gate) | copy-start | bytes 9437188
  12.5 1.9 %copy-start.1 = (bf16[192,4,2048]{2,1,0:T(4,128)(2,1)S(1)}, bf16[192,4,2048]{2,1,0:T(4,128)(2,1)}, u32[]{:S(2)}) copy-start(bf16[192,4,2048]{2,1,0:T(4,128)(2,1)} %up.1) | copy-start | bytes 9437188
  14.4 1.9 %copy-start.2 = (bf16[192,4,2048]{2,1,0:T(4,128)(2,1)S(1)}, bf16[192,4,2048]{2,1,0:T(4,128)(2,1)}, u32[]{:S(2)}) copy-start(bf16[192,4,2048]{2,1,0:T(4,128)(2,1)} %down.1) | copy-start | bytes 9437188
  20.9 1.0 %copy-start.3 = (bf16[32,2048]{1,0:T(8,128)(2,1)S(1)}, bf16[32,2048]{1,0:T(8,128)(2,1)}, u32[]{:S(2)}) copy-start(bf16[32,2048]{1,0:T(8,128)(2,1)} %refs_0_.1) | copy-start | bytes 393220
  20.9 17.2 %collective-permute-start.8 = (bf16[3,768,2048]{2,1,0:T(8,128)(2,1)}, bf16[3,768,2048]{2,1,0:T(8,128)(2,1)}, u32[]{:S(2)}, u32[]{:S(2)}) collective-permute-start(bf16[3,768,2048]{2,1,0:T(8,128)(2,1)} %merge_units.1.refs_5_.refs_7_.refs_9_.refs_6_.refs_8_.refs_10_), channel_id=1, source_target_pairs={{0,1},{1,0},{2,3},{3,2},{4,5},{5,4},{6,7},{7,6},{8,9},{9,8},{10,11... | collective-permute-start | bytes 28311560 | tf_op jit(solution)/shard_map/ppermute | solution.py:103
  21.1 15.5 %collective-permute-start.7 = (bf16[128,2176]{1,0:T(8,128)(2,1)S(1)}, bf16[128,2176]{1,0:T(8,128)(2,1)S(1)}, u32[]{:S(2)}, u32[]{:S(2)}) collective-permute-start(bf16[128,2176]{1,0:T(8,128)(2,1)S(1)} %pad_maximum_fusion), channel_id=1, source_target_pairs={{0,2},{1,3},{2,0},{3,1},{4,6},{5,7},{6,4},{7,5},{8,10},{9,11},{10,... | collective-permute-start | bytes 1671176 | tf_op jit(solution)/shard_map/ppermute | solution.py:103
  21.9 8.2 %collective-permute-start.6 = (bf16[32,2048]{1,0:T(8,128)(2,1)S(1)}, bf16[32,2048]{1,0:T(8,128)(2,1)S(1)}, u32[]{:S(2)}, u32[]{:S(2)}) collective-permute-start(bf16[32,2048]{1,0:T(8,128)(2,1)S(1)} %copy-done.3), channel_id=1, source_target_pairs={{0,12},{4,8},{8,4},{12,0},{1,13},{5,9},{9,5},{13,1},{2,14},{6,10},... | collective-permute-start | bytes 393224 | tf_op jit(solution)/shard_map/ppermute | solution.py:99
  25.5 8.2 %collective-permute-start.5 = (bf16[32,2048]{1,0:T(8,128)(2,1)S(1)}, bf16[32,2048]{1,0:T(8,128)(2,1)S(1)}, u32[]{:S(2)}, u32[]{:S(2)}) collective-permute-start(bf16[32,2048]{1,0:T(8,128)(2,1)S(1)} %copy-done.3), channel_id=1, source_target_pairs={{0,4},{4,0},{8,12},{12,8},{1,5},{5,1},{9,13},{13,9},{2,6},{6,2},{1... | collective-permute-start | bytes 393224 | tf_op jit(solution)/shard_map/ppermute | solution.py:99
  25.5 11.1 %collective-permute-start.4 = (bf16[32,2048]{1,0:T(8,128)(2,1)S(1)}, bf16[32,2048]{1,0:T(8,128)(2,1)S(1)}, u32[]{:S(2)}, u32[]{:S(2)}) collective-permute-start(bf16[32,2048]{1,0:T(8,128)(2,1)S(1)} %copy-done.3), channel_id=1, source_target_pairs={{0,8},{4,12},{8,0},{12,4},{1,9},{5,13},{9,1},{13,5},{2,10},{6,14},... | collective-permute-start | bytes 393224 | tf_op jit(solution)/shard_map/ppermute | solution.py:99
  36.6 15.2 %collective-permute-start.9 = (bf16[96,2048]{1,0:T(8,128)(2,1)S(1)}, bf16[96,2048]{1,0:T(8,128)(2,1)S(1)}, u32[]{:S(2)}, u32[]{:S(2)}) collective-permute-start(bf16[96,2048]{1,0:T(8,128)(2,1)S(1)} %pad_maximum_fusion.1), channel_id=1, source_target_pairs={{0,2},{1,3},{2,0},{3,1},{4,6},{5,7},{6,4},{7,5},{8,10},{9,11},{10,... | collective-permute-start | bytes 1179656 | tf_op jit(solution)/shard_map/ppermute | solution.py:103
  51.9 14.1 %collective-permute-start.10 = (bf16[128,2048]{1,0:T(8,128)(2,1)S(1)}, bf16[128,2048]{1,0:T(8,128)(2,1)S(1)}, u32[]{:S(2)}, u32[]{:S(2)}) collective-permute-start(bf16[128,2048]{1,0:T(8,128)(2,1)S(1)} %slice.49), channel_id=1, source_target_pairs={{0,2},{1,3},{2,0},{3,1},{4,6},{5,7},{6,4},{7,5},{8,10},{9,11},{10,... | collective-permute-start | bytes 1572872 | tf_op jit(solution)/shard_map/ppermute | solution.py:103
  66.2 7.1 %collective-permute-start.12 = (bf16[64,2048]{1,0:T(8,128)(2,1)S(1)}, bf16[64,2048]{1,0:T(8,128)(2,1)S(1)}, u32[]{:S(2)}, u32[]{:S(2)}) collective-permute-start(bf16[64,2048]{1,0:T(8,128)(2,1)S(1)} %slice.88), channel_id=1, source_target_pairs={{0,4},{4,0},{8,12},{12,8},{1,5},{5,1},{9,13},{13,9},{2,6},{6,2},{1... | collective-permute-start | bytes 786440 | tf_op jit(solution)/shard_map/ppermute | solution.py:99
  67.2 7.5 %collective-permute-start.11 = (bf16[64,2176]{1,0:T(8,128)(2,1)S(1)}, bf16[64,2176]{1,0:T(8,128)(2,1)S(1)}, u32[]{:S(2)}, u32[]{:S(2)}) collective-permute-start(bf16[64,2176]{1,0:T(8,128)(2,1)S(1)} %get-tuple-element.79), channel_id=1, source_target_pairs={{0,2},{1,3},{2,0},{3,1},{4,6},{5,7},{6,4},{7,5},{8,10},{9,11},{10,... | collective-permute-start | bytes 835592 | tf_op jit(solution)/shard_map/ppermute | solution.py:103
  74.6 12.4 %collective-permute-start.16 = (bf16[768,2048]{1,0:T(8,128)(2,1)S(1)}, bf16[768,2048]{1,0:T(8,128)(2,1)S(1)}, u32[]{:S(2)}, u32[]{:S(2)}) collective-permute-start(bf16[768,2048]{1,0:T(8,128)(2,1)S(1)} %convolution_convert_fusion), channel_id=1, source_target_pairs={{0,1},{1,0},{2,3},{3,2},{4,5},{5,4},{6,7},{7,6},{8,9},{9,8},{10,11... | collective-permute-start | bytes 9437192 | tf_op jit(solution)/shard_map/ppermute | solution.py:103
  74.7 9.1 %collective-permute-start.14 = (bf16[64,2176]{1,0:T(8,128)(2,1)S(1)}, bf16[64,2176]{1,0:T(8,128)(2,1)S(1)}, u32[]{:S(2)}, u32[]{:S(2)}) collective-permute-start(bf16[64,2176]{1,0:T(8,128)(2,1)S(1)} %get-tuple-element.78), channel_id=1, source_target_pairs={{0,2},{1,3},{2,0},{3,1},{4,6},{5,7},{6,4},{7,5},{8,10},{9,11},{10,... | collective-permute-start | bytes 835592 | tf_op jit(solution)/shard_map/ppermute | solution.py:103
  75.4 11.7 %collective-permute-start.13 = (bf16[64,2176]{1,0:T(8,128)(2,1)S(1)}, bf16[64,2176]{1,0:T(8,128)(2,1)S(1)}, u32[]{:S(2)}, u32[]{:S(2)}) collective-permute-start(bf16[64,2176]{1,0:T(8,128)(2,1)S(1)} %add_convert_fusion), channel_id=1, source_target_pairs={{0,4},{4,0},{8,12},{12,8},{1,5},{5,1},{9,13},{13,9},{2,6},{6,2},{1... | collective-permute-start | bytes 835592 | tf_op jit(solution)/shard_map/ppermute | solution.py:99
  77.2 9.0 %collective-permute-start.15 = (bf16[32,2048]{1,0:T(8,128)(2,1)S(1)}, bf16[32,2048]{1,0:T(8,128)(2,1)S(1)}, u32[]{:S(2)}, u32[]{:S(2)}) collective-permute-start(bf16[32,2048]{1,0:T(8,128)(2,1)S(1)} %slice.91), channel_id=1, source_target_pairs={{0,8},{4,12},{8,0},{12,4},{1,9},{5,13},{9,1},{13,5},{2,10},{6,14},... | collective-permute-start | bytes 393224 | tf_op jit(solution)/shard_map/ppermute | solution.py:99
  87.2 9.0 %collective-permute-start.17 = (bf16[32,2176]{1,0:T(8,128)(2,1)S(1)}, bf16[32,2176]{1,0:T(8,128)(2,1)S(1)}, u32[]{:S(2)}, u32[]{:S(2)}) collective-permute-start(bf16[32,2176]{1,0:T(8,128)(2,1)S(1)} %slice.89), channel_id=1, source_target_pairs={{0,8},{4,12},{8,0},{12,4},{1,9},{5,13},{9,1},{13,5},{2,10},{6,14},... | collective-permute-start | bytes 417800 | tf_op jit(solution)/shard_map/ppermute | solution.py:99
  90.5 6.4 %copy-start.4 = (s32[32,8]{0,1:T(8,128)S(1)}, s32[32,8]{0,1:T(8,128)}, u32[]{:S(2)}) copy-start(s32[32,8]{0,1:T(8,128)} %param.10) | copy-start | bytes 3076

commit v4 on v3

--- a/solution.py
+++ b/solution.py
@@ -135,86 +135,80 @@
         start += count
 
 
-def forward_kernel(spread, collect, *refs):
-    del collect
-    pieces, refs = refs[:5], refs[5:]
-    gate_a, gate_b, up_a, up_b, down_a, down_b, out, gate_out, up_out, mask, weighted, rows = refs
-    step = pl.program_id(0)
-    tiles = weighted.shape[1] // UNIT_TILE
-    features = gate_a.shape[1]
-
-    @pl.when(step == 0)
-    def _():
-        place_rows(pieces, rows)
-        mask[...] = dot_plain(rows[:, features:], spread[...])
-
-    def units(gate_w, up_w):
-        token_rows = rows[:, :features]
-        gate_pre = dot_last(token_rows, gate_w[...])
-        up_pre = dot_last(token_rows, up_w[...])
-        gate_out[...] = gate_pre
-        up_out[...] = up_pre
+def bring(sources, held, sems, order):
+    copies = {}
+    for half, slot in order:
+        copy = pltpu.make_async_copy(sources[half].at[slot], held[half].at[slot], sems.at[half, slot])
+        copy.start()
+        copies[half, slot] = copy
+    return copies
+
+
+def unit_tiles(half_rows):
+    return [(half, at) for half in range(2) for at in range(0, half_rows, UNIT_TILE)]
+
+
+def forward_kernel(spread, *refs):
+    pieces, (weights_a, weights_b, out, gate_out, up_out, mask, weighted, rows, held_a, held_b, sems) = refs[:5], refs[5:]
+    held = (held_a, held_b)
+    order = [(0, 0), (0, 1), (1, 0), (1, 1), (0, 2), (1, 2)]
+    copies = bring((weights_a, weights_b), held, sems, order)
+    half_rows, features = held_a.shape[1:]
+    place_rows(pieces, rows)
+    mask[...] = dot_plain(rows[:, features:], spread[...])
+    for half, at in unit_tiles(half_rows):
+        if at == 0:
+            copies[half, 0].wait()
+            copies[half, 1].wait()
+        units = pl.ds(at, UNIT_TILE)
+        gate_pre = dot_last(rows[:, :features], held[half][0, units, :])
+        up_pre = dot_last(rows[:, :features], held[half][1, units, :])
+        columns = pl.ds(half * half_rows + at, UNIT_TILE)
+        gate_out[:, columns] = gate_pre
+        up_out[:, columns] = up_pre
         hidden = gate_pre * jax.nn.sigmoid(gate_pre) * up_pre
-        at = pl.multiple_of(step * UNIT_TILE, UNIT_TILE)
-        weighted[:, pl.ds(at, UNIT_TILE)] = (hidden * mask[...]).astype(jnp.bfloat16)
-
-    @pl.when(step < tiles // 2)
-    def _():
-        units(gate_a, up_a)
-
-    @pl.when((step >= tiles // 2) & (step < tiles))
-    def _():
-        units(gate_b, up_b)
-
-    @pl.when(step >= tiles)
-    def _():
-        half = down_a.shape[0]
-        total = dot_plain(weighted[:, :half], down_a[...]) + dot_plain(weighted[:, half:], down_b[...])
-        out[...] = total.astype(jnp.bfloat16)
-
-
-def backward_kernel(spread, collect, *refs):
-    del spread
+        weighted[:, columns] = (hidden * mask[...]).astype(jnp.bfloat16)
+    copies[0, 2].wait()
+    copies[1, 2].wait()
+    for at in range(0, features, WIDTH_TILE):
+        columns = pl.ds(at, WIDTH_TILE)
+        total = dot_plain(weighted[:, :half_rows], held_a[2, :, columns])
+        total += dot_plain(weighted[:, half_rows:], held_b[2, :, columns])
+        out[:, columns] = total.astype(jnp.bfloat16)
+
+
+def backward_kernel(collect, *refs):
     pieces, refs = refs[:6], refs[6:]
-    gate_a, gate_b, up_a, up_b, down_a, down_b, gate_in, up_in, mask, out, product_out, rows, gate_grad, up_grad, product = refs
-    step = pl.program_id(0)
-    tiles = gate_grad.shape[1] // UNIT_TILE
-
-    @pl.when(step == 0)
-    def _():
-        place_rows(pieces, rows)
-        product[...] = jnp.zeros_like(product)
-
-    def units(down_w):
-        hidden_grad = dot_last(rows[...], down_w[...])
-        gate_pre, up_pre, weight = gate_in[...], up_in[...], mask[...]
+    weights_a, weights_b, gate_in, up_in, mask, out, product_out, rows, gate_grad, up_grad, product, held_a, held_b, sems = refs
+    held = (held_a, held_b)
+    order = [(0, 2), (1, 2), (0, 0), (1, 0), (0, 1), (1, 1)]
+    copies = bring((weights_a, weights_b), held, sems, order)
+    half_rows, features = held_a.shape[1:]
+    place_rows(pieces, rows)
+    for half, at in unit_tiles(half_rows):
+        if at == 0:
+            copies[half, 2].wait()
+        hidden_grad = dot_last(rows[...], held[half][2, pl.ds(at, UNIT_TILE), :])
+        columns = pl.ds(half * half_rows + at, UNIT_TILE)
+        gate_pre, up_pre, weight = gate_in[:, columns], up_in[:, columns], mask[...]
         sig = jax.nn.sigmoid(gate_pre)
         gate_sig = gate_pre * sig
-        product[...] += jnp.where(weight > 0, gate_sig * up_pre * hidden_grad, 0.0)
+        term = jnp.where(weight > 0, gate_sig * up_pre * hidden_grad, 0.0)
+        product[...] = term if half == 0 and at == 0 else product[...] + term
         hidden_grad = hidden_grad * weight
-        at = pl.multiple_of(step * UNIT_TILE, UNIT_TILE)
         slope = sig * (1.0 + gate_pre * (1.0 - sig))
-        gate_grad[:, pl.ds(at, UNIT_TILE)] = (hidden_grad * up_pre * slope).astype(jnp.bfloat16)
-        up_grad[:, pl.ds(at, UNIT_TILE)] = (hidden_grad * gate_sig).astype(jnp.bfloat16)
-
-    @pl.when(step < tiles // 2)
-    def _():
-        units(down_a)
-
-    @pl.when((step >= tiles // 2) & (step < tiles))
-    def _():
-        units(down_b)
-
-    @pl.when(step == tiles)
-    def _():
-        product_out[...] = dot_plain(product[...].astype(jnp.bfloat16), collect[...]).astype(jnp.bfloat16)
-
-    @pl.when(step >= tiles)
-    def _():
-        half = gate_a.shape[0]
-        total = dot_plain(gate_grad[:, :half], gate_a[...]) + dot_plain(gate_grad[:, half:], gate_b[...])
-        total += dot_plain(up_grad[:, :half], up_a[...]) + dot_plain(up_grad[:, half:], up_b[...])
-        out[...] = total.astype(jnp.bfloat16)
+        gate_grad[:, columns] = (hidden_grad * up_pre * slope).astype(jnp.bfloat16)
+        up_grad[:, columns] = (hidden_grad * gate_sig).astype(jnp.bfloat16)
+    product_out[...] = dot_plain(product[...].astype(jnp.bfloat16), collect[...]).astype(jnp.bfloat16)
+    for half, slot in order[2:]:
+        copies[half, slot].wait()
+    for at in range(0, features, WIDTH_TILE):
+        columns = pl.ds(at, WIDTH_TILE)
+        total = dot_plain(gate_grad[:, :half_rows], held_a[0, :, columns])
+        total += dot_plain(gate_grad[:, half_rows:], held_b[0, :, columns])
+        total += dot_plain(up_grad[:, :half_rows], held_a[1, :, columns])
+        total += dot_plain(up_grad[:, half_rows:], held_b[1, :, columns])
+        out[:, columns] = total.astype(jnp.bfloat16)
 
 
 def merge_kernel(gate, up, down, merged):
@@ -242,23 +236,6 @@
     return pl.BlockSpec(array.shape, lambda i: (0, 0))
 
 
-def by_units(array, slot, first):
-    last = array.shape[1] // UNIT_TILE - 1
-    return pl.BlockSpec((None, UNIT_TILE, array.shape[2]), lambda i: (slot, jnp.clip(i - first, 0, last), 0))
-
-
-def by_width(array, slot, first):
-    return pl.BlockSpec((None, array.shape[1], WIDTH_TILE), lambda i: (slot, 0, jnp.maximum(i - first, 0)))
-
-
-def unit_columns(rows, tiles):
-    return pl.BlockSpec((rows, UNIT_TILE), lambda i: (0, jnp.minimum(i, tiles - 1)))
-
-
-def width_columns(rows, tiles):
-    return pl.BlockSpec((rows, WIDTH_TILE), lambda i: (0, jnp.maximum(i - tiles, 0)))
-
-
 def cost(rows, units, features, products):
     return pl.CostEstimate(
         flops=2 * rows * units * features * products,
@@ -268,74 +245,55 @@
 
 
 PARAMS = dict(dimension_semantics=("arbitrary",), vmem_limit_bytes=24 * 1024 * 1024)
-
-
-def forward(tables, pieces, weights):
+IN_VMEM = pl.BlockSpec(memory_space=pltpu.VMEM)
+
+
+def products(kernel, name, table, pieces, weights, saved, out_shape, scratch):
     half, features = weights[0].shape[1:]
     rows = sum(piece.shape[0] for piece in pieces)
-    tiles = 2 * half // UNIT_TILE
-    operands = [*tables, *pieces, *weights * 3]
-    specs = [whole(x) for x in (*tables, *pieces)]
-    specs += [by_units(w, slot, n * tiles // 2) for slot in range(2) for n, w in enumerate(weights)]
-    specs += [by_width(w, 2, tiles) for w in weights]
+    held = [pltpu.VMEM(w.shape, w.dtype) for w in weights]
     return pl.pallas_call(
-        forward_kernel,
-        grid=(tiles + features // WIDTH_TILE,),
-        in_specs=specs,
-        out_specs=[
-            width_columns(rows, tiles),
-            unit_columns(rows, tiles),
-            unit_columns(rows, tiles),
-            pl.BlockSpec((rows, UNIT_TILE), lambda i: (0, 0)),
-            pl.BlockSpec((rows, 2 * half), lambda i: (0, 0)),
-        ],
-        out_shape=[
-            jax.ShapeDtypeStruct((rows, features), jnp.bfloat16),
-            jax.ShapeDtypeStruct((rows, 2 * half), jnp.float32),
-            jax.ShapeDtypeStruct((rows, 2 * half), jnp.float32),
-            jax.ShapeDtypeStruct((rows, UNIT_TILE), jnp.float32),
-            jax.ShapeDtypeStruct((rows, 2 * half), jnp.bfloat16),
-        ],
-        scratch_shapes=[pltpu.VMEM((rows, pieces[0].shape[1]), jnp.bfloat16)],
-        compiler_params=pltpu.CompilerParams(**PARAMS),
+        kernel,
+        in_specs=[IN_VMEM] * (1 + len(pieces)) + [pl.BlockSpec(memory_space=pl.ANY)] * 2 + [IN_VMEM] * len(saved),
+        out_specs=[IN_VMEM] * len(out_shape),
+        out_shape=out_shape,
+        scratch_shapes=[*scratch, *held, pltpu.SemaphoreType.DMA((2, 3))],
+        compiler_params=pltpu.CompilerParams(vmem_limit_bytes=PRODUCT_VMEM),
         cost_estimate=cost(rows, 2 * half, features, 3),
-        name="forward_products",
-    )(*operands)
-
-
-def backward(tables, pieces, weights, gate_pre, up_pre, mask):
+        name=name,
+    )(table, *pieces, *weights, *saved)
+
+
+PRODUCT_VMEM = 34 * 1024 * 1024
+
+
+def forward(spread, pieces, weights):
     half, features = weights[0].shape[1:]
     rows = sum(piece.shape[0] for piece in pieces)
-    tiles = 2 * half // UNIT_TILE
-    operands = [*tables, *pieces, *weights * 3, gate_pre, up_pre, mask]
-    specs = [whole(x) for x in (*tables, *pieces)]
-    specs += [by_width(w, slot, tiles) for slot in range(2) for w in weights]
-    specs += [by_units(w, 2, n * tiles // 2) for n, w in enumerate(weights)]
-    specs += [unit_columns(rows, tiles), unit_columns(rows, tiles), whole(mask)]
-    side = tables[1].shape[1]
-    return pl.pallas_call(
-        backward_kernel,
-        grid=(tiles + features // WIDTH_TILE,),
-        in_specs=specs,
-        out_specs=[
-            width_columns(rows, tiles),
-            pl.BlockSpec((rows, side), lambda i: (0, 0)),
-            pl.BlockSpec((rows, features), lambda i: (0, 0)),
-        ],
-        out_shape=[
-            jax.ShapeDtypeStruct((rows, features), jnp.bfloat16),
-            jax.ShapeDtypeStruct((rows, side), jnp.bfloat16),
-            jax.ShapeDtypeStruct((rows, features), jnp.bfloat16),
-        ],
-        scratch_shapes=[
-            pltpu.VMEM((rows, 2 * half), jnp.bfloat16),
-            pltpu.VMEM((rows, 2 * half), jnp.bfloat16),
-            pltpu.VMEM((rows, UNIT_TILE), jnp.float32),
-        ],
-        compiler_params=pltpu.CompilerParams(**PARAMS),
-        cost_estimate=cost(rows, 2 * half, features, 3),
-        name="backward_products",
-    )(*operands)
+    shape = jax.ShapeDtypeStruct
+    out_shape = [
+        shape((rows, features), jnp.bfloat16),
+        shape((rows, 2 * half), jnp.float32),
+        shape((rows, 2 * half), jnp.float32),
+        shape((rows, UNIT_TILE), jnp.float32),
+        shape((rows, 2 * half), jnp.bfloat16),
+    ]
+    scratch = [pltpu.VMEM((rows, pieces[0].shape[1]), jnp.bfloat16)]
+    return products(forward_kernel, "forward_products", spread, pieces, weights, [], out_shape, scratch)
+
+
+def backward(collect, pieces, weights, gate_pre, up_pre, mask):
+    half, features = weights[0].shape[1:]
+    rows = sum(piece.shape[0] for piece in pieces)
+    shape = jax.ShapeDtypeStruct
+    out_shape = [
+        shape((rows, features), jnp.bfloat16),
+        shape((rows, collect.shape[1]), jnp.bfloat16),
+        shape((rows, features), jnp.bfloat16),
+    ]
+    scratch = [pltpu.VMEM((rows, 2 * half), jnp.bfloat16)] * 2 + [pltpu.VMEM((rows, UNIT_TILE), jnp.float32)]
+    saved = [gate_pre, up_pre, mask]
+    return products(backward_kernel, "backward_products", collect, pieces, weights, saved, out_shape, scratch)
 
 
 def share_kernel(weighted, rows, other, out):
@@ -380,7 +338,7 @@
     columns = jnp.arange(side, dtype=jnp.int32)
     spread = (columns[:, None] % experts == unit_expert[None, :]) & (columns < 2 * experts)[:, None]
     collect = (unit_expert[:, None] == columns[None, :]).astype(jnp.bfloat16)
-    tables = (spread.astype(jnp.bfloat16), collect)
+    spread = spread.astype(jnp.bfloat16)
 
     own_t = jnp.concatenate([tokens, routed], axis=1)
     own_t, own_g, w_gate = lax.optimization_barrier((own_t, out_grad, w_gate))
@@ -397,14 +355,14 @@
 
     away_gx = over_dp(jnp.concatenate(column_g, axis=0), 2)
     weights = [weights, weights_b]
-    out_part, gate_pre, up_pre, mask, weighted = forward(tables, [*pieces_t, column_tx], weights)
+    out_part, gate_pre, up_pre, mask, weighted = forward(spread, [*pieces_t, column_tx], weights)
     out_part, away_gx = lax.optimization_barrier((out_part, away_gx))
 
     half = out_part.shape[0] // 2
     pair, block = half // 2, half // 4
     out_x = over_dp(out_part[half:], 2)
     grad_pieces = [out_grad, *column_g, own_gx, away_gx]
-    grad_part, product_part, grad_rows = backward(tables, grad_pieces, weights, gate_pre, up_pre, mask)
+    grad_part, product_part, grad_rows = backward(collect, grad_pieces, weights, gate_pre, up_pre, mask)
     weighted_b = weighted[:, unit_rows:]
     grad_part, product_part, out_x, weighted_b = lax.optimization_barrier((grad_part, product_part, out_x, weighted_b))
 

time: 98.1 us -> 91.1 us (0.929)
  Pallas kernels: 34.6 us -> 25.8 us
  waiting for transfers between devices: 26.6 us -> 27.8 us
    pallas_call x2, Pallas kernels: 27.1 us -> 18.3 us  [products(): pl.pallas_call(kernel, in_specs=[IN_VMEM] * (1 + len(pieces)) + [pl.Block...]
    ppermute x8, waiting for transfers between devices: 6.11 us -> 8.14 us  [over_dp(): lax.ppermute(rows, 'dp', [(i, i ^ bit) for i in range(lax.axis_size('dp'))])]
  transfers between devices with their start and end apart: 18 -> 18, of which waited for: 9 -> 11; matrix products, arithmetic and copies ran while one was open for 2% -> 2% of each run, Pallas kernels for 35% -> 28%
where the time goes in v4:
time: 91.1 us; the launch traced here: 90.8 us
  waiting for transfers between devices  27.8 us (31%)
  Pallas kernels  25.8 us (28%)
  starting transfers between devices  24.1 us (26%)
  local copies, waits for them, and re-layouts  6.86 us (8%)
  other arithmetic  4.39 us (5%)
  matrix products  1.01 us (1%)
    ppermute x10, waiting for transfers between devices, over_z(): lax.ppermute(rows, 'expert', [(i, i ^ bit) for i in range(lax.axis_size('...  19.6 us
    pallas_call x2, Pallas kernels, products(): pl.pallas_call(kernel, in_specs=[IN_VMEM] * (1 + len(pieces)) + [pl.Block...  18.3 us
    ppermute x10, starting transfers between devices, over_z(): lax.ppermute(rows, 'expert', [(i, i ^ bit) for i in range(lax.axis_size('...  17.5 us
    ppermute x8, waiting for transfers between devices, over_dp(): lax.ppermute(rows, 'dp', [(i, i ^ bit) for i in range(lax.axis_size('dp'))])  8.14 us
    ppermute x8, starting transfers between devices, over_dp(): lax.ppermute(rows, 'dp', [(i, i ^ bit) for i in range(lax.axis_size('dp'))])  6.64 us
    unnamed x11, local copies, waits for them, and re-layouts  5.78 us
    pallas_call x1, Pallas kernels, merge_units(): pl.pallas_call(merge_kernel, grid=(units // tile,), in_specs=[block] * 3,...  4.58 us
    pallas_call x1, Pallas kernels, finish_share(): pl.pallas_call(share_kernel, grid=(units // tile,), in_specs=[pl.BlockSpe...  2.91 us
  transfers between devices with their start and end apart: 18, of which 11 were waited for; matrix products, arithmetic and copies ran while one was open for 2% of the time, Pallas kernels for 28%

profile of v4, /device:TPU:0, one launch (start us, length us, event | category | flops | bytes accessed | tf_op | source)
XLA Modules:
  0.0 90.8 jit_solution(10222780813102423792)
XLA Ops:
  3.2 5.1 %collective-permute-start.2 = (bf16[32,2176]{1,0:T(8,128)(2,1)S(1)}, bf16[32,2176]{1,0:T(8,128)(2,1)S(1)}, u32[]{:S(2)}, u32[]{:S(2)}) collective-permute-start(bf16[32,2176]{1,0:T(8,128)(2,1)S(1)} %pad_maximum_fusion.2.refs_0_), channel_id=1, source_target_pairs={{0,12},{4,8},{8,4},{12,0},{1,13},{5,9},{9,5},{13,1},{2,14},{6,10},... | collective-permute-start | bytes 417800 | tf_op jit(solution)/shard_map/ppermute | solution.py:99
  9.0 1.6 %collective-permute-start.3 = (bf16[32,2048]{1,0:T(8,128)(2,1)}, bf16[32,2048]{1,0:T(8,128)(2,1)S(1)}, u32[]{:S(2)}, u32[]{:S(2)}) collective-permute-start(bf16[32,2048]{1,0:T(8,128)(2,1)} %refs_0_.1), channel_id=1, source_target_pairs={{0,2},{1,3},{2,0},{3,1},{4,6},{5,7},{6,4},{7,5},{8,10},{9,11},{10,... | collective-permute-start | bytes 393224 | tf_op jit(solution)/shard_map/ppermute | solution.py:103
  10.6 1.9 %copy-done = bf16[192,4,2048]{2,1,0:T(4,128)(2,1)S(1)} copy-done((bf16[192,4,2048]{2,1,0:T(4,128)(2,1)S(1)}, bf16[192,4,2048]{2,1,0:T(4,128)(2,1)}, u32[]{:S(2)}) %copy-start) | copy-done | bytes 3145752
  12.5 1.9 %copy-done.1 = bf16[192,4,2048]{2,1,0:T(4,128)(2,1)S(1)} copy-done((bf16[192,4,2048]{2,1,0:T(4,128)(2,1)S(1)}, bf16[192,4,2048]{2,1,0:T(4,128)(2,1)}, u32[]{:S(2)}) %copy-start.1) | copy-done | bytes 3145752
  14.4 1.9 %copy-done.2 = bf16[192,4,2048]{2,1,0:T(4,128)(2,1)S(1)} copy-done((bf16[192,4,2048]{2,1,0:T(4,128)(2,1)S(1)}, bf16[192,4,2048]{2,1,0:T(4,128)(2,1)}, u32[]{:S(2)}) %copy-start.2) | copy-done | bytes 3145752
  16.3 4.6 %merge_units.1.refs_5_.refs_6_ = bf16[3,768,2048]{2,1,0:T(8,128)(2,1)} custom-call(bf16[192,4,2048]{2,1,0:T(4,128)(2,1)S(1)} %copy-done, bf16[192,4,2048]{2,1,0:T(4,128)(2,1)S(1)} %copy-done.1, bf16[192,4,2048]{2,1,0:T(4,128)(2,1)S(1)} %copy-done.2), custom_call_target="tpu_custom_call" | custom-call | bytes 18874368 | tf_op jit(solution)/shard_map/merge_units/pallas_call | solution.py:223
  21.8 3.6 %collective-permute-start.6 = (bf16[32,2048]{1,0:T(8,128)(2,1)S(1)}, bf16[32,2048]{1,0:T(8,128)(2,1)S(1)}, u32[]{:S(2)}, u32[]{:S(2)}) collective-permute-start(bf16[32,2048]{1,0:T(8,128)(2,1)S(1)} %copy-done.3), channel_id=1, source_target_pairs={{0,12},{4,8},{8,4},{12,0},{1,13},{5,9},{9,5},{13,1},{2,14},{6,10},... | collective-permute-start | bytes 393224 | tf_op jit(solution)/shard_map/ppermute | solution.py:99
  26.3 3.7 %collective-permute-done.6.refs_3_ = bf16[32,2048]{1,0:T(8,128)(2,1)S(1)} collective-permute-done((bf16[32,2048]{1,0:T(8,128)(2,1)S(1)}, bf16[32,2048]{1,0:T(8,128)(2,1)S(1)}, u32[]{:S(2)}, u32[]{:S(2)}) %collective-permute-start.6) | collective-permute-done | bytes 131104 | tf_op jit(solution)/shard_map/ppermute | solution.py:99
  30.0 3.5 %collective-permute-done.5.refs_2_ = bf16[32,2048]{1,0:T(8,128)(2,1)S(1)} collective-permute-done((bf16[32,2048]{1,0:T(8,128)(2,1)S(1)}, bf16[32,2048]{1,0:T(8,128)(2,1)S(1)}, u32[]{:S(2)}, u32[]{:S(2)}) %collective-permute-start.5) | collective-permute-done | bytes 131104 | tf_op jit(solution)/shard_map/ppermute | solution.py:99
  33.5 2.9 %collective-permute-done.4.refs_1_ = bf16[32,2048]{1,0:T(8,128)(2,1)S(1)} collective-permute-done((bf16[32,2048]{1,0:T(8,128)(2,1)S(1)}, bf16[32,2048]{1,0:T(8,128)(2,1)S(1)}, u32[]{:S(2)}, u32[]{:S(2)}) %collective-permute-start.4) | collective-permute-done | bytes 131104 | tf_op jit(solution)/shard_map/ppermute | solution.py:99
  36.5 1.6 %collective-permute-start.9 = (bf16[96,2048]{1,0:T(8,128)(2,1)S(1)}, bf16[96,2048]{1,0:T(8,128)(2,1)S(1)}, u32[]{:S(2)}, u32[]{:S(2)}) collective-permute-start(bf16[96,2048]{1,0:T(8,128)(2,1)S(1)} %pad_maximum_fusion.1), channel_id=1, source_target_pairs={{0,2},{1,3},{2,0},{3,1},{4,6},{5,7},{6,4},{7,5},{8,10},{9,11},{10,... | collective-permute-start | bytes 1179656 | tf_op jit(solution)/shard_map/ppermute | solution.py:103
  38.0 8.4 %forward_products.1 = (bf16[256,2048]{1,0:T(8,128)(2,1)S(1)}, f32[256,1536]{1,0:T(8,128)S(1)}, f32[256,1536]{1,0:T(8,128)S(1)}, f32[256,256]{1,0:T(8,128)S(1)}, bf16[256,1536]{1,0:T(8,128)(2,1)S(1)}) custom-call(bf16[128,256]{1,0:T(8,128)(2,1)S(1)} %and_convert_fusion.spread, bf16[32,2176]{1,0:T(8,128)(2,1)S(1)} %pad_maximum_fusion.2.refs_0_, ...), custom_call_target="tpu_custom_call" | custom-call | flops 4831838208 | bytes 20971520 | tf_op jit(solution)/shard_map/forward_products/pallas_call | solution.py:255
  47.0 1.6 %collective-permute-start.10 = (bf16[128,2048]{1,0:T(8,128)(2,1)S(1)}, bf16[128,2048]{1,0:T(8,128)(2,1)S(1)}, u32[]{:S(2)}, u32[]{:S(2)}) collective-permute-start(bf16[128,2048]{1,0:T(8,128)(2,1)S(1)} %slice.49), channel_id=1, source_target_pairs={{0,2},{1,3},{2,0},{3,1},{4,6},{5,7},{6,4},{7,5},{8,10},{9,11},{10,... | collective-permute-start | bytes 1572872 | tf_op jit(solution)/shard_map/ppermute | solution.py:103
  48.7 9.9 %backward_products.1 = (bf16[256,2048]{1,0:T(8,128)(2,1)S(1)}, bf16[256,128]{1,0:T(8,128)(2,1)S(1)}, bf16[256,2048]{1,0:T(8,128)(2,1)S(1)}) custom-call(bf16[256,128]{1,0:T(8,128)(2,1)S(1)} %fusion.1.collect, bf16[32,2048]{1,0:T(8,128)(2,1)S(1)} %copy-done.3, bf16[32,2048]{1,0:T(8,128)(2,1)S(1)} %collective-permute-done.4.refs_1_, ...), custom_call_target="tpu_custom_call" | custom-call | flops 4831838208 | bytes 20971520 | tf_op jit(solution)/shard_map/backward_products/pallas_call | solution.py:255
  59.7 1.5 %collective-permute-start.12 = (bf16[64,2048]{1,0:T(8,128)(2,1)S(1)}, bf16[64,2048]{1,0:T(8,128)(2,1)S(1)}, u32[]{:S(2)}, u32[]{:S(2)}) collective-permute-start(bf16[64,2048]{1,0:T(8,128)(2,1)S(1)} %slice.88), channel_id=1, source_target_pairs={{0,4},{4,0},{8,12},{12,8},{1,5},{5,1},{9,13},{13,9},{2,6},{6,2},{1... | collective-permute-start | bytes 786440 | tf_op jit(solution)/shard_map/ppermute | solution.py:99
  62.9 3.2 %collective-permute-done.12 = bf16[64,2048]{1,0:T(8,128)(2,1)S(1)} collective-permute-done((bf16[64,2048]{1,0:T(8,128)(2,1)S(1)}, bf16[64,2048]{1,0:T(8,128)(2,1)S(1)}, u32[]{:S(2)}, u32[]{:S(2)}) %collective-permute-start.12) | collective-permute-done | bytes 262176 | tf_op jit(solution)/shard_map/ppermute | solution.py:99
  66.2 1.8 %collective-permute-done.11 = bf16[64,2176]{1,0:T(8,128)(2,1)S(1)} collective-permute-done((bf16[64,2176]{1,0:T(8,128)(2,1)S(1)}, bf16[64,2176]{1,0:T(8,128)(2,1)S(1)}, u32[]{:S(2)}, u32[]{:S(2)}) %collective-permute-start.11) | collective-permute-done | bytes 278560 | tf_op jit(solution)/shard_map/ppermute | solution.py:103
  68.6 1.4 %collective-permute-start.13 = (bf16[64,2176]{1,0:T(8,128)(2,1)S(1)}, bf16[64,2176]{1,0:T(8,128)(2,1)S(1)}, u32[]{:S(2)}, u32[]{:S(2)}) collective-permute-start(bf16[64,2176]{1,0:T(8,128)(2,1)S(1)} %add_convert_fusion), channel_id=1, source_target_pairs={{0,4},{4,0},{8,12},{12,8},{1,5},{5,1},{9,13},{13,9},{2,6},{6,2},{1... | collective-permute-start | bytes 835592 | tf_op jit(solution)/shard_map/ppermute | solution.py:99
  70.1 2.0 %collective-permute-start.15 = (bf16[32,2048]{1,0:T(8,128)(2,1)S(1)}, bf16[32,2048]{1,0:T(8,128)(2,1)S(1)}, u32[]{:S(2)}, u32[]{:S(2)}) collective-permute-start(bf16[32,2048]{1,0:T(8,128)(2,1)S(1)} %slice.91), channel_id=1, source_target_pairs={{0,8},{4,12},{8,0},{12,4},{1,9},{5,13},{9,1},{13,5},{2,10},{6,14},... | collective-permute-start | bytes 393224 | tf_op jit(solution)/shard_map/ppermute | solution.py:99
  72.0 5.0 %collective-permute-done.14 = bf16[64,2176]{1,0:T(8,128)(2,1)S(1)} collective-permute-done((bf16[64,2176]{1,0:T(8,128)(2,1)S(1)}, bf16[64,2176]{1,0:T(8,128)(2,1)S(1)}, u32[]{:S(2)}, u32[]{:S(2)}) %collective-permute-start.14) | collective-permute-done | bytes 278560 | tf_op jit(solution)/shard_map/ppermute | solution.py:103
  77.0 2.1 %collective-permute-done.15 = bf16[32,2048]{1,0:T(8,128)(2,1)S(1)} collective-permute-done((bf16[32,2048]{1,0:T(8,128)(2,1)S(1)}, bf16[32,2048]{1,0:T(8,128)(2,1)S(1)}, u32[]{:S(2)}, u32[]{:S(2)}) %collective-permute-start.15) | collective-permute-done | bytes 131104 | tf_op jit(solution)/shard_map/ppermute | solution.py:99
  80.4 2.4 %collective-permute-start.17 = (bf16[32,2176]{1,0:T(8,128)(2,1)S(1)}, bf16[32,2176]{1,0:T(8,128)(2,1)S(1)}, u32[]{:S(2)}, u32[]{:S(2)}) collective-permute-start(bf16[32,2176]{1,0:T(8,128)(2,1)S(1)} %slice.89), channel_id=1, source_target_pairs={{0,8},{4,12},{8,0},{12,4},{1,9},{5,13},{9,1},{13,5},{2,10},{6,14},... | collective-permute-start | bytes 417800 | tf_op jit(solution)/shard_map/ppermute | solution.py:99
  83.4 2.9 %finish_share.1 = bf16[192,4,2048]{2,1,0:T(4,128)(2,1)} custom-call(bf16[256,1536]{1,0:T(8,128)(2,1)S(1)} %get-tuple-element.62.weighted, bf16[256,2048]{1,0:T(8,128)(2,1)S(1)} %get-tuple-element.67.rows, bf16[768,2048]{1,0:T(8,128)(2,1)S(1)} %collective-permute-done.16.other), custom_call_target="tpu_custom_call" | custom-call | flops 805306368 | bytes 6291456 | tf_op jit(solution)/shard_map/finish_share/pallas_call | solution.py:308
  86.3 3.1 %collective-permute-done.17 = bf16[32,2176]{1,0:T(8,128)(2,1)S(1)} collective-permute-done((bf16[32,2176]{1,0:T(8,128)(2,1)S(1)}, bf16[32,2176]{1,0:T(8,128)(2,1)S(1)}, u32[]{:S(2)}, u32[]{:S(2)}) %collective-permute-start.17) | collective-permute-done | bytes 139296 | tf_op jit(solution)/shard_map/ppermute | solution.py:99
  (60 shorter events, 12.5 us)
Async XLA Ops:
  3.2 17.7 %collective-permute-start.2 = (bf16[32,2176]{1,0:T(8,128)(2,1)S(1)}, bf16[32,2176]{1,0:T(8,128)(2,1)S(1)}, u32[]{:S(2)}, u32[]{:S(2)}) collective-permute-start(bf16[32,2176]{1,0:T(8,128)(2,1)S(1)} %pad_maximum_fusion.2.refs_0_), channel_id=1, source_target_pairs={{0,12},{4,8},{8,4},{12,0},{1,13},{5,9},{9,5},{13,1},{2,14},{6,10},... | collective-permute-start | bytes 417800 | tf_op jit(solution)/shard_map/ppermute | solution.py:99
  8.3 12.5 %collective-permute-start.1 = (bf16[32,2176]{1,0:T(8,128)(2,1)S(1)}, bf16[32,2176]{1,0:T(8,128)(2,1)S(1)}, u32[]{:S(2)}, u32[]{:S(2)}) collective-permute-start(bf16[32,2176]{1,0:T(8,128)(2,1)S(1)} %pad_maximum_fusion.2.refs_0_), channel_id=1, source_target_pairs={{0,4},{4,0},{8,12},{12,8},{1,5},{5,1},{9,13},{13,9},{2,6},{6,2},{1... | collective-permute-start | bytes 417800 | tf_op jit(solution)/shard_map/ppermute | solution.py:99
  8.3 12.6 %collective-permute-start = (bf16[32,2176]{1,0:T(8,128)(2,1)S(1)}, bf16[32,2176]{1,0:T(8,128)(2,1)S(1)}, u32[]{:S(2)}, u32[]{:S(2)}) collective-permute-start(bf16[32,2176]{1,0:T(8,128)(2,1)S(1)} %pad_maximum_fusion.2.refs_0_), channel_id=1, source_target_pairs={{0,8},{4,12},{8,0},{12,4},{1,9},{5,13},{9,1},{13,5},{2,10},{6,14},... | collective-permute-start | bytes 417800 | tf_op jit(solution)/shard_map/ppermute | solution.py:99
  9.0 11.9 %collective-permute-start.3 = (bf16[32,2048]{1,0:T(8,128)(2,1)}, bf16[32,2048]{1,0:T(8,128)(2,1)S(1)}, u32[]{:S(2)}, u32[]{:S(2)}) collective-permute-start(bf16[32,2048]{1,0:T(8,128)(2,1)} %refs_0_.1), channel_id=1, source_target_pairs={{0,2},{1,3},{2,0},{3,1},{4,6},{5,7},{6,4},{7,5},{8,10},{9,11},{10,... | collective-permute-start | bytes 393224 | tf_op jit(solution)/shard_map/ppermute | solution.py:103
  10.6 1.9 %copy-start = (bf16[192,4,2048]{2,1,0:T(4,128)(2,1)S(1)}, bf16[192,4,2048]{2,1,0:T(4,128)(2,1)}, u32[]{:S(2)}) copy-start(bf16[192,4,2048]{2,1,0:T(4,128)(2,1)} %gate) | copy-start | bytes 9437188
  12.5 1.9 %copy-start.1 = (bf16[192,4,2048]{2,1,0:T(4,128)(2,1)S(1)}, bf16[192,4,2048]{2,1,0:T(4,128)(2,1)}, u32[]{:S(2)}) copy-start(bf16[192,4,2048]{2,1,0:T(4,128)(2,1)} %up.1) | copy-start | bytes 9437188
  14.4 1.9 %copy-start.2 = (bf16[192,4,2048]{2,1,0:T(4,128)(2,1)S(1)}, bf16[192,4,2048]{2,1,0:T(4,128)(2,1)}, u32[]{:S(2)}) copy-start(bf16[192,4,2048]{2,1,0:T(4,128)(2,1)} %down.1) | copy-start | bytes 9437188
  20.9 0.9 copy-start.3
  20.9 17.1 %collective-permute-start.8 = (bf16[3,768,2048]{2,1,0:T(8,128)(2,1)}, bf16[3,768,2048]{2,1,0:T(8,128)(2,1)}, u32[]{:S(2)}, u32[]{:S(2)}) collective-permute-start(bf16[3,768,2048]{2,1,0:T(8,128)(2,1)} %merge_units.1.refs_5_.refs_6_), channel_id=1, source_target_pairs={{0,1},{1,0},{2,3},{3,2},{4,5},{5,4},{6,7},{7,6},{8,9},{9,8},{10,11... | collective-permute-start | bytes 28311560 | tf_op jit(solution)/shard_map/ppermute | solution.py:103
  21.0 15.4 %collective-permute-start.7 = (bf16[128,2176]{1,0:T(8,128)(2,1)S(1)}, bf16[128,2176]{1,0:T(8,128)(2,1)S(1)}, u32[]{:S(2)}, u32[]{:S(2)}) collective-permute-start(bf16[128,2176]{1,0:T(8,128)(2,1)S(1)} %pad_maximum_fusion), channel_id=1, source_target_pairs={{0,2},{1,3},{2,0},{3,1},{4,6},{5,7},{6,4},{7,5},{8,10},{9,11},{10,... | collective-permute-start | bytes 1671176 | tf_op jit(solution)/shard_map/ppermute | solution.py:103
  21.8 8.2 %collective-permute-start.6 = (bf16[32,2048]{1,0:T(8,128)(2,1)S(1)}, bf16[32,2048]{1,0:T(8,128)(2,1)S(1)}, u32[]{:S(2)}, u32[]{:S(2)}) collective-permute-start(bf16[32,2048]{1,0:T(8,128)(2,1)S(1)} %copy-done.3), channel_id=1, source_target_pairs={{0,12},{4,8},{8,4},{12,0},{1,13},{5,9},{9,5},{13,1},{2,14},{6,10},... | collective-permute-start | bytes 393224 | tf_op jit(solution)/shard_map/ppermute | solution.py:99
  25.4 8.1 %collective-permute-start.5 = (bf16[32,2048]{1,0:T(8,128)(2,1)S(1)}, bf16[32,2048]{1,0:T(8,128)(2,1)S(1)}, u32[]{:S(2)}, u32[]{:S(2)}) collective-permute-start(bf16[32,2048]{1,0:T(8,128)(2,1)S(1)} %copy-done.3), channel_id=1, source_target_pairs={{0,4},{4,0},{8,12},{12,8},{1,5},{5,1},{9,13},{13,9},{2,6},{6,2},{1... | collective-permute-start | bytes 393224 | tf_op jit(solution)/shard_map/ppermute | solution.py:99
  25.4 11.1 %collective-permute-start.4 = (bf16[32,2048]{1,0:T(8,128)(2,1)S(1)}, bf16[32,2048]{1,0:T(8,128)(2,1)S(1)}, u32[]{:S(2)}, u32[]{:S(2)}) collective-permute-start(bf16[32,2048]{1,0:T(8,128)(2,1)S(1)} %copy-done.3), channel_id=1, source_target_pairs={{0,8},{4,12},{8,0},{12,4},{1,9},{5,13},{9,1},{13,5},{2,10},{6,14},... | collective-permute-start | bytes 393224 | tf_op jit(solution)/shard_map/ppermute | solution.py:99
  36.5 10.5 %collective-permute-start.9 = (bf16[96,2048]{1,0:T(8,128)(2,1)S(1)}, bf16[96,2048]{1,0:T(8,128)(2,1)S(1)}, u32[]{:S(2)}, u32[]{:S(2)}) collective-permute-start(bf16[96,2048]{1,0:T(8,128)(2,1)S(1)} %pad_maximum_fusion.1), channel_id=1, source_target_pairs={{0,2},{1,3},{2,0},{3,1},{4,6},{5,7},{6,4},{7,5},{8,10},{9,11},{10,... | collective-permute-start | bytes 1179656 | tf_op jit(solution)/shard_map/ppermute | solution.py:103
  47.0 12.5 %collective-permute-start.10 = (bf16[128,2048]{1,0:T(8,128)(2,1)S(1)}, bf16[128,2048]{1,0:T(8,128)(2,1)S(1)}, u32[]{:S(2)}, u32[]{:S(2)}) collective-permute-start(bf16[128,2048]{1,0:T(8,128)(2,1)S(1)} %slice.49), channel_id=1, source_target_pairs={{0,2},{1,3},{2,0},{3,1},{4,6},{5,7},{6,4},{7,5},{8,10},{9,11},{10,... | collective-permute-start | bytes 1572872 | tf_op jit(solution)/shard_map/ppermute | solution.py:103
  59.7 6.4 %collective-permute-start.12 = (bf16[64,2048]{1,0:T(8,128)(2,1)S(1)}, bf16[64,2048]{1,0:T(8,128)(2,1)S(1)}, u32[]{:S(2)}, u32[]{:S(2)}) collective-permute-start(bf16[64,2048]{1,0:T(8,128)(2,1)S(1)} %slice.88), channel_id=1, source_target_pairs={{0,4},{4,0},{8,12},{12,8},{1,5},{5,1},{9,13},{13,9},{2,6},{6,2},{1... | collective-permute-start | bytes 786440 | tf_op jit(solution)/shard_map/ppermute | solution.py:99
  61.3 6.6 %collective-permute-start.11 = (bf16[64,2176]{1,0:T(8,128)(2,1)S(1)}, bf16[64,2176]{1,0:T(8,128)(2,1)S(1)}, u32[]{:S(2)}, u32[]{:S(2)}) collective-permute-start(bf16[64,2176]{1,0:T(8,128)(2,1)S(1)} %get-tuple-element.79), channel_id=1, source_target_pairs={{0,2},{1,3},{2,0},{3,1},{4,6},{5,7},{6,4},{7,5},{8,10},{9,11},{10,... | collective-permute-start | bytes 835592 | tf_op jit(solution)/shard_map/ppermute | solution.py:103
  67.9 12.3 %collective-permute-start.16 = (bf16[768,2048]{1,0:T(8,128)(2,1)S(1)}, bf16[768,2048]{1,0:T(8,128)(2,1)S(1)}, u32[]{:S(2)}, u32[]{:S(2)}) collective-permute-start(bf16[768,2048]{1,0:T(8,128)(2,1)S(1)} %convolution_convert_fusion), channel_id=1, source_target_pairs={{0,1},{1,0},{2,3},{3,2},{4,5},{5,4},{6,7},{7,6},{8,9},{9,8},{10,11... | collective-permute-start | bytes 9437192 | tf_op jit(solution)/shard_map/ppermute | solution.py:103
  67.9 9.1 %collective-permute-start.14 = (bf16[64,2176]{1,0:T(8,128)(2,1)S(1)}, bf16[64,2176]{1,0:T(8,128)(2,1)S(1)}, u32[]{:S(2)}, u32[]{:S(2)}) collective-permute-start(bf16[64,2176]{1,0:T(8,128)(2,1)S(1)} %get-tuple-element.78), channel_id=1, source_target_pairs={{0,2},{1,3},{2,0},{3,1},{4,6},{5,7},{6,4},{7,5},{8,10},{9,11},{10,... | collective-permute-start | bytes 835592 | tf_op jit(solution)/shard_map/ppermute | solution.py:103
  68.6 11.7 %collective-permute-start.13 = (bf16[64,2176]{1,0:T(8,128)(2,1)S(1)}, bf16[64,2176]{1,0:T(8,128)(2,1)S(1)}, u32[]{:S(2)}, u32[]{:S(2)}) collective-permute-start(bf16[64,2176]{1,0:T(8,128)(2,1)S(1)} %add_convert_fusion), channel_id=1, source_target_pairs={{0,4},{4,0},{8,12},{12,8},{1,5},{5,1},{9,13},{13,9},{2,6},{6,2},{1... | collective-permute-start | bytes 835592 | tf_op jit(solution)/shard_map/ppermute | solution.py:99
  70.1 9.0 %collective-permute-start.15 = (bf16[32,2048]{1,0:T(8,128)(2,1)S(1)}, bf16[32,2048]{1,0:T(8,128)(2,1)S(1)}, u32[]{:S(2)}, u32[]{:S(2)}) collective-permute-start(bf16[32,2048]{1,0:T(8,128)(2,1)S(1)} %slice.91), channel_id=1, source_target_pairs={{0,8},{4,12},{8,0},{12,4},{1,9},{5,13},{9,1},{13,5},{2,10},{6,14},... | collective-permute-start | bytes 393224 | tf_op jit(solution)/shard_map/ppermute | solution.py:99
  80.4 9.0 %collective-permute-start.17 = (bf16[32,2176]{1,0:T(8,128)(2,1)S(1)}, bf16[32,2176]{1,0:T(8,128)(2,1)S(1)}, u32[]{:S(2)}, u32[]{:S(2)}) collective-permute-start(bf16[32,2176]{1,0:T(8,128)(2,1)S(1)} %slice.89), channel_id=1, source_target_pairs={{0,8},{4,12},{8,0},{12,4},{1,9},{5,13},{9,1},{13,5},{2,10},{6,14},... | collective-permute-start | bytes 417800 | tf_op jit(solution)/shard_map/ppermute | solution.py:99
  83.4 6.8 %copy-start.4 = (s32[32,8]{0,1:T(8,128)S(1)}, s32[32,8]{0,1:T(8,128)}, u32[]{:S(2)}) copy-start(s32[32,8]{0,1:T(8,128)} %param.10) | copy-start | bytes 3076

commit v5 on v4

--- a/solution.py
+++ b/solution.py
@@ -1,3 +1,5 @@
+import functools
+
 import jax
 import jax.numpy as jnp
 from jax import lax
@@ -133,6 +135,35 @@
         count = piece.shape[0]
         rows[pl.ds(start, count), :] = piece[...]
         start += count
+
+
+def payload_kernel(experts, tokens, ids, pos, weights, out):
+    picks, count = ids.shape
+    expert = lax.broadcasted_iota(jnp.int32, (experts, count), 0)
+    weight = jnp.zeros((experts, count), jnp.float32)
+    for k in range(picks):
+        row = pl.ds(k, 1)
+        weight += jnp.where((ids[row, :] == expert) & (pos[row, :] >= 0), weights[row, :], 0.0)
+    high = weight.astype(jnp.bfloat16)
+    low = (weight - high.astype(jnp.float32)).astype(jnp.bfloat16)
+    both = jnp.concatenate([high, low], axis=0)
+    width = tokens.shape[1]
+    spot = (both.shape[0], out.shape[1] - width)
+    same = lax.broadcasted_iota(jnp.int32, spot, 0) == lax.broadcasted_iota(jnp.int32, spot, 1)
+    routed = dot_first(both, same.astype(jnp.float32).astype(jnp.bfloat16))
+    out[:, :width] = tokens[...]
+    out[:, width:] = routed.astype(jnp.bfloat16)
+
+
+def payload(tokens, ids, pos, weights, experts, side):
+    rows, width = tokens.shape
+    return pl.pallas_call(
+        functools.partial(payload_kernel, experts),
+        in_specs=[IN_VMEM] * 4,
+        out_specs=IN_VMEM,
+        out_shape=jax.ShapeDtypeStruct((rows, width + side), tokens.dtype),
+        name="payload",
+    )(tokens, ids.T, pos.T, weights.T)
 
 
 def bring(sources, held, sems, order):
@@ -179,7 +210,7 @@
 
 def backward_kernel(collect, *refs):
     pieces, refs = refs[:6], refs[6:]
-    weights_a, weights_b, gate_in, up_in, mask, out, product_out, rows, gate_grad, up_grad, product, held_a, held_b, sems = refs
+    weights_a, weights_b, gate_in, up_in, mask, weighted, out, product_out, rows, share, gate_grad, up_grad, product, held_a, held_b, sems = refs
     held = (held_a, held_b)
     order = [(0, 2), (1, 2), (0, 0), (1, 0), (0, 1), (1, 1)]
     copies = bring((weights_a, weights_b), held, sems, order)
@@ -200,6 +231,9 @@
         gate_grad[:, columns] = (hidden_grad * up_pre * slope).astype(jnp.bfloat16)
         up_grad[:, columns] = (hidden_grad * gate_sig).astype(jnp.bfloat16)
     product_out[...] = dot_plain(product[...].astype(jnp.bfloat16), collect[...]).astype(jnp.bfloat16)
+    for at in range(0, half_rows, UNIT_TILE):
+        part = dot_first(weighted[:, pl.ds(half_rows + at, UNIT_TILE)], rows[...])
+        share[pl.ds(at, UNIT_TILE), :] = part.astype(jnp.bfloat16)
     for half, slot in order[2:]:
         copies[half, slot].wait()
     for at in range(0, features, WIDTH_TILE):
@@ -282,7 +316,7 @@
     return products(forward_kernel, "forward_products", spread, pieces, weights, [], out_shape, scratch)
 
 
-def backward(collect, pieces, weights, gate_pre, up_pre, mask):
+def backward(collect, pieces, weights, *saved):
     half, features = weights[0].shape[1:]
     rows = sum(piece.shape[0] for piece in pieces)
     shape = jax.ShapeDtypeStruct
@@ -290,9 +324,9 @@
         shape((rows, features), jnp.bfloat16),
         shape((rows, collect.shape[1]), jnp.bfloat16),
         shape((rows, features), jnp.bfloat16),
+        shape((half, features), jnp.bfloat16),
     ]
     scratch = [pltpu.VMEM((rows, 2 * half), jnp.bfloat16)] * 2 + [pltpu.VMEM((rows, UNIT_TILE), jnp.float32)]
-    saved = [gate_pre, up_pre, mask]
     return products(backward_kernel, "backward_products", collect, pieces, weights, saved, out_shape, scratch)
 
 
@@ -329,18 +363,14 @@
     first_expert = lax.axis_index("expert") * local_experts
     unit_rows = units * local_experts
     picked = (expert_ids[:, :, None] == jnp.arange(experts, dtype=jnp.int32)) & (slot_pos >= 0)[:, :, None]
-    weight = jnp.sum(jnp.where(picked, combine_weight[:, :, None], 0.0), axis=1)
-    high = lax.reduce_precision(weight, 8, 7)
     side = -(-2 * experts // 128) * 128
-    routed = jnp.concatenate([high, weight - high], axis=1).astype(jnp.bfloat16)
-    routed = jnp.pad(routed, ((0, 0), (0, side - 2 * experts)))
     unit_expert = first_expert + jnp.arange(UNIT_TILE, dtype=jnp.int32) % local_experts
     columns = jnp.arange(side, dtype=jnp.int32)
     spread = (columns[:, None] % experts == unit_expert[None, :]) & (columns < 2 * experts)[:, None]
     collect = (unit_expert[:, None] == columns[None, :]).astype(jnp.bfloat16)
     spread = spread.astype(jnp.bfloat16)
 
-    own_t = jnp.concatenate([tokens, routed], axis=1)
+    own_t = payload(tokens, expert_ids, slot_pos, combine_weight, experts, side)
     own_t, own_g, w_gate = lax.optimization_barrier((own_t, out_grad, w_gate))
     column_t = [over_z(own_t, bit) for bit in (2, 1, 3)]
     own_gx = over_dp(own_g, 2)
@@ -362,22 +392,21 @@
     pair, block = half // 2, half // 4
     out_x = over_dp(out_part[half:], 2)
     grad_pieces = [out_grad, *column_g, own_gx, away_gx]
-    grad_part, product_part, grad_rows = backward(collect, grad_pieces, weights, gate_pre, up_pre, mask)
-    weighted_b = weighted[:, unit_rows:]
-    grad_part, product_part, out_x, weighted_b = lax.optimization_barrier((grad_part, product_part, out_x, weighted_b))
+    saved = (gate_pre, up_pre, mask, weighted)
+    grad_part, product_part, grad_rows, share_b = backward(collect, grad_pieces, weights, *saved)
+    grad_part, product_part, out_x, share_b = lax.optimization_barrier((grad_part, product_part, out_x, share_b))
 
     grad_part = jnp.concatenate([grad_part, product_part], axis=1)
     near_x = over_dp(grad_part[half + pair :], 2)
     out_sum = add(out_part[:half], out_x)
     out_near = over_z(narrow(out_sum[pair:]), 1)
-    share_b = narrow(dot_first(weighted_b, grad_rows))
-    near_x, out_near, share_b = lax.optimization_barrier((near_x, out_near, share_b))
+    other_share = over_dp(share_b, 1)
+    near_x, out_near = lax.optimization_barrier((near_x, out_near))
 
     grad_near = over_z(narrow(add(grad_part[pair:half], near_x)), 1)
     pair_x = over_dp(grad_part[half : half + pair], 2)
     out_sum = add(out_sum[:pair], out_near)
     out_far = over_z(narrow(out_sum[block:]), 2)
-    other_share = over_dp(share_b, 1)
     grad_near, pair_x, out_far, other_share = lax.optimization_barrier((grad_near, pair_x, out_far, other_share))
 
     sums = add(add(grad_part[:pair], pair_x), grad_near)
@@ -397,7 +426,7 @@
     slots = tokens.shape[0] * expert_ids.shape[1] // lax.axis_size("expert")
     unit_rows = w_gate.shape[0] * w_gate.shape[1]
     tiled = w_gate.shape[0] % 64 == 0 and unit_rows % UNIT_TILE == 0 and UNIT_TILE % w_gate.shape[1] == 0
-    tiled = tiled and w_gate.shape[2] % WIDTH_TILE == 0 and tokens.shape[0] % 32 == 0
+    tiled = tiled and w_gate.shape[1] % 2 == 0 and w_gate.shape[2] % WIDTH_TILE == 0 and tokens.shape[0] % 32 == 0
     four = lax.axis_size("expert") == 4 and lax.axis_size("dp") == 4
     if tokens.shape[0] < slots and tiled and four:
         return local_tokens(*args)

time: 91.1 us -> 88.8 us (0.975)
  other arithmetic: 4.39 us -> 1.95 us
  Pallas kernels: 25.8 us -> 27.5 us
  matrix products: 1.01 us -> 0 us
    pallas_call x0 -> x1, Pallas kernels: none -> 1.77 us  [payload(): pl.pallas_call(functools.partial(payload_kernel, experts), in_specs=[IN_V...]
    ppermute x8, starting transfers between devices: 6.64 us -> 5.08 us  [over_dp(): lax.ppermute(rows, 'dp', [(i, i ^ bit) for i in range(lax.axis_size('dp'))])]
    ppermute x10, starting transfers between devices: 17.5 us -> 18.8 us  [over_z(): lax.ppermute(rows, 'expert', [(i, i ^ bit) for i in range(lax.axis_size('...]
    ppermute x8, waiting for transfers between devices: 8.14 us -> 7 us  [over_dp(): lax.ppermute(rows, 'dp', [(i, i ^ bit) for i in range(lax.axis_size('dp'))])]
    dot_general x1 -> x0, matrix products: 1.01 us -> none  [dot_first(): lax.dot_general(a, b, (((0,), (0,)), ((), ())), preferred_element_type=jn...]
    concatenate x2 -> x0, other arithmetic: 1 us -> none  [the longest x1 0.92 us: local_tokens(): own_t = jnp.concatenate([tokens, routed], axis=1)]
    unnamed x11 -> x15, local copies, waits for them, and re-layouts: 5.78 us -> 6.08 us
  transfers between devices with their start and end apart: 18 -> 18, of which waited for: 11 -> 11; matrix products, arithmetic and copies ran while one was open for 2% -> 2% of each run, Pallas kernels for 28% -> 29%
where the time goes in v5:
time: 88.8 us; the launch traced here: 88.5 us
  Pallas kernels  27.5 us (31%)
  waiting for transfers between devices  27.4 us (31%)
  starting transfers between devices  23.9 us (27%)
  local copies, waits for them, and re-layouts  6.99 us (8%)
  other arithmetic  1.95 us (2%)
    ppermute x10, waiting for transfers between devices, over_z(): lax.ppermute(rows, 'expert', [(i, i ^ bit) for i in range(lax.axis_size('...  20.4 us
    ppermute x10, starting transfers between devices, over_z(): lax.ppermute(rows, 'expert', [(i, i ^ bit) for i in range(lax.axis_size('...  18.8 us
    pallas_call x2, Pallas kernels, products(): pl.pallas_call(kernel, in_specs=[IN_VMEM] * (1 + len(pieces)) + [pl.Block...  18.3 us
    ppermute x8, waiting for transfers between devices, over_dp(): lax.ppermute(rows, 'dp', [(i, i ^ bit) for i in range(lax.axis_size('dp'))])  7 us
    unnamed x15, local copies, waits for them, and re-layouts  6.08 us
    ppermute x8, starting transfers between devices, over_dp(): lax.ppermute(rows, 'dp', [(i, i ^ bit) for i in range(lax.axis_size('dp'))])  5.08 us
    pallas_call x1, Pallas kernels, merge_units(): pl.pallas_call(merge_kernel, grid=(units // tile,), in_specs=[block] * 3,...  4.55 us
    pallas_call x1, Pallas kernels, finish_share(): pl.pallas_call(share_kernel, grid=(units // tile,), in_specs=[pl.BlockSpe...  2.91 us
  transfers between devices with their start and end apart: 18, of which 11 were waited for; matrix products, arithmetic and copies ran while one was open for 2% of the time, Pallas kernels for 29%

profile of v5, /device:TPU:0, one launch (start us, length us, event | category | flops | bytes accessed | tf_op | source)
XLA Modules:
  0.0 88.5 jit_solution(15400872184416424524)
XLA Ops:
  0.6 1.8 %payload.1.refs_0_ = bf16[32,2176]{1,0:T(8,128)(2,1)} custom-call(bf16[32,2048]{1,0:T(8,128)(2,1)} %tokens.1, s32[8,32]{1,0:T(8,128)} %bitcast.3, s32[8,32]{1,0:T(8,128)} %bitcast.4, f32[8,32]{1,0:T(8,128)} %bitcast.5), custom_call_target="tpu_custom_call" | custom-call | tf_op jit(solution)/shard_map/payload/pallas_call | solution.py:160
  2.4 4.0 %collective-permute-start = (bf16[32,2176]{1,0:T(8,128)(2,1)}, bf16[32,2176]{1,0:T(8,128)(2,1)S(1)}, u32[]{:S(2)}, u32[]{:S(2)}) collective-permute-start(bf16[32,2176]{1,0:T(8,128)(2,1)} %payload.1.refs_0_), channel_id=1, source_target_pairs={{0,8},{4,12},{8,0},{12,4},{1,9},{5,13},{9,1},{13,5},{2,10},{6,14},... | collective-permute-start | bytes 417800 | tf_op jit(solution)/shard_map/ppermute | solution.py:101
  6.4 1.6 %collective-permute-start.1 = (bf16[32,2176]{1,0:T(8,128)(2,1)}, bf16[32,2176]{1,0:T(8,128)(2,1)S(1)}, u32[]{:S(2)}, u32[]{:S(2)}) collective-permute-start(bf16[32,2176]{1,0:T(8,128)(2,1)} %payload.1.refs_0_), channel_id=1, source_target_pairs={{0,4},{4,0},{8,12},{12,8},{1,5},{5,1},{9,13},{13,9},{2,6},{6,2},{1... | collective-permute-start | bytes 417800 | tf_op jit(solution)/shard_map/ppermute | solution.py:101
  8.0 1.7 %collective-permute-start.3 = (bf16[32,2048]{1,0:T(8,128)(2,1)}, bf16[32,2048]{1,0:T(8,128)(2,1)S(1)}, u32[]{:S(2)}, u32[]{:S(2)}) collective-permute-start(bf16[32,2048]{1,0:T(8,128)(2,1)} %refs_0_.1), channel_id=1, source_target_pairs={{0,2},{1,3},{2,0},{3,1},{4,6},{5,7},{6,4},{7,5},{8,10},{9,11},{10,... | collective-permute-start | bytes 393224 | tf_op jit(solution)/shard_map/ppermute | solution.py:105
  9.7 1.9 %copy-done = bf16[192,4,2048]{2,1,0:T(4,128)(2,1)S(1)} copy-done((bf16[192,4,2048]{2,1,0:T(4,128)(2,1)S(1)}, bf16[192,4,2048]{2,1,0:T(4,128)(2,1)}, u32[]{:S(2)}) %copy-start) | copy-done | bytes 3145752
  11.6 1.9 %copy-done.1 = bf16[192,4,2048]{2,1,0:T(4,128)(2,1)S(1)} copy-done((bf16[192,4,2048]{2,1,0:T(4,128)(2,1)S(1)}, bf16[192,4,2048]{2,1,0:T(4,128)(2,1)}, u32[]{:S(2)}) %copy-start.1) | copy-done | bytes 3145752
  13.5 1.9 %copy-done.2 = bf16[192,4,2048]{2,1,0:T(4,128)(2,1)S(1)} copy-done((bf16[192,4,2048]{2,1,0:T(4,128)(2,1)S(1)}, bf16[192,4,2048]{2,1,0:T(4,128)(2,1)}, u32[]{:S(2)}) %copy-start.2) | copy-done | bytes 3145752
  15.4 4.5 %merge_units.1.refs_5_.refs_6_ = bf16[3,768,2048]{2,1,0:T(8,128)(2,1)} custom-call(bf16[192,4,2048]{2,1,0:T(4,128)(2,1)S(1)} %copy-done, bf16[192,4,2048]{2,1,0:T(4,128)(2,1)S(1)} %copy-done.1, bf16[192,4,2048]{2,1,0:T(4,128)(2,1)S(1)} %copy-done.2), custom_call_target="tpu_custom_call" | custom-call | bytes 18874368 | tf_op jit(solution)/shard_map/merge_units/pallas_call | solution.py:257
  20.9 2.8 %collective-permute-start.4 = (bf16[32,2048]{1,0:T(8,128)(2,1)S(1)}, bf16[32,2048]{1,0:T(8,128)(2,1)S(1)}, u32[]{:S(2)}, u32[]{:S(2)}) collective-permute-start(bf16[32,2048]{1,0:T(8,128)(2,1)S(1)} %copy-done.4), channel_id=1, source_target_pairs={{0,8},{4,12},{8,0},{12,4},{1,9},{5,13},{9,1},{13,5},{2,10},{6,14},... | collective-permute-start | bytes 393224 | tf_op jit(solution)/shard_map/ppermute | solution.py:101
  25.4 5.8 %collective-permute-done.4.refs_1_ = bf16[32,2048]{1,0:T(8,128)(2,1)S(1)} collective-permute-done((bf16[32,2048]{1,0:T(8,128)(2,1)S(1)}, bf16[32,2048]{1,0:T(8,128)(2,1)S(1)}, u32[]{:S(2)}, u32[]{:S(2)}) %collective-permute-start.4) | collective-permute-done | bytes 131104 | tf_op jit(solution)/shard_map/ppermute | solution.py:101
  31.1 2.9 %collective-permute-done.6.refs_3_ = bf16[32,2048]{1,0:T(8,128)(2,1)S(1)} collective-permute-done((bf16[32,2048]{1,0:T(8,128)(2,1)S(1)}, bf16[32,2048]{1,0:T(8,128)(2,1)S(1)}, u32[]{:S(2)}, u32[]{:S(2)}) %collective-permute-start.6) | collective-permute-done | bytes 131104 | tf_op jit(solution)/shard_map/ppermute | solution.py:101
  35.6 8.4 %forward_products.1 = (bf16[256,2048]{1,0:T(8,128)(2,1)S(1)}, f32[256,1536]{1,0:T(8,128)S(1)}, f32[256,1536]{1,0:T(8,128)S(1)}, f32[256,256]{1,0:T(8,128)S(1)}, bf16[256,1536]{1,0:T(8,128)(2,1)S(1)}) custom-call(bf16[128,256]{1,0:T(8,128)(2,1)S(1)} %and_convert_fusion.spread, bf16[32,2176]{1,0:T(8,128)(2,1)S(1)} %copy-done.3, ...), custom_call_target="tpu_custom_call" | custom-call | flops 4831838208 | bytes 20971520 | tf_op jit(solution)/shard_map/forward_products/pallas_call | solution.py:289
  44.0 2.0 %collective-permute-done.9.refs_5_ = bf16[96,2048]{1,0:T(8,128)(2,1)S(1)} collective-permute-done((bf16[96,2048]{1,0:T(8,128)(2,1)S(1)}, bf16[96,2048]{1,0:T(8,128)(2,1)S(1)}, u32[]{:S(2)}, u32[]{:S(2)}) %collective-permute-start.9) | collective-permute-done | bytes 393248 | tf_op jit(solution)/shard_map/ppermute | solution.py:105
  46.5 9.9 %backward_products.1 = (bf16[256,2048]{1,0:T(8,128)(2,1)S(1)}, bf16[256,128]{1,0:T(8,128)(2,1)S(1)}, bf16[256,2048]{1,0:T(8,128)(2,1)S(1)}, bf16[768,2048]{1,0:T(8,128)(2,1)S(1)}) custom-call(bf16[256,128]{1,0:T(8,128)(2,1)S(1)} %fusion.1.collect, bf16[32,2048]{1,0:T(8,128)(2,1)S(1)} %copy-done.4, bf16[32,2048]{1,0:T(8,128)(2,1)S(1)} %collective-permute-done.4.refs_1_, ...), custom_call_target="tpu_custom_call" | custom-call | flops 4831838208 | bytes 20971520 | tf_op jit(solution)/shard_map/backward_products/pallas_call | solution.py:289
  56.5 2.3 %collective-permute-done.10 = bf16[128,2048]{1,0:T(8,128)(2,1)S(1)} collective-permute-done((bf16[128,2048]{1,0:T(8,128)(2,1)S(1)}, bf16[128,2048]{1,0:T(8,128)(2,1)S(1)}, u32[]{:S(2)}, u32[]{:S(2)}) %collective-permute-start.10) | collective-permute-done | bytes 524320 | tf_op jit(solution)/shard_map/ppermute | solution.py:105
  59.5 1.8 %collective-permute-start.12 = (bf16[64,2048]{1,0:T(8,128)(2,1)S(1)}, bf16[64,2048]{1,0:T(8,128)(2,1)S(1)}, u32[]{:S(2)}, u32[]{:S(2)}) collective-permute-start(bf16[64,2048]{1,0:T(8,128)(2,1)S(1)} %slice.84), channel_id=1, source_target_pairs={{0,4},{4,0},{8,12},{12,8},{1,5},{5,1},{9,13},{13,9},{2,6},{6,2},{1... | collective-permute-start | bytes 786440 | tf_op jit(solution)/shard_map/ppermute | solution.py:101
  61.3 1.7 %collective-permute-start.14 = (bf16[64,2176]{1,0:T(8,128)(2,1)S(1)}, bf16[64,2176]{1,0:T(8,128)(2,1)S(1)}, u32[]{:S(2)}, u32[]{:S(2)}) collective-permute-start(bf16[64,2176]{1,0:T(8,128)(2,1)S(1)} %get-tuple-element.78), channel_id=1, source_target_pairs={{0,2},{1,3},{2,0},{3,1},{4,6},{5,7},{6,4},{7,5},{8,10},{9,11},{10,... | collective-permute-start | bytes 835592 | tf_op jit(solution)/shard_map/ppermute | solution.py:105
  63.0 5.0 %collective-permute-done.12 = bf16[64,2048]{1,0:T(8,128)(2,1)S(1)} collective-permute-done((bf16[64,2048]{1,0:T(8,128)(2,1)S(1)}, bf16[64,2048]{1,0:T(8,128)(2,1)S(1)}, u32[]{:S(2)}, u32[]{:S(2)}) %collective-permute-start.12) | collective-permute-done | bytes 262176 | tf_op jit(solution)/shard_map/ppermute | solution.py:101
  68.5 1.8 %collective-permute-start.13 = (bf16[64,2176]{1,0:T(8,128)(2,1)S(1)}, bf16[64,2176]{1,0:T(8,128)(2,1)S(1)}, u32[]{:S(2)}, u32[]{:S(2)}) collective-permute-start(bf16[64,2176]{1,0:T(8,128)(2,1)S(1)} %add_convert_fusion), channel_id=1, source_target_pairs={{0,4},{4,0},{8,12},{12,8},{1,5},{5,1},{9,13},{13,9},{2,6},{6,2},{1... | collective-permute-start | bytes 835592 | tf_op jit(solution)/shard_map/ppermute | solution.py:101
  70.4 2.5 %collective-permute-start.15 = (bf16[32,2048]{1,0:T(8,128)(2,1)S(1)}, bf16[32,2048]{1,0:T(8,128)(2,1)S(1)}, u32[]{:S(2)}, u32[]{:S(2)}) collective-permute-start(bf16[32,2048]{1,0:T(8,128)(2,1)S(1)} %slice.87), channel_id=1, source_target_pairs={{0,8},{4,12},{8,0},{12,4},{1,9},{5,13},{9,1},{13,5},{2,10},{6,14},... | collective-permute-start | bytes 393224 | tf_op jit(solution)/shard_map/ppermute | solution.py:101
  74.0 4.5 %collective-permute-done.15 = bf16[32,2048]{1,0:T(8,128)(2,1)S(1)} collective-permute-done((bf16[32,2048]{1,0:T(8,128)(2,1)S(1)}, bf16[32,2048]{1,0:T(8,128)(2,1)S(1)}, u32[]{:S(2)}, u32[]{:S(2)}) %collective-permute-start.15) | collective-permute-done | bytes 131104 | tf_op jit(solution)/shard_map/ppermute | solution.py:101
  79.4 2.7 %collective-permute-start.17 = (bf16[32,2176]{1,0:T(8,128)(2,1)S(1)}, bf16[32,2176]{1,0:T(8,128)(2,1)S(1)}, u32[]{:S(2)}, u32[]{:S(2)}) collective-permute-start(bf16[32,2176]{1,0:T(8,128)(2,1)S(1)} %slice.85), channel_id=1, source_target_pairs={{0,8},{4,12},{8,0},{12,4},{1,9},{5,13},{9,1},{13,5},{2,10},{6,14},... | collective-permute-start | bytes 417800 | tf_op jit(solution)/shard_map/ppermute | solution.py:101
  82.8 2.9 %finish_share.1 = bf16[192,4,2048]{2,1,0:T(4,128)(2,1)} custom-call(bf16[256,1536]{1,0:T(8,128)(2,1)S(1)} %get-tuple-element.59.refs_11_.weighted, bf16[256,2048]{1,0:T(8,128)(2,1)S(1)} %get-tuple-element.72.rows, bf16[768,2048]{1,0:T(8,128)(2,1)S(1)} %collective-permute-done.16.other), custom_call_target="tpu_custom_call" | custom-call | flops 805306368 | bytes 6291456 | tf_op jit(solution)/shard_map/finish_share/pallas_call | solution.py:342
  85.7 1.4 %collective-permute-done.17 = bf16[32,2176]{1,0:T(8,128)(2,1)S(1)} collective-permute-done((bf16[32,2176]{1,0:T(8,128)(2,1)S(1)}, bf16[32,2176]{1,0:T(8,128)(2,1)S(1)}, u32[]{:S(2)}, u32[]{:S(2)}) %collective-permute-start.17) | collective-permute-done | bytes 139296 | tf_op jit(solution)/shard_map/ppermute | solution.py:101
  (56 shorter events, 10.0 us)
Async XLA Ops:
  2.4 17.6 %collective-permute-start = (bf16[32,2176]{1,0:T(8,128)(2,1)}, bf16[32,2176]{1,0:T(8,128)(2,1)S(1)}, u32[]{:S(2)}, u32[]{:S(2)}) collective-permute-start(bf16[32,2176]{1,0:T(8,128)(2,1)} %payload.1.refs_0_), channel_id=1, source_target_pairs={{0,8},{4,12},{8,0},{12,4},{1,9},{5,13},{9,1},{13,5},{2,10},{6,14},... | collective-permute-start | bytes 417800 | tf_op jit(solution)/shard_map/ppermute | solution.py:101
  6.4 13.5 %collective-permute-start.1 = (bf16[32,2176]{1,0:T(8,128)(2,1)}, bf16[32,2176]{1,0:T(8,128)(2,1)S(1)}, u32[]{:S(2)}, u32[]{:S(2)}) collective-permute-start(bf16[32,2176]{1,0:T(8,128)(2,1)} %payload.1.refs_0_), channel_id=1, source_target_pairs={{0,4},{4,0},{8,12},{12,8},{1,5},{5,1},{9,13},{13,9},{2,6},{6,2},{1... | collective-permute-start | bytes 417800 | tf_op jit(solution)/shard_map/ppermute | solution.py:101
  8.0 12.0 %collective-permute-start.2 = (bf16[32,2176]{1,0:T(8,128)(2,1)}, bf16[32,2176]{1,0:T(8,128)(2,1)S(1)}, u32[]{:S(2)}, u32[]{:S(2)}) collective-permute-start(bf16[32,2176]{1,0:T(8,128)(2,1)} %payload.1.refs_0_), channel_id=1, source_target_pairs={{0,12},{4,8},{8,4},{12,0},{1,13},{5,9},{9,5},{13,1},{2,14},{6,10},... | collective-permute-start | bytes 417800 | tf_op jit(solution)/shard_map/ppermute | solution.py:101
  8.0 11.9 %collective-permute-start.3 = (bf16[32,2048]{1,0:T(8,128)(2,1)}, bf16[32,2048]{1,0:T(8,128)(2,1)S(1)}, u32[]{:S(2)}, u32[]{:S(2)}) collective-permute-start(bf16[32,2048]{1,0:T(8,128)(2,1)} %refs_0_.1), channel_id=1, source_target_pairs={{0,2},{1,3},{2,0},{3,1},{4,6},{5,7},{6,4},{7,5},{8,10},{9,11},{10,... | collective-permute-start | bytes 393224 | tf_op jit(solution)/shard_map/ppermute | solution.py:105
  9.7 1.9 %copy-start = (bf16[192,4,2048]{2,1,0:T(4,128)(2,1)S(1)}, bf16[192,4,2048]{2,1,0:T(4,128)(2,1)}, u32[]{:S(2)}) copy-start(bf16[192,4,2048]{2,1,0:T(4,128)(2,1)} %gate) | copy-start | bytes 9437188
  11.6 1.9 %copy-start.1 = (bf16[192,4,2048]{2,1,0:T(4,128)(2,1)S(1)}, bf16[192,4,2048]{2,1,0:T(4,128)(2,1)}, u32[]{:S(2)}) copy-start(bf16[192,4,2048]{2,1,0:T(4,128)(2,1)} %up.1) | copy-start | bytes 9437188
  13.5 1.9 %copy-start.2 = (bf16[192,4,2048]{2,1,0:T(4,128)(2,1)S(1)}, bf16[192,4,2048]{2,1,0:T(4,128)(2,1)}, u32[]{:S(2)}) copy-start(bf16[192,4,2048]{2,1,0:T(4,128)(2,1)} %down.1) | copy-start | bytes 9437188
  15.4 4.7 %copy-start.3 = (bf16[32,2176]{1,0:T(8,128)(2,1)S(1)}, bf16[32,2176]{1,0:T(8,128)(2,1)}, u32[]{:S(2)}) copy-start(bf16[32,2176]{1,0:T(8,128)(2,1)} %payload.1.refs_0_) | copy-start | bytes 417796
  20.0 15.7 %collective-permute-start.8 = (bf16[3,768,2048]{2,1,0:T(8,128)(2,1)}, bf16[3,768,2048]{2,1,0:T(8,128)(2,1)}, u32[]{:S(2)}, u32[]{:S(2)}) collective-permute-start(bf16[3,768,2048]{2,1,0:T(8,128)(2,1)} %merge_units.1.refs_5_.refs_6_), channel_id=1, source_target_pairs={{0,1},{1,0},{2,3},{3,2},{4,5},{5,4},{6,7},{7,6},{8,9},{9,8},{10,11... | collective-permute-start | bytes 28311560 | tf_op jit(solution)/shard_map/ppermute | solution.py:105
  20.1 15.1 %collective-permute-start.7 = (bf16[128,2176]{1,0:T(8,128)(2,1)S(1)}, bf16[128,2176]{1,0:T(8,128)(2,1)S(1)}, u32[]{:S(2)}, u32[]{:S(2)}) collective-permute-start(bf16[128,2176]{1,0:T(8,128)(2,1)S(1)} %pad_maximum_fusion), channel_id=1, source_target_pairs={{0,2},{1,3},{2,0},{3,1},{4,6},{5,7},{6,4},{7,5},{8,10},{9,11},{10,... | collective-permute-start | bytes 1671176 | tf_op jit(solution)/shard_map/ppermute | solution.py:105
  20.9 10.3 %collective-permute-start.4 = (bf16[32,2048]{1,0:T(8,128)(2,1)S(1)}, bf16[32,2048]{1,0:T(8,128)(2,1)S(1)}, u32[]{:S(2)}, u32[]{:S(2)}) collective-permute-start(bf16[32,2048]{1,0:T(8,128)(2,1)S(1)} %copy-done.4), channel_id=1, source_target_pairs={{0,8},{4,12},{8,0},{12,4},{1,9},{5,13},{9,1},{13,5},{2,10},{6,14},... | collective-permute-start | bytes 393224 | tf_op jit(solution)/shard_map/ppermute | solution.py:101
  23.6 7.5 %collective-permute-start.5 = (bf16[32,2048]{1,0:T(8,128)(2,1)S(1)}, bf16[32,2048]{1,0:T(8,128)(2,1)S(1)}, u32[]{:S(2)}, u32[]{:S(2)}) collective-permute-start(bf16[32,2048]{1,0:T(8,128)(2,1)S(1)} %copy-done.4), channel_id=1, source_target_pairs={{0,4},{4,0},{8,12},{12,8},{1,5},{5,1},{9,13},{13,9},{2,6},{6,2},{1... | collective-permute-start | bytes 393224 | tf_op jit(solution)/shard_map/ppermute | solution.py:101
  25.0 9.0 %collective-permute-start.6 = (bf16[32,2048]{1,0:T(8,128)(2,1)S(1)}, bf16[32,2048]{1,0:T(8,128)(2,1)S(1)}, u32[]{:S(2)}, u32[]{:S(2)}) collective-permute-start(bf16[32,2048]{1,0:T(8,128)(2,1)S(1)} %copy-done.4), channel_id=1, source_target_pairs={{0,12},{4,8},{8,4},{12,0},{1,13},{5,9},{9,5},{13,1},{2,14},{6,10},... | collective-permute-start | bytes 393224 | tf_op jit(solution)/shard_map/ppermute | solution.py:101
  35.2 10.8 %collective-permute-start.9 = (bf16[96,2048]{1,0:T(8,128)(2,1)S(1)}, bf16[96,2048]{1,0:T(8,128)(2,1)S(1)}, u32[]{:S(2)}, u32[]{:S(2)}) collective-permute-start(bf16[96,2048]{1,0:T(8,128)(2,1)S(1)} %pad_maximum_fusion.1), channel_id=1, source_target_pairs={{0,2},{1,3},{2,0},{3,1},{4,6},{5,7},{6,4},{7,5},{8,10},{9,11},{10,... | collective-permute-start | bytes 1179656 | tf_op jit(solution)/shard_map/ppermute | solution.py:105
  46.1 12.7 %collective-permute-start.10 = (bf16[128,2048]{1,0:T(8,128)(2,1)S(1)}, bf16[128,2048]{1,0:T(8,128)(2,1)S(1)}, u32[]{:S(2)}, u32[]{:S(2)}) collective-permute-start(bf16[128,2048]{1,0:T(8,128)(2,1)S(1)} %slice.46), channel_id=1, source_target_pairs={{0,2},{1,3},{2,0},{3,1},{4,6},{5,7},{6,4},{7,5},{8,10},{9,11},{10,... | collective-permute-start | bytes 1572872 | tf_op jit(solution)/shard_map/ppermute | solution.py:105
  58.8 20.5 %collective-permute-start.16 = (bf16[768,2048]{1,0:T(8,128)(2,1)S(1)}, bf16[768,2048]{1,0:T(8,128)(2,1)S(1)}, u32[]{:S(2)}, u32[]{:S(2)}) collective-permute-start(bf16[768,2048]{1,0:T(8,128)(2,1)S(1)} %get-tuple-element.69), channel_id=1, source_target_pairs={{0,1},{1,0},{2,3},{3,2},{4,5},{5,4},{6,7},{7,6},{8,9},{9,8},{10,11... | collective-permute-start | bytes 9437192 | tf_op jit(solution)/shard_map/ppermute | solution.py:105
  58.9 9.5 %collective-permute-start.11 = (bf16[64,2176]{1,0:T(8,128)(2,1)S(1)}, bf16[64,2176]{1,0:T(8,128)(2,1)S(1)}, u32[]{:S(2)}, u32[]{:S(2)}) collective-permute-start(bf16[64,2176]{1,0:T(8,128)(2,1)S(1)} %get-tuple-element.79), channel_id=1, source_target_pairs={{0,2},{1,3},{2,0},{3,1},{4,6},{5,7},{6,4},{7,5},{8,10},{9,11},{10,... | collective-permute-start | bytes 835592 | tf_op jit(solution)/shard_map/ppermute | solution.py:105
  59.5 8.5 %collective-permute-start.12 = (bf16[64,2048]{1,0:T(8,128)(2,1)S(1)}, bf16[64,2048]{1,0:T(8,128)(2,1)S(1)}, u32[]{:S(2)}, u32[]{:S(2)}) collective-permute-start(bf16[64,2048]{1,0:T(8,128)(2,1)S(1)} %slice.84), channel_id=1, source_target_pairs={{0,4},{4,0},{8,12},{12,8},{1,5},{5,1},{9,13},{13,9},{2,6},{6,2},{1... | collective-permute-start | bytes 786440 | tf_op jit(solution)/shard_map/ppermute | solution.py:101
  61.3 11.6 %copy-start.6 = (s32[32,8]{0,1:T(8,128)S(1)}, s32[32,8]{0,1:T(8,128)}, u32[]{:S(2)}) copy-start(s32[32,8]{0,1:T(8,128)} %param.11) | copy-start | bytes 3076
  61.3 12.8 %collective-permute-start.14 = (bf16[64,2176]{1,0:T(8,128)(2,1)S(1)}, bf16[64,2176]{1,0:T(8,128)(2,1)S(1)}, u32[]{:S(2)}, u32[]{:S(2)}) collective-permute-start(bf16[64,2176]{1,0:T(8,128)(2,1)S(1)} %get-tuple-element.78), channel_id=1, source_target_pairs={{0,2},{1,3},{2,0},{3,1},{4,6},{5,7},{6,4},{7,5},{8,10},{9,11},{10,... | collective-permute-start | bytes 835592 | tf_op jit(solution)/shard_map/ppermute | solution.py:105
  68.5 10.8 %collective-permute-start.13 = (bf16[64,2176]{1,0:T(8,128)(2,1)S(1)}, bf16[64,2176]{1,0:T(8,128)(2,1)S(1)}, u32[]{:S(2)}, u32[]{:S(2)}) collective-permute-start(bf16[64,2176]{1,0:T(8,128)(2,1)S(1)} %add_convert_fusion), channel_id=1, source_target_pairs={{0,4},{4,0},{8,12},{12,8},{1,5},{5,1},{9,13},{13,9},{2,6},{6,2},{1... | collective-permute-start | bytes 835592 | tf_op jit(solution)/shard_map/ppermute | solution.py:101
  70.4 8.2 %collective-permute-start.15 = (bf16[32,2048]{1,0:T(8,128)(2,1)S(1)}, bf16[32,2048]{1,0:T(8,128)(2,1)S(1)}, u32[]{:S(2)}, u32[]{:S(2)}) collective-permute-start(bf16[32,2048]{1,0:T(8,128)(2,1)S(1)} %slice.87), channel_id=1, source_target_pairs={{0,8},{4,12},{8,0},{12,4},{1,9},{5,13},{9,1},{13,5},{2,10},{6,14},... | collective-permute-start | bytes 393224 | tf_op jit(solution)/shard_map/ppermute | solution.py:101
  79.4 7.7 %collective-permute-start.17 = (bf16[32,2176]{1,0:T(8,128)(2,1)S(1)}, bf16[32,2176]{1,0:T(8,128)(2,1)S(1)}, u32[]{:S(2)}, u32[]{:S(2)}) collective-permute-start(bf16[32,2176]{1,0:T(8,128)(2,1)S(1)} %slice.85), channel_id=1, source_target_pairs={{0,8},{4,12},{8,0},{12,4},{1,9},{5,13},{9,1},{13,5},{2,10},{6,14},... | collective-permute-start | bytes 417800 | tf_op jit(solution)/shard_map/ppermute | solution.py:101
  82.8 5.1 %copy-start.5 = (s32[32,8]{0,1:T(8,128)S(1)}, s32[32,8]{0,1:T(8,128)}, u32[]{:S(2)}) copy-start(s32[32,8]{0,1:T(8,128)} %param.10) | copy-start | bytes 3076
  (1 other events, 0.9 us)

commit v6 on v5

--- a/solution.py
+++ b/solution.py
@@ -180,7 +180,7 @@
 
 
 def forward_kernel(spread, *refs):
-    pieces, (weights_a, weights_b, out, gate_out, up_out, mask, weighted, rows, held_a, held_b, sems) = refs[:5], refs[5:]
+    pieces, (weights_a, weights_b, kept, sent, gate_out, up_out, mask, weighted, rows, held_a, held_b, sems) = refs[:5], refs[5:]
     held = (held_a, held_b)
     order = [(0, 0), (0, 1), (1, 0), (1, 1), (0, 2), (1, 2)]
     copies = bring((weights_a, weights_b), held, sems, order)
@@ -205,12 +205,20 @@
         columns = pl.ds(at, WIDTH_TILE)
         total = dot_plain(weighted[:, :half_rows], held_a[2, :, columns])
         total += dot_plain(weighted[:, half_rows:], held_b[2, :, columns])
-        out[:, columns] = total.astype(jnp.bfloat16)
+        spread_out(total, (kept, sent), at, WIDTH_TILE)
+
+
+def spread_out(total, outs, at, width):
+    start = 0
+    for out in outs:
+        count = out.shape[0]
+        out[:, pl.ds(at, width)] = total[start : start + count].astype(jnp.bfloat16)
+        start += count
 
 
 def backward_kernel(collect, *refs):
     pieces, refs = refs[:6], refs[6:]
-    weights_a, weights_b, gate_in, up_in, mask, weighted, out, product_out, rows, share, gate_grad, up_grad, product, held_a, held_b, sems = refs
+    weights_a, weights_b, gate_in, up_in, mask, weighted, kept, pair_out, near_out, rows, share, gate_grad, up_grad, product, held_a, held_b, sems = refs
     held = (held_a, held_b)
     order = [(0, 2), (1, 2), (0, 0), (1, 0), (0, 1), (1, 1)]
     copies = bring((weights_a, weights_b), held, sems, order)
@@ -230,7 +238,8 @@
         slope = sig * (1.0 + gate_pre * (1.0 - sig))
         gate_grad[:, columns] = (hidden_grad * up_pre * slope).astype(jnp.bfloat16)
         up_grad[:, columns] = (hidden_grad * gate_sig).astype(jnp.bfloat16)
-    product_out[...] = dot_plain(product[...].astype(jnp.bfloat16), collect[...]).astype(jnp.bfloat16)
+    outs = (kept, pair_out, near_out)
+    spread_out(dot_plain(product[...].astype(jnp.bfloat16), collect[...]), outs, features, kept.shape[1] - features)
     for at in range(0, half_rows, UNIT_TILE):
         part = dot_first(weighted[:, pl.ds(half_rows + at, UNIT_TILE)], rows[...])
         share[pl.ds(at, UNIT_TILE), :] = part.astype(jnp.bfloat16)
@@ -242,7 +251,7 @@
         total += dot_plain(gate_grad[:, half_rows:], held_b[0, :, columns])
         total += dot_plain(up_grad[:, :half_rows], held_a[1, :, columns])
         total += dot_plain(up_grad[:, half_rows:], held_b[1, :, columns])
-        out[:, columns] = total.astype(jnp.bfloat16)
+        spread_out(total, outs, at, WIDTH_TILE)
 
 
 def merge_kernel(gate, up, down, merged):
@@ -306,7 +315,8 @@
     rows = sum(piece.shape[0] for piece in pieces)
     shape = jax.ShapeDtypeStruct
     out_shape = [
-        shape((rows, features), jnp.bfloat16),
+        shape((rows // 2, features), jnp.bfloat16),
+        shape((rows // 2, features), jnp.bfloat16),
         shape((rows, 2 * half), jnp.float32),
         shape((rows, 2 * half), jnp.float32),
         shape((rows, UNIT_TILE), jnp.float32),
@@ -321,8 +331,9 @@
     rows = sum(piece.shape[0] for piece in pieces)
     shape = jax.ShapeDtypeStruct
     out_shape = [
-        shape((rows, features), jnp.bfloat16),
-        shape((rows, collect.shape[1]), jnp.bfloat16),
+        shape((rows // 2, features + collect.shape[1]), jnp.bfloat16),
+        shape((rows // 4, features + collect.shape[1]), jnp.bfloat16),
+        shape((rows // 4, features + collect.shape[1]), jnp.bfloat16),
         shape((rows, features), jnp.bfloat16),
         shape((half, features), jnp.bfloat16),
     ]
@@ -385,31 +396,30 @@
 
     away_gx = over_dp(jnp.concatenate(column_g, axis=0), 2)
     weights = [weights, weights_b]
-    out_part, gate_pre, up_pre, mask, weighted = forward(spread, [*pieces_t, column_tx], weights)
-    out_part, away_gx = lax.optimization_barrier((out_part, away_gx))
-
-    half = out_part.shape[0] // 2
-    pair, block = half // 2, half // 4
-    out_x = over_dp(out_part[half:], 2)
+    out_kept, out_sent, gate_pre, up_pre, mask, weighted = forward(spread, [*pieces_t, column_tx], weights)
+    out_sent, away_gx = lax.optimization_barrier((out_sent, away_gx))
+
+    block = tokens.shape[0]
+    pair = 2 * block
+    out_x = over_dp(out_sent, 2)
     grad_pieces = [out_grad, *column_g, own_gx, away_gx]
     saved = (gate_pre, up_pre, mask, weighted)
-    grad_part, product_part, grad_rows, share_b = backward(collect, grad_pieces, weights, *saved)
-    grad_part, product_part, out_x, share_b = lax.optimization_barrier((grad_part, product_part, out_x, share_b))
-
-    grad_part = jnp.concatenate([grad_part, product_part], axis=1)
-    near_x = over_dp(grad_part[half + pair :], 2)
-    out_sum = add(out_part[:half], out_x)
+    kept, pair_sent, near_sent, grad_rows, share_b = backward(collect, grad_pieces, weights, *saved)
+    near_sent, out_x, share_b = lax.optimization_barrier((near_sent, out_x, share_b))
+
+    near_x = over_dp(near_sent, 2)
+    out_sum = add(out_kept, out_x)
     out_near = over_z(narrow(out_sum[pair:]), 1)
     other_share = over_dp(share_b, 1)
-    near_x, out_near = lax.optimization_barrier((near_x, out_near))
-
-    grad_near = over_z(narrow(add(grad_part[pair:half], near_x)), 1)
-    pair_x = over_dp(grad_part[half : half + pair], 2)
+    near_x, pair_sent = lax.optimization_barrier((near_x, pair_sent))
+
+    grad_near = over_z(narrow(add(kept[pair:], near_x)), 1)
+    pair_x = over_dp(pair_sent, 2)
     out_sum = add(out_sum[:pair], out_near)
     out_far = over_z(narrow(out_sum[block:]), 2)
     grad_near, pair_x, out_far, other_share = lax.optimization_barrier((grad_near, pair_x, out_far, other_share))
 
-    sums = add(add(grad_part[:pair], pair_x), grad_near)
+    sums = add(add(kept[:pair], pair_x), grad_near)
     grad_far = over_z(narrow(sums[block:]), 2)
     layer_out = narrow(add(out_sum[:block], out_far))
     down_grad = finish_share(weighted, grad_rows, other_share, local_experts)

time: 88.8 us -> 88.3 us (level)
  starting transfers between devices: 23.9 us -> 22.9 us
  waiting for transfers between devices: 27.4 us -> 28.3 us
    ppermute x8, waiting for transfers between devices: 7 us -> 12.2 us  [over_dp(): lax.ppermute(rows, 'dp', [(i, i ^ bit) for i in range(lax.axis_size('dp'))])]
    ppermute x10, waiting for transfers between devices: 20.4 us -> 16.1 us  [over_z(): lax.ppermute(rows, 'expert', [(i, i ^ bit) for i in range(lax.axis_size('...]
    ppermute x8, starting transfers between devices: 5.08 us -> 3.64 us  [over_dp(): lax.ppermute(rows, 'dp', [(i, i ^ bit) for i in range(lax.axis_size('dp'))])]
    unnamed x15 -> x14, local copies, waits for them, and re-layouts: 6.08 us -> 5.69 us
  transfers between devices with their start and end apart: 18 -> 18, of which waited for: 11 -> 10; matrix products, arithmetic and copies ran while one was open for 2% -> 1% of each run, Pallas kernels for 29% -> 29%
where the time goes in v6:
time: 88.3 us; the launch traced here: 88 us
  waiting for transfers between devices  28.3 us (32%)
  Pallas kernels  27.6 us (31%)
  starting transfers between devices  22.9 us (26%)
  local copies, waits for them, and re-layouts  6.49 us (7%)
  other arithmetic  1.95 us (2%)
    ppermute x10, starting transfers between devices, over_z(): lax.ppermute(rows, 'expert', [(i, i ^ bit) for i in range(lax.axis_size('...  19.3 us
    pallas_call x2, Pallas kernels, products(): pl.pallas_call(kernel, in_specs=[IN_VMEM] * (1 + len(pieces)) + [pl.Block...  18.3 us
    ppermute x10, waiting for transfers between devices, over_z(): lax.ppermute(rows, 'expert', [(i, i ^ bit) for i in range(lax.axis_size('...  16.1 us
    ppermute x8, waiting for transfers between devices, over_dp(): lax.ppermute(rows, 'dp', [(i, i ^ bit) for i in range(lax.axis_size('dp'))])  12.2 us
    unnamed x14, local copies, waits for them, and re-layouts  5.69 us
    pallas_call x1, Pallas kernels, merge_units(): pl.pallas_call(merge_kernel, grid=(units // tile,), in_specs=[block] * 3,...  4.54 us
    ppermute x8, starting transfers between devices, over_dp(): lax.ppermute(rows, 'dp', [(i, i ^ bit) for i in range(lax.axis_size('dp'))])  3.64 us
    pallas_call x1, Pallas kernels, finish_share(): pl.pallas_call(share_kernel, grid=(units // tile,), in_specs=[pl.BlockSpe...  2.91 us
  transfers between devices with their start and end apart: 18, of which 10 were waited for; matrix products, arithmetic and copies ran while one was open for 1% of the time, Pallas kernels for 29%

profile of v6, /device:TPU:0, one launch (start us, length us, event | category | flops | bytes accessed | tf_op | source)
XLA Modules:
  0.0 88.0 jit_solution(4515779078905884264)
XLA Ops:
  0.6 1.8 %payload.1.refs_0_ = bf16[32,2176]{1,0:T(8,128)(2,1)} custom-call(bf16[32,2048]{1,0:T(8,128)(2,1)} %tokens.1, s32[8,32]{1,0:T(8,128)} %bitcast.3, s32[8,32]{1,0:T(8,128)} %bitcast.4, f32[8,32]{1,0:T(8,128)} %bitcast.5), custom_call_target="tpu_custom_call" | custom-call | tf_op jit(solution)/shard_map/payload/pallas_call | solution.py:160
  2.5 4.0 %collective-permute-start = (bf16[32,2176]{1,0:T(8,128)(2,1)}, bf16[32,2176]{1,0:T(8,128)(2,1)S(1)}, u32[]{:S(2)}, u32[]{:S(2)}) collective-permute-start(bf16[32,2176]{1,0:T(8,128)(2,1)} %payload.1.refs_0_), channel_id=1, source_target_pairs={{0,8},{4,12},{8,0},{12,4},{1,9},{5,13},{9,1},{13,5},{2,10},{6,14},... | collective-permute-start | bytes 417800 | tf_op jit(solution)/shard_map/ppermute | solution.py:101
  6.5 1.6 %collective-permute-start.1 = (bf16[32,2176]{1,0:T(8,128)(2,1)}, bf16[32,2176]{1,0:T(8,128)(2,1)S(1)}, u32[]{:S(2)}, u32[]{:S(2)}) collective-permute-start(bf16[32,2176]{1,0:T(8,128)(2,1)} %payload.1.refs_0_), channel_id=1, source_target_pairs={{0,4},{4,0},{8,12},{12,8},{1,5},{5,1},{9,13},{13,9},{2,6},{6,2},{1... | collective-permute-start | bytes 417800 | tf_op jit(solution)/shard_map/ppermute | solution.py:101
  8.1 1.7 %collective-permute-start.3 = (bf16[32,2048]{1,0:T(8,128)(2,1)}, bf16[32,2048]{1,0:T(8,128)(2,1)S(1)}, u32[]{:S(2)}, u32[]{:S(2)}) collective-permute-start(bf16[32,2048]{1,0:T(8,128)(2,1)} %refs_0_.1), channel_id=1, source_target_pairs={{0,2},{1,3},{2,0},{3,1},{4,6},{5,7},{6,4},{7,5},{8,10},{9,11},{10,... | collective-permute-start | bytes 393224 | tf_op jit(solution)/shard_map/ppermute | solution.py:105
  9.8 1.9 %copy-done = bf16[192,4,2048]{2,1,0:T(4,128)(2,1)S(1)} copy-done((bf16[192,4,2048]{2,1,0:T(4,128)(2,1)S(1)}, bf16[192,4,2048]{2,1,0:T(4,128)(2,1)}, u32[]{:S(2)}) %copy-start) | copy-done | bytes 3145752
  11.7 1.9 %copy-done.1 = bf16[192,4,2048]{2,1,0:T(4,128)(2,1)S(1)} copy-done((bf16[192,4,2048]{2,1,0:T(4,128)(2,1)S(1)}, bf16[192,4,2048]{2,1,0:T(4,128)(2,1)}, u32[]{:S(2)}) %copy-start.1) | copy-done | bytes 3145752
  13.6 1.9 %copy-done.2 = bf16[192,4,2048]{2,1,0:T(4,128)(2,1)S(1)} copy-done((bf16[192,4,2048]{2,1,0:T(4,128)(2,1)S(1)}, bf16[192,4,2048]{2,1,0:T(4,128)(2,1)}, u32[]{:S(2)}) %copy-start.2) | copy-done | bytes 3145752
  15.5 4.5 %merge_units.1.refs_5_.refs_6_ = bf16[3,768,2048]{2,1,0:T(8,128)(2,1)} custom-call(bf16[192,4,2048]{2,1,0:T(4,128)(2,1)S(1)} %copy-done, bf16[192,4,2048]{2,1,0:T(4,128)(2,1)S(1)} %copy-done.1, bf16[192,4,2048]{2,1,0:T(4,128)(2,1)S(1)} %copy-done.2), custom_call_target="tpu_custom_call" | custom-call | bytes 18874368 | tf_op jit(solution)/shard_map/merge_units/pallas_call | solution.py:266
  20.6 3.1 %collective-permute-start.4 = (bf16[32,2048]{1,0:T(8,128)(2,1)S(1)}, bf16[32,2048]{1,0:T(8,128)(2,1)S(1)}, u32[]{:S(2)}, u32[]{:S(2)}) collective-permute-start(bf16[32,2048]{1,0:T(8,128)(2,1)S(1)} %copy-done.4), channel_id=1, source_target_pairs={{0,8},{4,12},{8,0},{12,4},{1,9},{5,13},{9,1},{13,5},{2,10},{6,14},... | collective-permute-start | bytes 393224 | tf_op jit(solution)/shard_map/ppermute | solution.py:101
  23.7 1.3 %collective-permute-start.5 = (bf16[32,2048]{1,0:T(8,128)(2,1)S(1)}, bf16[32,2048]{1,0:T(8,128)(2,1)S(1)}, u32[]{:S(2)}, u32[]{:S(2)}) collective-permute-start(bf16[32,2048]{1,0:T(8,128)(2,1)S(1)} %copy-done.4), channel_id=1, source_target_pairs={{0,4},{4,0},{8,12},{12,8},{1,5},{5,1},{9,13},{13,9},{2,6},{6,2},{1... | collective-permute-start | bytes 393224 | tf_op jit(solution)/shard_map/ppermute | solution.py:101
  25.3 5.5 %collective-permute-done.4.refs_1_ = bf16[32,2048]{1,0:T(8,128)(2,1)S(1)} collective-permute-done((bf16[32,2048]{1,0:T(8,128)(2,1)S(1)}, bf16[32,2048]{1,0:T(8,128)(2,1)S(1)}, u32[]{:S(2)}, u32[]{:S(2)}) %collective-permute-start.4) | collective-permute-done | bytes 131104 | tf_op jit(solution)/shard_map/ppermute | solution.py:101
  31.2 2.9 %collective-permute-done.6.refs_3_ = bf16[32,2048]{1,0:T(8,128)(2,1)S(1)} collective-permute-done((bf16[32,2048]{1,0:T(8,128)(2,1)S(1)}, bf16[32,2048]{1,0:T(8,128)(2,1)S(1)}, u32[]{:S(2)}, u32[]{:S(2)}) %collective-permute-start.6) | collective-permute-done | bytes 131104 | tf_op jit(solution)/shard_map/ppermute | solution.py:101
  34.1 1.2 %collective-permute-done.7.refs_4_ = bf16[128,2176]{1,0:T(8,128)(2,1)S(1)} collective-permute-done((bf16[128,2176]{1,0:T(8,128)(2,1)S(1)}, bf16[128,2176]{1,0:T(8,128)(2,1)S(1)}, u32[]{:S(2)}, u32[]{:S(2)}) %collective-permute-start.7) | collective-permute-done | bytes 557088 | tf_op jit(solution)/shard_map/ppermute | solution.py:105
  35.7 8.4 %forward_products.1 = (bf16[128,2048]{1,0:T(8,128)(2,1)S(1)}, bf16[128,2048]{1,0:T(8,128)(2,1)S(1)}, f32[256,1536]{1,0:T(8,128)S(1)}, f32[256,1536]{1,0:T(8,128)...) custom-call(bf16[128,256]{1,0:T(8,128)(2,1)S(1)} %and_convert_fusion.spread, bf16[32,2176]{1,0:T(8,128)(2,1)S(1)} %copy-done.3, ...), custom_call_target="tpu_custom_call" | custom-call | flops 4831838208 | bytes 20971520 | tf_op jit(solution)/shard_map/forward_products/pallas_call | solution.py:298
  44.1 2.0 %collective-permute-done.9.refs_5_ = bf16[96,2048]{1,0:T(8,128)(2,1)S(1)} collective-permute-done((bf16[96,2048]{1,0:T(8,128)(2,1)S(1)}, bf16[96,2048]{1,0:T(8,128)(2,1)S(1)}, u32[]{:S(2)}, u32[]{:S(2)}) %collective-permute-start.9) | collective-permute-done | bytes 393248 | tf_op jit(solution)/shard_map/ppermute | solution.py:105
  46.5 9.9 %backward_products.1 = (bf16[128,2176]{1,0:T(8,128)(2,1)S(1)}, bf16[64,2176]{1,0:T(8,128)(2,1)S(1)}, bf16[64,2176]{1,0:T(8,128)(2,1)S(1)}, bf16[256,2048]{1,0:T(8,128)(2,1)S(1)}, bf16[768,2048]{1,0:T(8,128)(2,1)S(1)}) custom-call(bf16[256,128]{1,0:T(8,128)(2,1)S(1)} %fusion.1.collect, bf16[32,2048]{1,0:T(8,128)(2,1)S(1)} %copy-done.4, ...), custom_call_target="tpu_custom_call" | custom-call | flops 4831838208 | bytes 20971520 | tf_op jit(solution)/shard_map/backward_products/pallas_call | solution.py:298
  56.4 2.3 %collective-permute-done.10 = bf16[128,2048]{1,0:T(8,128)(2,1)S(1)} collective-permute-done((bf16[128,2048]{1,0:T(8,128)(2,1)S(1)}, bf16[128,2048]{1,0:T(8,128)(2,1)S(1)}, u32[]{:S(2)}, u32[]{:S(2)}) %collective-permute-start.10) | collective-permute-done | bytes 524320 | tf_op jit(solution)/shard_map/ppermute | solution.py:105
  59.3 1.7 %collective-permute-start.14 = (bf16[64,2048]{1,0:T(8,128)(2,1)S(1)}, bf16[64,2048]{1,0:T(8,128)(2,1)S(1)}, u32[]{:S(2)}, u32[]{:S(2)}) collective-permute-start(bf16[64,2048]{1,0:T(8,128)(2,1)S(1)} %slice.63), channel_id=1, source_target_pairs={{0,4},{4,0},{8,12},{12,8},{1,5},{5,1},{9,13},{13,9},{2,6},{6,2},{1... | collective-permute-start | bytes 786440 | tf_op jit(solution)/shard_map/ppermute | solution.py:101
  61.0 6.8 %collective-permute-done.11 = bf16[64,2176]{1,0:T(8,128)(2,1)S(1)} collective-permute-done((bf16[64,2176]{1,0:T(8,128)(2,1)S(1)}, bf16[64,2176]{1,0:T(8,128)(2,1)S(1)}, u32[]{:S(2)}, u32[]{:S(2)}) %collective-permute-start.11) | collective-permute-done | bytes 278560 | tf_op jit(solution)/shard_map/ppermute | solution.py:105
  67.8 1.8 %collective-permute-start.12 = (bf16[64,2176]{1,0:T(8,128)(2,1)S(1)}, bf16[64,2176]{1,0:T(8,128)(2,1)S(1)}, u32[]{:S(2)}, u32[]{:S(2)}) collective-permute-start(bf16[64,2176]{1,0:T(8,128)(2,1)S(1)} %add_convert_fusion), channel_id=1, source_target_pairs={{0,4},{4,0},{8,12},{12,8},{1,5},{5,1},{9,13},{13,9},{2,6},{6,2},{1... | collective-permute-start | bytes 835592 | tf_op jit(solution)/shard_map/ppermute | solution.py:101
  70.0 2.7 %collective-permute-start.15 = (bf16[32,2048]{1,0:T(8,128)(2,1)S(1)}, bf16[32,2048]{1,0:T(8,128)(2,1)S(1)}, u32[]{:S(2)}, u32[]{:S(2)}) collective-permute-start(bf16[32,2048]{1,0:T(8,128)(2,1)S(1)} %slice.66), channel_id=1, source_target_pairs={{0,8},{4,12},{8,0},{12,4},{1,9},{5,13},{9,1},{13,5},{2,10},{6,14},... | collective-permute-start | bytes 393224 | tf_op jit(solution)/shard_map/ppermute | solution.py:101
  72.8 5.5 %collective-permute-done.15 = bf16[32,2048]{1,0:T(8,128)(2,1)S(1)} collective-permute-done((bf16[32,2048]{1,0:T(8,128)(2,1)S(1)}, bf16[32,2048]{1,0:T(8,128)(2,1)S(1)}, u32[]{:S(2)}, u32[]{:S(2)}) %collective-permute-start.15) | collective-permute-done | bytes 131104 | tf_op jit(solution)/shard_map/ppermute | solution.py:101
  79.1 2.8 %collective-permute-start.17 = (bf16[32,2176]{1,0:T(8,128)(2,1)S(1)}, bf16[32,2176]{1,0:T(8,128)(2,1)S(1)}, u32[]{:S(2)}, u32[]{:S(2)}) collective-permute-start(bf16[32,2176]{1,0:T(8,128)(2,1)S(1)} %slice.64), channel_id=1, source_target_pairs={{0,8},{4,12},{8,0},{12,4},{1,9},{5,13},{9,1},{13,5},{2,10},{6,14},... | collective-permute-start | bytes 417800 | tf_op jit(solution)/shard_map/ppermute | solution.py:101
  82.6 2.9 %finish_share.1 = bf16[192,4,2048]{2,1,0:T(4,128)(2,1)} custom-call(bf16[256,1536]{1,0:T(8,128)(2,1)S(1)} %get-tuple-element.60.refs_11_.weighted, bf16[256,2048]{1,0:T(8,128)(2,1)S(1)} %get-tuple-element.74.rows, bf16[768,2048]{1,0:T(8,128)(2,1)S(1)} %collective-permute-done.16.other), custom_call_target="tpu_custom_call" | custom-call | flops 805306368 | bytes 6291456 | tf_op jit(solution)/shard_map/finish_share/pallas_call | solution.py:353
  (52 shorter events, 7.1 us)
Async XLA Ops:
  0.6 19.9 %copy-start.4 = (bf16[32,2048]{1,0:T(8,128)(2,1)S(1)}, bf16[32,2048]{1,0:T(8,128)(2,1)}, u32[]{:S(2)}) copy-start(bf16[32,2048]{1,0:T(8,128)(2,1)} %refs_0_.1) | copy-start | bytes 393220
  2.5 17.5 %collective-permute-start = (bf16[32,2176]{1,0:T(8,128)(2,1)}, bf16[32,2176]{1,0:T(8,128)(2,1)S(1)}, u32[]{:S(2)}, u32[]{:S(2)}) collective-permute-start(bf16[32,2176]{1,0:T(8,128)(2,1)} %payload.1.refs_0_), channel_id=1, source_target_pairs={{0,8},{4,12},{8,0},{12,4},{1,9},{5,13},{9,1},{13,5},{2,10},{6,14},... | collective-permute-start | bytes 417800 | tf_op jit(solution)/shard_map/ppermute | solution.py:101
  6.5 13.5 %collective-permute-start.1 = (bf16[32,2176]{1,0:T(8,128)(2,1)}, bf16[32,2176]{1,0:T(8,128)(2,1)S(1)}, u32[]{:S(2)}, u32[]{:S(2)}) collective-permute-start(bf16[32,2176]{1,0:T(8,128)(2,1)} %payload.1.refs_0_), channel_id=1, source_target_pairs={{0,4},{4,0},{8,12},{12,8},{1,5},{5,1},{9,13},{13,9},{2,6},{6,2},{1... | collective-permute-start | bytes 417800 | tf_op jit(solution)/shard_map/ppermute | solution.py:101
  8.1 11.9 %collective-permute-start.2 = (bf16[32,2176]{1,0:T(8,128)(2,1)}, bf16[32,2176]{1,0:T(8,128)(2,1)S(1)}, u32[]{:S(2)}, u32[]{:S(2)}) collective-permute-start(bf16[32,2176]{1,0:T(8,128)(2,1)} %payload.1.refs_0_), channel_id=1, source_target_pairs={{0,12},{4,8},{8,4},{12,0},{1,13},{5,9},{9,5},{13,1},{2,14},{6,10},... | collective-permute-start | bytes 417800 | tf_op jit(solution)/shard_map/ppermute | solution.py:101
  8.1 11.9 %collective-permute-start.3 = (bf16[32,2048]{1,0:T(8,128)(2,1)}, bf16[32,2048]{1,0:T(8,128)(2,1)S(1)}, u32[]{:S(2)}, u32[]{:S(2)}) collective-permute-start(bf16[32,2048]{1,0:T(8,128)(2,1)} %refs_0_.1), channel_id=1, source_target_pairs={{0,2},{1,3},{2,0},{3,1},{4,6},{5,7},{6,4},{7,5},{8,10},{9,11},{10,... | collective-permute-start | bytes 393224 | tf_op jit(solution)/shard_map/ppermute | solution.py:105
  9.8 1.9 %copy-start = (bf16[192,4,2048]{2,1,0:T(4,128)(2,1)S(1)}, bf16[192,4,2048]{2,1,0:T(4,128)(2,1)}, u32[]{:S(2)}) copy-start(bf16[192,4,2048]{2,1,0:T(4,128)(2,1)} %gate) | copy-start | bytes 9437188
  11.7 1.9 %copy-start.1 = (bf16[192,4,2048]{2,1,0:T(4,128)(2,1)S(1)}, bf16[192,4,2048]{2,1,0:T(4,128)(2,1)}, u32[]{:S(2)}) copy-start(bf16[192,4,2048]{2,1,0:T(4,128)(2,1)} %up.1) | copy-start | bytes 9437188
  15.4 4.7 %copy-start.3 = (bf16[32,2176]{1,0:T(8,128)(2,1)S(1)}, bf16[32,2176]{1,0:T(8,128)(2,1)}, u32[]{:S(2)}) copy-start(bf16[32,2176]{1,0:T(8,128)(2,1)} %payload.1.refs_0_) | copy-start | bytes 417796
  20.0 15.7 %collective-permute-start.8 = (bf16[3,768,2048]{2,1,0:T(8,128)(2,1)}, bf16[3,768,2048]{2,1,0:T(8,128)(2,1)}, u32[]{:S(2)}, u32[]{:S(2)}) collective-permute-start(bf16[3,768,2048]{2,1,0:T(8,128)(2,1)} %merge_units.1.refs_5_.refs_6_), channel_id=1, source_target_pairs={{0,1},{1,0},{2,3},{3,2},{4,5},{5,4},{6,7},{7,6},{8,9},{9,8},{10,11... | collective-permute-start | bytes 28311560 | tf_op jit(solution)/shard_map/ppermute | solution.py:105
  20.2 15.1 %collective-permute-start.7 = (bf16[128,2176]{1,0:T(8,128)(2,1)S(1)}, bf16[128,2176]{1,0:T(8,128)(2,1)S(1)}, u32[]{:S(2)}, u32[]{:S(2)}) collective-permute-start(bf16[128,2176]{1,0:T(8,128)(2,1)S(1)} %pad_maximum_fusion), channel_id=1, source_target_pairs={{0,2},{1,3},{2,0},{3,1},{4,6},{5,7},{6,4},{7,5},{8,10},{9,11},{10,... | collective-permute-start | bytes 1671176 | tf_op jit(solution)/shard_map/ppermute | solution.py:105
  20.6 10.3 %collective-permute-start.4 = (bf16[32,2048]{1,0:T(8,128)(2,1)S(1)}, bf16[32,2048]{1,0:T(8,128)(2,1)S(1)}, u32[]{:S(2)}, u32[]{:S(2)}) collective-permute-start(bf16[32,2048]{1,0:T(8,128)(2,1)S(1)} %copy-done.4), channel_id=1, source_target_pairs={{0,8},{4,12},{8,0},{12,4},{1,9},{5,13},{9,1},{13,5},{2,10},{6,14},... | collective-permute-start | bytes 393224 | tf_op jit(solution)/shard_map/ppermute | solution.py:101
  23.7 7.5 %collective-permute-start.5 = (bf16[32,2048]{1,0:T(8,128)(2,1)S(1)}, bf16[32,2048]{1,0:T(8,128)(2,1)S(1)}, u32[]{:S(2)}, u32[]{:S(2)}) collective-permute-start(bf16[32,2048]{1,0:T(8,128)(2,1)S(1)} %copy-done.4), channel_id=1, source_target_pairs={{0,4},{4,0},{8,12},{12,8},{1,5},{5,1},{9,13},{13,9},{2,6},{6,2},{1... | collective-permute-start | bytes 393224 | tf_op jit(solution)/shard_map/ppermute | solution.py:101
  25.0 9.1 %collective-permute-start.6 = (bf16[32,2048]{1,0:T(8,128)(2,1)S(1)}, bf16[32,2048]{1,0:T(8,128)(2,1)S(1)}, u32[]{:S(2)}, u32[]{:S(2)}) collective-permute-start(bf16[32,2048]{1,0:T(8,128)(2,1)S(1)} %copy-done.4), channel_id=1, source_target_pairs={{0,12},{4,8},{8,4},{12,0},{1,13},{5,9},{9,5},{13,1},{2,14},{6,10},... | collective-permute-start | bytes 393224 | tf_op jit(solution)/shard_map/ppermute | solution.py:101
  35.3 10.8 %collective-permute-start.9 = (bf16[96,2048]{1,0:T(8,128)(2,1)S(1)}, bf16[96,2048]{1,0:T(8,128)(2,1)S(1)}, u32[]{:S(2)}, u32[]{:S(2)}) collective-permute-start(bf16[96,2048]{1,0:T(8,128)(2,1)S(1)} %pad_maximum_fusion.1), channel_id=1, source_target_pairs={{0,2},{1,3},{2,0},{3,1},{4,6},{5,7},{6,4},{7,5},{8,10},{9,11},{10,... | collective-permute-start | bytes 1179656 | tf_op jit(solution)/shard_map/ppermute | solution.py:105
  46.0 12.6 %collective-permute-start.10 = (bf16[128,2048]{1,0:T(8,128)(2,1)S(1)}, bf16[128,2048]{1,0:T(8,128)(2,1)S(1)}, u32[]{:S(2)}, u32[]{:S(2)}) collective-permute-start(bf16[128,2048]{1,0:T(8,128)(2,1)S(1)} %get-tuple-element.63), channel_id=1, source_target_pairs={{0,2},{1,3},{2,0},{3,1},{4,6},{5,7},{6,4},{7,5},{8,10},{9,11},{10,... | collective-permute-start | bytes 1572872 | tf_op jit(solution)/shard_map/ppermute | solution.py:105
  58.7 20.3 %collective-permute-start.16 = (bf16[768,2048]{1,0:T(8,128)(2,1)S(1)}, bf16[768,2048]{1,0:T(8,128)(2,1)S(1)}, u32[]{:S(2)}, u32[]{:S(2)}) collective-permute-start(bf16[768,2048]{1,0:T(8,128)(2,1)S(1)} %get-tuple-element.71), channel_id=1, source_target_pairs={{0,1},{1,0},{2,3},{3,2},{4,5},{5,4},{6,7},{7,6},{8,9},{9,8},{10,11... | collective-permute-start | bytes 9437192 | tf_op jit(solution)/shard_map/ppermute | solution.py:105
  58.7 9.1 %collective-permute-start.11 = (bf16[64,2176]{1,0:T(8,128)(2,1)S(1)}, bf16[64,2176]{1,0:T(8,128)(2,1)S(1)}, u32[]{:S(2)}, u32[]{:S(2)}) collective-permute-start(bf16[64,2176]{1,0:T(8,128)(2,1)S(1)} %get-tuple-element.65), channel_id=1, source_target_pairs={{0,2},{1,3},{2,0},{3,1},{4,6},{5,7},{6,4},{7,5},{8,10},{9,11},{10,... | collective-permute-start | bytes 835592 | tf_op jit(solution)/shard_map/ppermute | solution.py:105
  59.2 13.6 %copy-start.6 = (s32[32,8]{0,1:T(8,128)S(1)}, s32[32,8]{0,1:T(8,128)}, u32[]{:S(2)}) copy-start(s32[32,8]{0,1:T(8,128)} %param.11) | copy-start | bytes 3076
  59.3 10.7 %collective-permute-start.14 = (bf16[64,2048]{1,0:T(8,128)(2,1)S(1)}, bf16[64,2048]{1,0:T(8,128)(2,1)S(1)}, u32[]{:S(2)}, u32[]{:S(2)}) collective-permute-start(bf16[64,2048]{1,0:T(8,128)(2,1)S(1)} %slice.63), channel_id=1, source_target_pairs={{0,4},{4,0},{8,12},{12,8},{1,5},{5,1},{9,13},{13,9},{2,6},{6,2},{1... | collective-permute-start | bytes 786440 | tf_op jit(solution)/shard_map/ppermute | solution.py:101
  67.8 11.2 %collective-permute-start.12 = (bf16[64,2176]{1,0:T(8,128)(2,1)S(1)}, bf16[64,2176]{1,0:T(8,128)(2,1)S(1)}, u32[]{:S(2)}, u32[]{:S(2)}) collective-permute-start(bf16[64,2176]{1,0:T(8,128)(2,1)S(1)} %add_convert_fusion), channel_id=1, source_target_pairs={{0,4},{4,0},{8,12},{12,8},{1,5},{5,1},{9,13},{13,9},{2,6},{6,2},{1... | collective-permute-start | bytes 835592 | tf_op jit(solution)/shard_map/ppermute | solution.py:101
  69.6 9.4 %collective-permute-start.13 = (bf16[64,2176]{1,0:T(8,128)(2,1)S(1)}, bf16[64,2176]{1,0:T(8,128)(2,1)S(1)}, u32[]{:S(2)}, u32[]{:S(2)}) collective-permute-start(bf16[64,2176]{1,0:T(8,128)(2,1)S(1)} %get-tuple-element.68), channel_id=1, source_target_pairs={{0,2},{1,3},{2,0},{3,1},{4,6},{5,7},{6,4},{7,5},{8,10},{9,11},{10,... | collective-permute-start | bytes 835592 | tf_op jit(solution)/shard_map/ppermute | solution.py:105
  70.0 8.2 %collective-permute-start.15 = (bf16[32,2048]{1,0:T(8,128)(2,1)S(1)}, bf16[32,2048]{1,0:T(8,128)(2,1)S(1)}, u32[]{:S(2)}, u32[]{:S(2)}) collective-permute-start(bf16[32,2048]{1,0:T(8,128)(2,1)S(1)} %slice.66), channel_id=1, source_target_pairs={{0,8},{4,12},{8,0},{12,4},{1,9},{5,13},{9,1},{13,5},{2,10},{6,14},... | collective-permute-start | bytes 393224 | tf_op jit(solution)/shard_map/ppermute | solution.py:101
  79.1 7.5 %collective-permute-start.17 = (bf16[32,2176]{1,0:T(8,128)(2,1)S(1)}, bf16[32,2176]{1,0:T(8,128)(2,1)S(1)}, u32[]{:S(2)}, u32[]{:S(2)}) collective-permute-start(bf16[32,2176]{1,0:T(8,128)(2,1)S(1)} %slice.64), channel_id=1, source_target_pairs={{0,8},{4,12},{8,0},{12,4},{1,9},{5,13},{9,1},{13,5},{2,10},{6,14},... | collective-permute-start | bytes 417800 | tf_op jit(solution)/shard_map/ppermute | solution.py:101
  82.6 4.8 %copy-start.5 = (s32[32,8]{0,1:T(8,128)S(1)}, s32[32,8]{0,1:T(8,128)}, u32[]{:S(2)}) copy-start(s32[32,8]{0,1:T(8,128)} %param.10) | copy-start | bytes 3076
  (1 other events, 1.9 us)

commit v7 on v6

--- a/solution.py
+++ b/solution.py
@@ -382,15 +382,17 @@
     spread = spread.astype(jnp.bfloat16)
 
     own_t = payload(tokens, expert_ids, slot_pos, combine_weight, experts, side)
-    own_t, own_g, w_gate = lax.optimization_barrier((own_t, out_grad, w_gate))
-    column_t = [over_z(own_t, bit) for bit in (2, 1, 3)]
+    own_t, own_g = lax.optimization_barrier((own_t, out_grad))
+    across = {bit: over_z(own_t, bit) for bit in (3, 2, 1)}
+    column_t = [across[bit] for bit in (2, 1, 3)]
     own_gx = over_dp(own_g, 2)
     weights = merge_units(w_gate, w_up, w_down)
     column_t, own_gx, own_g, weights = lax.optimization_barrier((column_t, own_gx, own_g, weights))
 
     pieces_t = [own_t, *column_t]
     column_tx = over_dp(jnp.concatenate(pieces_t, axis=0), 2)
-    column_g = [over_z(own_g, bit) for bit in (2, 1, 3)]
+    across = {bit: over_z(own_g, bit) for bit in (3, 2, 1)}
+    column_g = [across[bit] for bit in (2, 1, 3)]
     weights_b = over_dp(weights, 1)
     column_g, column_tx = lax.optimization_barrier((column_g, column_tx))
 

time: 88.3 us -> 88.3 us (level)
  no operation moved by 1% of the time
where the time goes in v7:
time: 88.3 us; the launch traced here: 88 us
  waiting for transfers between devices  28.3 us (32%)
  Pallas kernels  27.6 us (31%)
  starting transfers between devices  22.9 us (26%)
  local copies, waits for them, and re-layouts  6.49 us (7%)
  other arithmetic  1.95 us (2%)
    ppermute x10, starting transfers between devices, over_z(): lax.ppermute(rows, 'expert', [(i, i ^ bit) for i in range(lax.axis_size('...  19.3 us
    pallas_call x2, Pallas kernels, products(): pl.pallas_call(kernel, in_specs=[IN_VMEM] * (1 + len(pieces)) + [pl.Block...  18.3 us
    ppermute x10, waiting for transfers between devices, over_z(): lax.ppermute(rows, 'expert', [(i, i ^ bit) for i in range(lax.axis_size('...  16.1 us
    ppermute x8, waiting for transfers between devices, over_dp(): lax.ppermute(rows, 'dp', [(i, i ^ bit) for i in range(lax.axis_size('dp'))])  12.2 us
    unnamed x14, local copies, waits for them, and re-layouts  5.69 us
    pallas_call x1, Pallas kernels, merge_units(): pl.pallas_call(merge_kernel, grid=(units // tile,), in_specs=[block] * 3,...  4.54 us
    ppermute x8, starting transfers between devices, over_dp(): lax.ppermute(rows, 'dp', [(i, i ^ bit) for i in range(lax.axis_size('dp'))])  3.64 us
    pallas_call x1, Pallas kernels, finish_share(): pl.pallas_call(share_kernel, grid=(units // tile,), in_specs=[pl.BlockSpe...  2.91 us
  transfers between devices with their start and end apart: 18, of which 10 were waited for; matrix products, arithmetic and copies ran while one was open for 1% of the time, Pallas kernels for 29%

profile of v7, /device:TPU:0, one launch (start us, length us, event | category | flops | bytes accessed | tf_op | source)
XLA Modules:
  0.0 88.0 jit_solution(4515779078905884264)
XLA Ops:
  0.6 1.8 %payload.1.refs_0_ = bf16[32,2176]{1,0:T(8,128)(2,1)} custom-call(bf16[32,2048]{1,0:T(8,128)(2,1)} %tokens.1, s32[8,32]{1,0:T(8,128)} %bitcast.3, s32[8,32]{1,0:T(8,128)} %bitcast.4, f32[8,32]{1,0:T(8,128)} %bitcast.5), custom_call_target="tpu_custom_call" | custom-call | tf_op jit(solution)/shard_map/payload/pallas_call | solution.py:160
  2.5 4.0 %collective-permute-start = (bf16[32,2176]{1,0:T(8,128)(2,1)}, bf16[32,2176]{1,0:T(8,128)(2,1)S(1)}, u32[]{:S(2)}, u32[]{:S(2)}) collective-permute-start(bf16[32,2176]{1,0:T(8,128)(2,1)} %payload.1.refs_0_), channel_id=1, source_target_pairs={{0,8},{4,12},{8,0},{12,4},{1,9},{5,13},{9,1},{13,5},{2,10},{6,14},... | collective-permute-start | bytes 417800 | tf_op jit(solution)/shard_map/ppermute | solution.py:101
  6.5 1.6 %collective-permute-start.1 = (bf16[32,2176]{1,0:T(8,128)(2,1)}, bf16[32,2176]{1,0:T(8,128)(2,1)S(1)}, u32[]{:S(2)}, u32[]{:S(2)}) collective-permute-start(bf16[32,2176]{1,0:T(8,128)(2,1)} %payload.1.refs_0_), channel_id=1, source_target_pairs={{0,4},{4,0},{8,12},{12,8},{1,5},{5,1},{9,13},{13,9},{2,6},{6,2},{1... | collective-permute-start | bytes 417800 | tf_op jit(solution)/shard_map/ppermute | solution.py:101
  8.1 1.7 %collective-permute-start.3 = (bf16[32,2048]{1,0:T(8,128)(2,1)}, bf16[32,2048]{1,0:T(8,128)(2,1)S(1)}, u32[]{:S(2)}, u32[]{:S(2)}) collective-permute-start(bf16[32,2048]{1,0:T(8,128)(2,1)} %refs_0_.1), channel_id=1, source_target_pairs={{0,2},{1,3},{2,0},{3,1},{4,6},{5,7},{6,4},{7,5},{8,10},{9,11},{10,... | collective-permute-start | bytes 393224 | tf_op jit(solution)/shard_map/ppermute | solution.py:105
  9.8 1.9 %copy-done = bf16[192,4,2048]{2,1,0:T(4,128)(2,1)S(1)} copy-done((bf16[192,4,2048]{2,1,0:T(4,128)(2,1)S(1)}, bf16[192,4,2048]{2,1,0:T(4,128)(2,1)}, u32[]{:S(2)}) %copy-start) | copy-done | bytes 3145752
  11.7 1.9 %copy-done.1 = bf16[192,4,2048]{2,1,0:T(4,128)(2,1)S(1)} copy-done((bf16[192,4,2048]{2,1,0:T(4,128)(2,1)S(1)}, bf16[192,4,2048]{2,1,0:T(4,128)(2,1)}, u32[]{:S(2)}) %copy-start.1) | copy-done | bytes 3145752
  13.6 1.9 %copy-done.2 = bf16[192,4,2048]{2,1,0:T(4,128)(2,1)S(1)} copy-done((bf16[192,4,2048]{2,1,0:T(4,128)(2,1)S(1)}, bf16[192,4,2048]{2,1,0:T(4,128)(2,1)}, u32[]{:S(2)}) %copy-start.2) | copy-done | bytes 3145752
  15.5 4.5 %merge_units.1.refs_5_.refs_6_ = bf16[3,768,2048]{2,1,0:T(8,128)(2,1)} custom-call(bf16[192,4,2048]{2,1,0:T(4,128)(2,1)S(1)} %copy-done, bf16[192,4,2048]{2,1,0:T(4,128)(2,1)S(1)} %copy-done.1, bf16[192,4,2048]{2,1,0:T(4,128)(2,1)S(1)} %copy-done.2), custom_call_target="tpu_custom_call" | custom-call | bytes 18874368 | tf_op jit(solution)/shard_map/merge_units/pallas_call | solution.py:266
  20.6 3.1 %collective-permute-start.4 = (bf16[32,2048]{1,0:T(8,128)(2,1)S(1)}, bf16[32,2048]{1,0:T(8,128)(2,1)S(1)}, u32[]{:S(2)}, u32[]{:S(2)}) collective-permute-start(bf16[32,2048]{1,0:T(8,128)(2,1)S(1)} %copy-done.4), channel_id=1, source_target_pairs={{0,8},{4,12},{8,0},{12,4},{1,9},{5,13},{9,1},{13,5},{2,10},{6,14},... | collective-permute-start | bytes 393224 | tf_op jit(solution)/shard_map/ppermute | solution.py:101
  23.7 1.3 %collective-permute-start.5 = (bf16[32,2048]{1,0:T(8,128)(2,1)S(1)}, bf16[32,2048]{1,0:T(8,128)(2,1)S(1)}, u32[]{:S(2)}, u32[]{:S(2)}) collective-permute-start(bf16[32,2048]{1,0:T(8,128)(2,1)S(1)} %copy-done.4), channel_id=1, source_target_pairs={{0,4},{4,0},{8,12},{12,8},{1,5},{5,1},{9,13},{13,9},{2,6},{6,2},{1... | collective-permute-start | bytes 393224 | tf_op jit(solution)/shard_map/ppermute | solution.py:101
  25.3 5.5 %collective-permute-done.4.refs_1_ = bf16[32,2048]{1,0:T(8,128)(2,1)S(1)} collective-permute-done((bf16[32,2048]{1,0:T(8,128)(2,1)S(1)}, bf16[32,2048]{1,0:T(8,128)(2,1)S(1)}, u32[]{:S(2)}, u32[]{:S(2)}) %collective-permute-start.4) | collective-permute-done | bytes 131104 | tf_op jit(solution)/shard_map/ppermute | solution.py:101
  31.2 2.9 %collective-permute-done.6.refs_3_ = bf16[32,2048]{1,0:T(8,128)(2,1)S(1)} collective-permute-done((bf16[32,2048]{1,0:T(8,128)(2,1)S(1)}, bf16[32,2048]{1,0:T(8,128)(2,1)S(1)}, u32[]{:S(2)}, u32[]{:S(2)}) %collective-permute-start.6) | collective-permute-done | bytes 131104 | tf_op jit(solution)/shard_map/ppermute | solution.py:101
  34.1 1.2 %collective-permute-done.7.refs_4_ = bf16[128,2176]{1,0:T(8,128)(2,1)S(1)} collective-permute-done((bf16[128,2176]{1,0:T(8,128)(2,1)S(1)}, bf16[128,2176]{1,0:T(8,128)(2,1)S(1)}, u32[]{:S(2)}, u32[]{:S(2)}) %collective-permute-start.7) | collective-permute-done | bytes 557088 | tf_op jit(solution)/shard_map/ppermute | solution.py:105
  35.7 8.4 %forward_products.1 = (bf16[128,2048]{1,0:T(8,128)(2,1)S(1)}, bf16[128,2048]{1,0:T(8,128)(2,1)S(1)}, f32[256,1536]{1,0:T(8,128)S(1)}, f32[256,1536]{1,0:T(8,128)...) custom-call(bf16[128,256]{1,0:T(8,128)(2,1)S(1)} %and_convert_fusion.spread, bf16[32,2176]{1,0:T(8,128)(2,1)S(1)} %copy-done.3, ...), custom_call_target="tpu_custom_call" | custom-call | flops 4831838208 | bytes 20971520 | tf_op jit(solution)/shard_map/forward_products/pallas_call | solution.py:298
  44.1 2.0 %collective-permute-done.9.refs_5_ = bf16[96,2048]{1,0:T(8,128)(2,1)S(1)} collective-permute-done((bf16[96,2048]{1,0:T(8,128)(2,1)S(1)}, bf16[96,2048]{1,0:T(8,128)(2,1)S(1)}, u32[]{:S(2)}, u32[]{:S(2)}) %collective-permute-start.9) | collective-permute-done | bytes 393248 | tf_op jit(solution)/shard_map/ppermute | solution.py:105
  46.5 9.9 %backward_products.1 = (bf16[128,2176]{1,0:T(8,128)(2,1)S(1)}, bf16[64,2176]{1,0:T(8,128)(2,1)S(1)}, bf16[64,2176]{1,0:T(8,128)(2,1)S(1)}, bf16[256,2048]{1,0:T(8,128)(2,1)S(1)}, bf16[768,2048]{1,0:T(8,128)(2,1)S(1)}) custom-call(bf16[256,128]{1,0:T(8,128)(2,1)S(1)} %fusion.1.collect, bf16[32,2048]{1,0:T(8,128)(2,1)S(1)} %copy-done.4, ...), custom_call_target="tpu_custom_call" | custom-call | flops 4831838208 | bytes 20971520 | tf_op jit(solution)/shard_map/backward_products/pallas_call | solution.py:298
  56.4 2.3 %collective-permute-done.10 = bf16[128,2048]{1,0:T(8,128)(2,1)S(1)} collective-permute-done((bf16[128,2048]{1,0:T(8,128)(2,1)S(1)}, bf16[128,2048]{1,0:T(8,128)(2,1)S(1)}, u32[]{:S(2)}, u32[]{:S(2)}) %collective-permute-start.10) | collective-permute-done | bytes 524320 | tf_op jit(solution)/shard_map/ppermute | solution.py:105
  59.3 1.7 %collective-permute-start.14 = (bf16[64,2048]{1,0:T(8,128)(2,1)S(1)}, bf16[64,2048]{1,0:T(8,128)(2,1)S(1)}, u32[]{:S(2)}, u32[]{:S(2)}) collective-permute-start(bf16[64,2048]{1,0:T(8,128)(2,1)S(1)} %slice.63), channel_id=1, source_target_pairs={{0,4},{4,0},{8,12},{12,8},{1,5},{5,1},{9,13},{13,9},{2,6},{6,2},{1... | collective-permute-start | bytes 786440 | tf_op jit(solution)/shard_map/ppermute | solution.py:101
  61.0 6.8 %collective-permute-done.11 = bf16[64,2176]{1,0:T(8,128)(2,1)S(1)} collective-permute-done((bf16[64,2176]{1,0:T(8,128)(2,1)S(1)}, bf16[64,2176]{1,0:T(8,128)(2,1)S(1)}, u32[]{:S(2)}, u32[]{:S(2)}) %collective-permute-start.11) | collective-permute-done | bytes 278560 | tf_op jit(solution)/shard_map/ppermute | solution.py:105
  67.8 1.8 %collective-permute-start.12 = (bf16[64,2176]{1,0:T(8,128)(2,1)S(1)}, bf16[64,2176]{1,0:T(8,128)(2,1)S(1)}, u32[]{:S(2)}, u32[]{:S(2)}) collective-permute-start(bf16[64,2176]{1,0:T(8,128)(2,1)S(1)} %add_convert_fusion), channel_id=1, source_target_pairs={{0,4},{4,0},{8,12},{12,8},{1,5},{5,1},{9,13},{13,9},{2,6},{6,2},{1... | collective-permute-start | bytes 835592 | tf_op jit(solution)/shard_map/ppermute | solution.py:101
  70.0 2.7 %collective-permute-start.15 = (bf16[32,2048]{1,0:T(8,128)(2,1)S(1)}, bf16[32,2048]{1,0:T(8,128)(2,1)S(1)}, u32[]{:S(2)}, u32[]{:S(2)}) collective-permute-start(bf16[32,2048]{1,0:T(8,128)(2,1)S(1)} %slice.66), channel_id=1, source_target_pairs={{0,8},{4,12},{8,0},{12,4},{1,9},{5,13},{9,1},{13,5},{2,10},{6,14},... | collective-permute-start | bytes 393224 | tf_op jit(solution)/shard_map/ppermute | solution.py:101
  72.8 5.5 %collective-permute-done.15 = bf16[32,2048]{1,0:T(8,128)(2,1)S(1)} collective-permute-done((bf16[32,2048]{1,0:T(8,128)(2,1)S(1)}, bf16[32,2048]{1,0:T(8,128)(2,1)S(1)}, u32[]{:S(2)}, u32[]{:S(2)}) %collective-permute-start.15) | collective-permute-done | bytes 131104 | tf_op jit(solution)/shard_map/ppermute | solution.py:101
  79.1 2.8 %collective-permute-start.17 = (bf16[32,2176]{1,0:T(8,128)(2,1)S(1)}, bf16[32,2176]{1,0:T(8,128)(2,1)S(1)}, u32[]{:S(2)}, u32[]{:S(2)}) collective-permute-start(bf16[32,2176]{1,0:T(8,128)(2,1)S(1)} %slice.64), channel_id=1, source_target_pairs={{0,8},{4,12},{8,0},{12,4},{1,9},{5,13},{9,1},{13,5},{2,10},{6,14},... | collective-permute-start | bytes 417800 | tf_op jit(solution)/shard_map/ppermute | solution.py:101
  82.6 2.9 %finish_share.1 = bf16[192,4,2048]{2,1,0:T(4,128)(2,1)} custom-call(bf16[256,1536]{1,0:T(8,128)(2,1)S(1)} %get-tuple-element.58.refs_11_.weighted, bf16[256,2048]{1,0:T(8,128)(2,1)S(1)} %get-tuple-element.72.rows, bf16[768,2048]{1,0:T(8,128)(2,1)S(1)} %collective-permute-done.16.other), custom_call_target="tpu_custom_call" | custom-call | flops 805306368 | bytes 6291456 | tf_op jit(solution)/shard_map/finish_share/pallas_call | solution.py:353
  (52 shorter events, 7.1 us)
Async XLA Ops:
  0.6 19.9 %copy-start.4 = (bf16[32,2048]{1,0:T(8,128)(2,1)S(1)}, bf16[32,2048]{1,0:T(8,128)(2,1)}, u32[]{:S(2)}) copy-start(bf16[32,2048]{1,0:T(8,128)(2,1)} %refs_0_.1) | copy-start | bytes 393220
  2.5 17.5 %collective-permute-start = (bf16[32,2176]{1,0:T(8,128)(2,1)}, bf16[32,2176]{1,0:T(8,128)(2,1)S(1)}, u32[]{:S(2)}, u32[]{:S(2)}) collective-permute-start(bf16[32,2176]{1,0:T(8,128)(2,1)} %payload.1.refs_0_), channel_id=1, source_target_pairs={{0,8},{4,12},{8,0},{12,4},{1,9},{5,13},{9,1},{13,5},{2,10},{6,14},... | collective-permute-start | bytes 417800 | tf_op jit(solution)/shard_map/ppermute | solution.py:101
  6.5 13.5 %collective-permute-start.1 = (bf16[32,2176]{1,0:T(8,128)(2,1)}, bf16[32,2176]{1,0:T(8,128)(2,1)S(1)}, u32[]{:S(2)}, u32[]{:S(2)}) collective-permute-start(bf16[32,2176]{1,0:T(8,128)(2,1)} %payload.1.refs_0_), channel_id=1, source_target_pairs={{0,4},{4,0},{8,12},{12,8},{1,5},{5,1},{9,13},{13,9},{2,6},{6,2},{1... | collective-permute-start | bytes 417800 | tf_op jit(solution)/shard_map/ppermute | solution.py:101
  8.1 11.9 %collective-permute-start.2 = (bf16[32,2176]{1,0:T(8,128)(2,1)}, bf16[32,2176]{1,0:T(8,128)(2,1)S(1)}, u32[]{:S(2)}, u32[]{:S(2)}) collective-permute-start(bf16[32,2176]{1,0:T(8,128)(2,1)} %payload.1.refs_0_), channel_id=1, source_target_pairs={{0,12},{4,8},{8,4},{12,0},{1,13},{5,9},{9,5},{13,1},{2,14},{6,10},... | collective-permute-start | bytes 417800 | tf_op jit(solution)/shard_map/ppermute | solution.py:101
  8.1 11.9 %collective-permute-start.3 = (bf16[32,2048]{1,0:T(8,128)(2,1)}, bf16[32,2048]{1,0:T(8,128)(2,1)S(1)}, u32[]{:S(2)}, u32[]{:S(2)}) collective-permute-start(bf16[32,2048]{1,0:T(8,128)(2,1)} %refs_0_.1), channel_id=1, source_target_pairs={{0,2},{1,3},{2,0},{3,1},{4,6},{5,7},{6,4},{7,5},{8,10},{9,11},{10,... | collective-permute-start | bytes 393224 | tf_op jit(solution)/shard_map/ppermute | solution.py:105
  9.8 1.9 %copy-start = (bf16[192,4,2048]{2,1,0:T(4,128)(2,1)S(1)}, bf16[192,4,2048]{2,1,0:T(4,128)(2,1)}, u32[]{:S(2)}) copy-start(bf16[192,4,2048]{2,1,0:T(4,128)(2,1)} %gate.1) | copy-start | bytes 9437188
  11.7 1.9 %copy-start.1 = (bf16[192,4,2048]{2,1,0:T(4,128)(2,1)S(1)}, bf16[192,4,2048]{2,1,0:T(4,128)(2,1)}, u32[]{:S(2)}) copy-start(bf16[192,4,2048]{2,1,0:T(4,128)(2,1)} %up.1) | copy-start | bytes 9437188
  15.4 4.7 %copy-start.3 = (bf16[32,2176]{1,0:T(8,128)(2,1)S(1)}, bf16[32,2176]{1,0:T(8,128)(2,1)}, u32[]{:S(2)}) copy-start(bf16[32,2176]{1,0:T(8,128)(2,1)} %payload.1.refs_0_) | copy-start | bytes 417796
  20.0 15.7 %collective-permute-start.8 = (bf16[3,768,2048]{2,1,0:T(8,128)(2,1)}, bf16[3,768,2048]{2,1,0:T(8,128)(2,1)}, u32[]{:S(2)}, u32[]{:S(2)}) collective-permute-start(bf16[3,768,2048]{2,1,0:T(8,128)(2,1)} %merge_units.1.refs_5_.refs_6_), channel_id=1, source_target_pairs={{0,1},{1,0},{2,3},{3,2},{4,5},{5,4},{6,7},{7,6},{8,9},{9,8},{10,11... | collective-permute-start | bytes 28311560 | tf_op jit(solution)/shard_map/ppermute | solution.py:105
  20.2 15.1 %collective-permute-start.7 = (bf16[128,2176]{1,0:T(8,128)(2,1)S(1)}, bf16[128,2176]{1,0:T(8,128)(2,1)S(1)}, u32[]{:S(2)}, u32[]{:S(2)}) collective-permute-start(bf16[128,2176]{1,0:T(8,128)(2,1)S(1)} %pad_maximum_fusion), channel_id=1, source_target_pairs={{0,2},{1,3},{2,0},{3,1},{4,6},{5,7},{6,4},{7,5},{8,10},{9,11},{10,... | collective-permute-start | bytes 1671176 | tf_op jit(solution)/shard_map/ppermute | solution.py:105
  20.6 10.3 %collective-permute-start.4 = (bf16[32,2048]{1,0:T(8,128)(2,1)S(1)}, bf16[32,2048]{1,0:T(8,128)(2,1)S(1)}, u32[]{:S(2)}, u32[]{:S(2)}) collective-permute-start(bf16[32,2048]{1,0:T(8,128)(2,1)S(1)} %copy-done.4), channel_id=1, source_target_pairs={{0,8},{4,12},{8,0},{12,4},{1,9},{5,13},{9,1},{13,5},{2,10},{6,14},... | collective-permute-start | bytes 393224 | tf_op jit(solution)/shard_map/ppermute | solution.py:101
  23.7 7.5 %collective-permute-start.5 = (bf16[32,2048]{1,0:T(8,128)(2,1)S(1)}, bf16[32,2048]{1,0:T(8,128)(2,1)S(1)}, u32[]{:S(2)}, u32[]{:S(2)}) collective-permute-start(bf16[32,2048]{1,0:T(8,128)(2,1)S(1)} %copy-done.4), channel_id=1, source_target_pairs={{0,4},{4,0},{8,12},{12,8},{1,5},{5,1},{9,13},{13,9},{2,6},{6,2},{1... | collective-permute-start | bytes 393224 | tf_op jit(solution)/shard_map/ppermute | solution.py:101
  25.0 9.1 %collective-permute-start.6 = (bf16[32,2048]{1,0:T(8,128)(2,1)S(1)}, bf16[32,2048]{1,0:T(8,128)(2,1)S(1)}, u32[]{:S(2)}, u32[]{:S(2)}) collective-permute-start(bf16[32,2048]{1,0:T(8,128)(2,1)S(1)} %copy-done.4), channel_id=1, source_target_pairs={{0,12},{4,8},{8,4},{12,0},{1,13},{5,9},{9,5},{13,1},{2,14},{6,10},... | collective-permute-start | bytes 393224 | tf_op jit(solution)/shard_map/ppermute | solution.py:101
  35.3 10.8 %collective-permute-start.9 = (bf16[96,2048]{1,0:T(8,128)(2,1)S(1)}, bf16[96,2048]{1,0:T(8,128)(2,1)S(1)}, u32[]{:S(2)}, u32[]{:S(2)}) collective-permute-start(bf16[96,2048]{1,0:T(8,128)(2,1)S(1)} %pad_maximum_fusion.1), channel_id=1, source_target_pairs={{0,2},{1,3},{2,0},{3,1},{4,6},{5,7},{6,4},{7,5},{8,10},{9,11},{10,... | collective-permute-start | bytes 1179656 | tf_op jit(solution)/shard_map/ppermute | solution.py:105
  46.0 12.6 %collective-permute-start.10 = (bf16[128,2048]{1,0:T(8,128)(2,1)S(1)}, bf16[128,2048]{1,0:T(8,128)(2,1)S(1)}, u32[]{:S(2)}, u32[]{:S(2)}) collective-permute-start(bf16[128,2048]{1,0:T(8,128)(2,1)S(1)} %get-tuple-element.61), channel_id=1, source_target_pairs={{0,2},{1,3},{2,0},{3,1},{4,6},{5,7},{6,4},{7,5},{8,10},{9,11},{10,... | collective-permute-start | bytes 1572872 | tf_op jit(solution)/shard_map/ppermute | solution.py:105
  58.7 20.3 %collective-permute-start.16 = (bf16[768,2048]{1,0:T(8,128)(2,1)S(1)}, bf16[768,2048]{1,0:T(8,128)(2,1)S(1)}, u32[]{:S(2)}, u32[]{:S(2)}) collective-permute-start(bf16[768,2048]{1,0:T(8,128)(2,1)S(1)} %get-tuple-element.69), channel_id=1, source_target_pairs={{0,1},{1,0},{2,3},{3,2},{4,5},{5,4},{6,7},{7,6},{8,9},{9,8},{10,11... | collective-permute-start | bytes 9437192 | tf_op jit(solution)/shard_map/ppermute | solution.py:105
  58.7 9.1 %collective-permute-start.11 = (bf16[64,2176]{1,0:T(8,128)(2,1)S(1)}, bf16[64,2176]{1,0:T(8,128)(2,1)S(1)}, u32[]{:S(2)}, u32[]{:S(2)}) collective-permute-start(bf16[64,2176]{1,0:T(8,128)(2,1)S(1)} %get-tuple-element.63), channel_id=1, source_target_pairs={{0,2},{1,3},{2,0},{3,1},{4,6},{5,7},{6,4},{7,5},{8,10},{9,11},{10,... | collective-permute-start | bytes 835592 | tf_op jit(solution)/shard_map/ppermute | solution.py:105
  59.2 13.6 %copy-start.6 = (s32[32,8]{0,1:T(8,128)S(1)}, s32[32,8]{0,1:T(8,128)}, u32[]{:S(2)}) copy-start(s32[32,8]{0,1:T(8,128)} %param.11) | copy-start | bytes 3076
  59.3 10.7 %collective-permute-start.14 = (bf16[64,2048]{1,0:T(8,128)(2,1)S(1)}, bf16[64,2048]{1,0:T(8,128)(2,1)S(1)}, u32[]{:S(2)}, u32[]{:S(2)}) collective-permute-start(bf16[64,2048]{1,0:T(8,128)(2,1)S(1)} %slice.63), channel_id=1, source_target_pairs={{0,4},{4,0},{8,12},{12,8},{1,5},{5,1},{9,13},{13,9},{2,6},{6,2},{1... | collective-permute-start | bytes 786440 | tf_op jit(solution)/shard_map/ppermute | solution.py:101
  67.8 11.2 %collective-permute-start.12 = (bf16[64,2176]{1,0:T(8,128)(2,1)S(1)}, bf16[64,2176]{1,0:T(8,128)(2,1)S(1)}, u32[]{:S(2)}, u32[]{:S(2)}) collective-permute-start(bf16[64,2176]{1,0:T(8,128)(2,1)S(1)} %add_convert_fusion), channel_id=1, source_target_pairs={{0,4},{4,0},{8,12},{12,8},{1,5},{5,1},{9,13},{13,9},{2,6},{6,2},{1... | collective-permute-start | bytes 835592 | tf_op jit(solution)/shard_map/ppermute | solution.py:101
  69.6 9.4 %collective-permute-start.13 = (bf16[64,2176]{1,0:T(8,128)(2,1)S(1)}, bf16[64,2176]{1,0:T(8,128)(2,1)S(1)}, u32[]{:S(2)}, u32[]{:S(2)}) collective-permute-start(bf16[64,2176]{1,0:T(8,128)(2,1)S(1)} %get-tuple-element.66), channel_id=1, source_target_pairs={{0,2},{1,3},{2,0},{3,1},{4,6},{5,7},{6,4},{7,5},{8,10},{9,11},{10,... | collective-permute-start | bytes 835592 | tf_op jit(solution)/shard_map/ppermute | solution.py:105
  70.0 8.2 %collective-permute-start.15 = (bf16[32,2048]{1,0:T(8,128)(2,1)S(1)}, bf16[32,2048]{1,0:T(8,128)(2,1)S(1)}, u32[]{:S(2)}, u32[]{:S(2)}) collective-permute-start(bf16[32,2048]{1,0:T(8,128)(2,1)S(1)} %slice.66), channel_id=1, source_target_pairs={{0,8},{4,12},{8,0},{12,4},{1,9},{5,13},{9,1},{13,5},{2,10},{6,14},... | collective-permute-start | bytes 393224 | tf_op jit(solution)/shard_map/ppermute | solution.py:101
  79.1 7.5 %collective-permute-start.17 = (bf16[32,2176]{1,0:T(8,128)(2,1)S(1)}, bf16[32,2176]{1,0:T(8,128)(2,1)S(1)}, u32[]{:S(2)}, u32[]{:S(2)}) collective-permute-start(bf16[32,2176]{1,0:T(8,128)(2,1)S(1)} %slice.64), channel_id=1, source_target_pairs={{0,8},{4,12},{8,0},{12,4},{1,9},{5,13},{9,1},{13,5},{2,10},{6,14},... | collective-permute-start | bytes 417800 | tf_op jit(solution)/shard_map/ppermute | solution.py:101
  82.6 4.8 %copy-start.5 = (s32[32,8]{0,1:T(8,128)S(1)}, s32[32,8]{0,1:T(8,128)}, u32[]{:S(2)}) copy-start(s32[32,8]{0,1:T(8,128)} %param.10) | copy-start | bytes 3076
  (1 other events, 1.9 us)
